TPU v7x, 512 devices: a whole 4x4x16 slice. The times are simulated.
512 devices in a mesh: dp: 4 (over x), trow: 16 (over z_lo, core), tcol: 8 (over y, z_hi).
Axes of the slice: x: 4, y: 4, z: 16 (z_hi: 2, z_lo: 8; z = z_hi * 8 + z_lo), core: 2. Of those that a mesh axis runs over, the one named last changes fastest.
Arguments:
- hidden_in: bfloat16 [2048, 28672], P(('dp', 'tcol'), 'trow'), may hold values from -6 to 6
- down_weight: bfloat16 [28672, 8192], P('trow', 'tcol'), may hold values from -0.03125 to 0.03125
- block_scales: float32 [224, 64], P('trow', 'tcol'), may hold values from 0.5 to 2
- residual: bfloat16 [2048, 8192], P('dp', ('tcol', 'trow')), may hold values from -6 to 6
- projector: bfloat16 [8192, 1536], P(('tcol', 'trow')), may hold values from -0.0625 to 0.0625
- student: bfloat16 [2048, 1536], P(('dp', 'trow', 'tcol')), may hold values from -6 to 6
- segments: int32 [4, 512], P('dp'), may hold values from 0 to 7, never falling along the last dimension, each value on 1 to 192 neighbouring positions
Outputs:
- student_grad: float32 [2048, 1536], P(('dp', 'trow', 'tcol'))
- projector_grad: float32 [8192, 1536], P(('tcol', 'trow'))
Inputs may be any that keep to these rules, and one draw needn't show every extreme that they name: `segments`: within each group the passage numbers never fall, every number of 0 to 7 appears, and one passage has exactly 192 tokens.
All inputs are finite; a program needn't handle non-finite values.
Results may differ from a plain program's by a relative error of at most 0.029.
Values may be sent and summed in bfloat16 or wider, within the bound.
No kernel may reach another device: no remote copies, remote signals or barrier semaphores. Data moves between devices by JAX's collectives and lax.ppermute only.
A program may use at most 64 MiB of HBM per device.

v0:
```python
import math

import jax
import jax.numpy as jnp
from jax import lax
from jax.sharding import PartitionSpec as P

BLOCK = 128
COUNT = 8


def shards(hidden_in, down_weight, block_scales, residual, projector, student, segments):
    rows, cols = down_weight.shape
    effective = (
        (
            down_weight.reshape(rows // BLOCK, BLOCK, cols // BLOCK, BLOCK).astype(jnp.float32)
            * block_scales[:, None, :, None]
        )
        .reshape(rows, cols)
        .astype(jnp.bfloat16)
    )
    tok_group = residual.shape[0]
    owned = tok_group // lax.axis_size(("trow", "tcol"))
    partial_value = jnp.dot(
        lax.all_gather(hidden_in, "tcol", axis=0, tiled=True),
        effective,
        preferred_element_type=jnp.float32,
    )
    teacher = lax.psum_scatter(
        partial_value.astype(jnp.bfloat16), "trow", scatter_dimension=1, tiled=True
    ).astype(jnp.float32)
    hidden = (residual.astype(jnp.float32) + teacher).astype(jnp.bfloat16)
    projected = lax.psum_scatter(
        jnp.dot(hidden, projector, preferred_element_type=jnp.float32),
        ("trow", "tcol"),
        scatter_dimension=0,
        tiled=True,
    )
    passage = segments[0]
    same = (passage[:, None] == passage[None, :]).astype(jnp.float32)
    lengths = jnp.sum(same, axis=1)
    weight_all = jnp.float32(tok_group) / (COUNT * lengths)
    offset = lax.axis_index(("trow", "tcol")) * owned
    weight_rows = lax.dynamic_slice_in_dim(weight_all, offset, owned, 0)
    error = projected - student.astype(jnp.float32)
    scaled_f = weight_rows[:, None] * error
    student_grad = -scaled_f
    scaled = scaled_f.astype(jnp.bfloat16)
    local_grad = lax.dot_general(
        hidden,
        lax.all_gather(scaled, ("trow", "tcol"), axis=0, tiled=True),
        (((0,), (0,)), ((), ())),
        preferred_element_type=jnp.float32,
    )
    total_grad = lax.psum(local_grad.astype(jnp.bfloat16), "dp").astype(jnp.float32)
    factor = 1.0 / math.sqrt(tok_group * lax.axis_size("dp"))
    return (student_grad, total_grad * factor)


def solution(mesh):
    in_specs = (
        P(("dp", "tcol"), "trow"),
        P("trow", "tcol"),
        P("trow", "tcol"),
        P("dp", ("tcol", "trow")),
        P(("tcol", "trow"), None),
        P(("dp", "trow", "tcol"), None),
        P("dp", None),
    )
    out_specs = (P(("dp", "trow", "tcol"), None), P(("tcol", "trow"), None))
    return jax.shard_map(shards, mesh=mesh, in_specs=in_specs, out_specs=out_specs, check_vma=False)
```

profile of v0, /device:TPU:16, one launch (start us, length us, event | category | flops | bytes accessed | tf_op | source)
XLA Modules:
  0.0 1016.7 jit_solution(14135340873058124511)
XLA Ops:
  7.2 0.0 all-gather.4.cloned.1.call-start
  7.2 0.7 all-gather.4.cloned.1.call-update
  7.9 0.0 reduce-scatter.2.cloned.1.call-start
  8.0 0.8 copy.11
  8.7 117.5 %all-gather.4.cloned.1.call-done = bf16[512,1792]{1,0:T(8,128)(2,1)} async-done(((bf16[64,1792]{1,0:T(8,128)(2,1)}), bf16[512,1792]{1,0:T(8,128)(2,1)}) %all-gather.4.cloned.1.call-update) | async-done | bytes 1835024 | tf_op jit(solution)/shard_map/all_gather | solution.py:25
  126.3 0.5 mul.42
  126.8 1.5 copy-done.1
  128.3 0.6 copy-done.2
  128.9 3.3 fusion.6
  132.2 0.0 all-reduce.6.cloned.1.call-start
  132.3 99.2 %reduce-scatter.2.cloned.1.call-done = bf16[512,64]{0,1:T(8,128)(2,1)} async-done(((bf16[512,1024]{0,1:T(8,128)(2,1)}), bf16[512,64]{0,1:T(8,128)(2,1)}) %reduce-scatter.2.cloned.1.call-update) | async-done | bytes 65552 | tf_op jit(solution)/shard_map/reduce_scatter | solution.py:29
  231.5 3.1 fusion.9
  234.7 0.0 all-gather.6.cloned.1.call-start
  234.7 1.3 dynamic-slice
  236.6 0.2 convert_reduce_fusion
  236.9 0.1 dynamic_slice.3
  237.0 347.2 %all-reduce.6.cloned.1.call-done = f32[512,1536]{1,0:T(8,128)} async-done(((f32[512,1536]{1,0:T(8,128)}), f32[512,1536]{1,0:T(8,128)}) %all-reduce.6.cloned.1.call-update) | async-done | bytes 3145744
  584.2 1.5 convert_bitcast_fusion
  585.7 0.0 all-reduce.4.cloned.1.call-start
  585.8 356.1 %all-gather.6.cloned.1.call-done = bf16[128,4,1536]{2,1,0:T(4,128)(2,1)} async-done(((bf16[1,4,1536]{2,1,0:T(4,128)(2,1)}), bf16[128,4,1536]{2,1,0:T(4,128)(2,1)}) %all-gather.6.cloned.1.call-update) | async-done | bytes 1572880 | tf_op jit(solution)/shard_map/all_gather | solution.py:51
  941.8 2.7 reshape.11
  944.6 1.1 convolution_convert_fusion
  945.7 62.7 %all-reduce.4.cloned.1.call-done = bf16[64,1536]{1,0:T(8,128)(2,1)} async-done(((bf16[64,1536]{1,0:T(8,128)(2,1)}), bf16[64,1536]{1,0:T(8,128)(2,1)}) %all-reduce.4.cloned.1.call-update) | async-done | bytes 196624 | tf_op jit(solution)/shard_map/psum | solution.py:55
  1008.4 1.7 convert_multiply_fusion
  (17 shorter events, 0.1 us)
Async XLA Ops:
  7.2 224.3 %copy-start = (bf16[64,1536]{1,0:T(8,128)(2,1)S(1)}, bf16[64,1536]{1,0:T(8,128)(2,1)}, u32[]{:S(2)}) copy-start(bf16[64,1536]{1,0:T(8,128)(2,1)} %param.11) | copy-start | bytes 589828
  7.2 119.1 %all-gather.4.cloned.1.call-start = ((), (), s32[]{:S(2)}) async-start(), calls=%async_computation.1 | async-start | bytes 2064384 | tf_op jit(solution)/shard_map/all_gather | solution.py:25
  7.9 223.6 %reduce-scatter.2.cloned.1.call-start = ((), (), s32[]{:S(2)}) async-start(), calls=%async_computation.2 | async-start | bytes 1114112 | tf_op jit(solution)/shard_map/reduce_scatter | solution.py:29
  126.3 2.0 copy-start.1
  126.3 2.6 copy-start.2
  128.9 102.6 %copy-start.3 = (bf16[512,64]{0,1:T(8,128)(2,1)S(1)}, bf16[512,64]{0,1:T(8,128)(2,1)}, u32[]{:S(2)}) copy-start(bf16[512,64]{0,1:T(8,128)(2,1)} %param.10) | copy-start | bytes 196612
  132.2 104.4 %copy-start.6 = (s32[1,512]{1,0:T(1,128)S(1)}, s32[1,512]{1,0:T(1,128)}, u32[]{:S(2)}) copy-start(s32[1,512]{1,0:T(1,128)} %param.13) | copy-start | bytes 6148
  132.2 452.0 %copy-start.5 = (bf16[4,1536]{1,0:T(4,128)(2,1)S(1)}, bf16[4,1536]{1,0:T(4,128)(2,1)}, u32[]{:S(2)}) copy-start(bf16[4,1536]{1,0:T(4,128)(2,1)} %param.12) | copy-start | bytes 36868
  132.2 452.0 %all-reduce.6.cloned.1.call-start = ((), (), s32[]{:S(2)}) async-start(), calls=%async_computation.5 | async-start | bytes 6291456
  234.6 710.0 %copy-start.4 = (bf16[512,64]{0,1:T(8,128)(2,1)S(1)}, bf16[512,64]{0,1:T(8,128)(2,1)}, u32[]{:S(2)}) copy-start(bf16[512,64]{0,1:T(8,128)(2,1)} %reduce-scatter.2.cloned.1.call-done) | copy-start | bytes 196612
  234.7 707.2 %all-gather.6.cloned.1.call-start = ((), (), s32[]{:S(2)}) async-start(), calls=%async_computation.4 | async-start | bytes 1585152 | tf_op jit(solution)/shard_map/all_gather | solution.py:51
  585.7 422.7 %all-reduce.4.cloned.1.call-start = ((), (), s32[]{:S(2)}) async-start(), calls=%async_computation.3 | async-start | bytes 393216 | tf_op jit(solution)/shard_map/psum | solution.py:55
Sparse Core Ops, SparseCore 0:
  11.2 115.0 all-gather.3
  132.3 99.1 reduce-scatter.1
  235.4 348.8 all-reduce.5
  587.0 354.7 all-gather.5
  945.8 62.5 all-reduce.3
where the time goes:
time: 1020 us
  waiting for transfers between devices  984 us (96%)
  between operations  14.5 us (1%)
    all_gather x1, waiting for transfers between devices, shards(): lax.all_gather(scaled, ('trow', 'tcol'), axis=0, tiled=True)  356 us
    unnamed x6, waiting for transfers between devices  348 us
    all_gather x1, waiting for transfers between devices, shards(): lax.all_gather(hidden_in, 'tcol', axis=0, tiled=True)  118 us
    reduce_scatter x1, waiting for transfers between devices, shards(): lax.psum_scatter(partial_value.astype(jnp.bfloat16), 'trow', scatter_dime...  99.2 us
    psum x1, waiting for transfers between devices, shards(): lax.psum(local_grad.astype(jnp.bfloat16), 'dp').astype(jnp.float32)  62.7 us
  transfers between devices with their start and end apart: 5, of which 5 were waited for; matrix products, arithmetic and copies ran while one was open for 0% of the time, Pallas kernels for 0%

commit v1 on v0

v1 whole, which is shorter than its diff:
```python
import math

import jax
import jax.numpy as jnp
from jax import lax
from jax.sharding import PartitionSpec as P

BLOCK = 128
COUNT = 8
BF = jnp.bfloat16
F32 = jnp.float32


def swap(x, axis, mask):
    return lax.ppermute(x, axis, [(i, i ^ mask) for i in range(lax.axis_size(axis))])


def pick(x, index, axis):
    return lax.dynamic_index_in_dim(x, index, axis, keepdims=False)


def halve(x, axis, mask, bit, at):
    got = swap(pick(x, 1 - bit, at), axis, mask)
    return (pick(x, bit, at).astype(F32) + got.astype(F32)).astype(BF)


def join(x, axis, mask, bit, at):
    got = swap(x, axis, mask)
    return jnp.where(bit == 0, jnp.concatenate([x, got], at), jnp.concatenate([got, x], at))


def shards(hidden_in, down_weight, block_scales, residual, projector, student, segments):
    x, t, c = lax.axis_index("dp"), lax.axis_index("trow"), lax.axis_index("tcol")
    core, zl0, zl1, zl2 = t & 1, (t >> 1) & 1, (t >> 2) & 1, (t >> 3) & 1
    zh, y0, y1 = c & 1, (c >> 1) & 1, (c >> 2) & 1
    rows, cols = down_weight.shape

    far = swap(hidden_in, "tcol", 1)
    near_all = [hidden_in] + [swap(hidden_in, "tcol", 2 * k) for k in (1, 2, 3)]
    far_all = [far] + [swap(far, "tcol", 2 * k) for k in (1, 2, 3)]

    pg = pick(projector.reshape(4, 16, -1), x, 0)[None, None]
    pg = pg.reshape(1, 1, 1, 16, -1)
    pg = join(pg, "trow", 8, zl2, 0)
    zparts = pg
    got = swap(zparts, "trow", 4)
    a, b = jnp.stack([zparts, got], 1), jnp.stack([got, zparts], 1)
    pg = jnp.where(zl1 == 0, a, b).reshape(4, 1, 1, 16, -1)
    got = swap(pg, "trow", 2)
    a, b = jnp.stack([pg, got], 1), jnp.stack([got, pg], 1)
    pg = jnp.where(zl0 == 0, a, b).reshape(8, 1, 1, 16, -1)
    pg = join(pg, "dp", 1, x & 1, 2)
    got = swap(pg, "dp", 2)
    pg = jnp.where((x >> 1) == 0, jnp.concatenate([pg, got], 2), jnp.concatenate([got, pg], 2))
    pg = join(pg, "trow", 1, core, 1)
    pg = pg.reshape(cols, -1)

    effective = (
        (
            down_weight.reshape(rows // BLOCK, BLOCK, cols // BLOCK, BLOCK).astype(F32)
            * block_scales[:, None, :, None]
        )
        .reshape(rows, cols)
        .astype(BF)
    )
    slots = c ^ jnp.array([0, 2, 4, 6, 1, 3, 5, 7], jnp.int32)
    res = jnp.take(residual.reshape(8, 64, 64), slots, axis=0).reshape(512, 64)
    place = (jnp.arange(cols)[None, :] == t * 64 + jnp.arange(64)[:, None]).astype(BF)
    part = jnp.dot(jnp.concatenate(near_all + far_all, 0), effective, preferred_element_type=F32)
    part = (part + jnp.dot(res, place, preferred_element_type=F32)).astype(BF)

    acc = halve(part.reshape(8, 2, 32, cols), "trow", 1, core, 1)
    acc = halve(acc.reshape(2, 4, 32, cols), "trow", 2, zh ^ zl0, 0)
    acc = halve(acc.reshape(2, 2, 32, cols), "trow", 4, y0 ^ zl1, 1)
    hid = halve(acc, "trow", 8, y1 ^ zl2, 0)

    hid_all = jnp.concatenate([hid] + [swap(hid, "dp", k) for k in (1, 2, 3)], 0)

    mine = (jnp.arange(32) // 4 == c)[:, None]
    own_student = jnp.where(mine, jnp.tile(student.astype(F32), (8, 1)), 0.0)
    err = jnp.dot(hid, pg, preferred_element_type=F32) - own_student
    err = err + swap(err.astype(BF), "tcol", 1).astype(F32)
    sent = err.astype(BF)
    err = err + sum(swap(sent, "tcol", 2 * k).astype(F32) for k in (1, 2, 3))

    passage = segments[0]
    same = (passage[:, None] == passage[None, :]).astype(F32)
    weight_all = F32(512) / (COUNT * jnp.sum(same, axis=1))
    weight = lax.dynamic_slice_in_dim(weight_all, t * 32, 32, 0)
    scaled_f = weight[:, None] * err
    student_grad = -lax.dynamic_slice_in_dim(scaled_f, c * 4, 4, 0)
    scaled = scaled_f.astype(BF)

    quarter = lambda k: lax.dynamic_slice_in_dim(scaled, (x ^ k) * 384, 384, 1)
    scaled_all = jnp.concatenate([quarter(0)] + [swap(quarter(k), "dp", k) for k in (1, 2, 3)], 0)
    grad = lax.dot_general(hid_all, scaled_all, (((0,), (0,)), ((), ())), preferred_element_type=F32)
    grad = grad.astype(BF)
    grad = halve(grad.reshape(8, 2, 64, 384), "trow", 1, core, 1)
    grad = halve(grad.reshape(4, 2, 64, 384), "trow", 2, zl0, 1)
    grad = halve(grad.reshape(2, 2, 64, 384), "trow", 4, zl1, 1)
    grad = halve(grad, "trow", 8, zl2, 0)
    pieces = jnp.stack([grad] + [swap(grad, "dp", k) for k in (1, 2, 3)])
    total = jnp.concatenate([pick(pieces, x ^ k, 0) for k in range(4)], 1)
    factor = 1.0 / math.sqrt(512 * lax.axis_size("dp"))
    return (student_grad, total.astype(F32) * factor)


def solution(mesh):
    in_specs = (
        P(("dp", "tcol"), "trow"),
        P("trow", "tcol"),
        P("trow", "tcol"),
        P("dp", ("tcol", "trow")),
        P(("tcol", "trow"), None),
        P(("dp", "trow", "tcol"), None),
        P("dp", None),
    )
    out_specs = (P(("dp", "trow", "tcol"), None), P(("tcol", "trow"), None))
    return jax.shard_map(shards, mesh=mesh, in_specs=in_specs, out_specs=out_specs, check_vma=False)
```

time: 1020 us -> 244 us (0.24)
  the two profiles are of different devices: /device:TPU:16 before, /device:TPU:2 now
where the time goes in v1:
time: 244 us; the launch traced here: 243 us
  starting transfers between devices  123 us (50%)
  waiting for transfers between devices  97.9 us (40%)
  local copies, waits for them, and re-layouts  11 us (5%)
  other arithmetic  6.16 us (3%)
  matrix products  3.76 us (2%)
    ppermute x34, starting transfers between devices, swap(): lax.ppermute(x, axis, [(i, i ^ mask) for i in range(lax.axis_size(axis))])  123 us
    ppermute x34, waiting for transfers between devices, swap(): lax.ppermute(x, axis, [(i, i ^ mask) for i in range(lax.axis_size(axis))])  97.9 us
    unnamed x21, local copies, waits for them, and re-layouts  7.51 us
  transfers between devices with their start and end apart: 34, of which 18 were waited for; matrix products, arithmetic and copies ran while one was open for 6% of the time, Pallas kernels for 0%

profile of v1, /device:TPU:2, one launch (start us, length us, event | category | flops | bytes accessed | tf_op | source)
XLA Modules:
  0.0 243.0 jit_solution(15930024150197202401)
XLA Ops:
  0.6 3.6 %collective-permute-start = (bf16[64,1792]{1,0:T(8,128)(2,1)}, bf16[64,1792]{1,0:T(8,128)(2,1)S(1)}, u32[]{:S(2)}, u32[]{:S(2)}) collective-permute-start(bf16[64,1792]{1,0:T(8,128)(2,1)} %param.8), channel_id=1, source_target_pairs={{0,2},{1,3},{2,0},{3,1},{4,6},{5,7},{6,4},{7,5},{8,10},{9,11},{10,... | collective-permute-start | bytes 688136 | tf_op jit(solution)/shard_map/ppermute | solution.py:15
  4.3 4.8 %collective-permute-start.1 = (bf16[64,1792]{1,0:T(8,128)(2,1)}, bf16[64,1792]{1,0:T(8,128)(2,1)S(1)}, u32[]{:S(2)}, u32[]{:S(2)}) collective-permute-start(bf16[64,1792]{1,0:T(8,128)(2,1)} %param.8), channel_id=1, source_target_pairs={{0,4},{1,5},{2,6},{3,7},{4,0},{5,1},{6,2},{7,3},{8,12},{9,13},{10,... | collective-permute-start | bytes 688136 | tf_op jit(solution)/shard_map/ppermute | solution.py:15
  11.2 15.7 %collective-permute-start.3 = (bf16[64,1792]{1,0:T(8,128)(2,1)}, bf16[64,1792]{1,0:T(8,128)(2,1)S(1)}, u32[]{:S(2)}, u32[]{:S(2)}) collective-permute-start(bf16[64,1792]{1,0:T(8,128)(2,1)} %param.8), channel_id=1, source_target_pairs={{0,1},{1,0},{2,3},{3,2},{4,5},{5,4},{6,7},{7,6},{8,9},{9,8},{10,11... | collective-permute-start | bytes 688136 | tf_op jit(solution)/shard_map/ppermute | solution.py:15
  27.8 4.3 %collective-permute-start.11 = (bf16[1,1,1,16,1536]{4,3,0,2,1:T(8,128)(2,1)S(1)}, bf16[1,1,1,16,1536]{4,3,0,2,1:T(8,128)(2,1)S(1)}, u32[]{:S(2)}, u32[]{:S(2)}) collective-permute-start(bf16[1,1,1,16,1536]{4,3,0,2,1:T(8,128)(2,1)S(1)} %get-tuple-element.11), channel_id=1, source_target_pairs={{0,64},{8,72},{16,80},{24,88},{32,96},{40,104},{48,112},{56,120},{... | collective-permute-start | bytes 147464 | tf_op jit(solution)/shard_map/ppermute | solution.py:15
  35.9 15.6 %collective-permute-done.11 = bf16[1,1,1,16,1536]{4,3,0,2,1:T(8,128)(2,1)S(1)} collective-permute-done((bf16[1,1,1,16,1536]{4,3,0,2,1:T(8,128)(2,1)S(1)}, bf16[1,1,1,16,1536]{4,3,0,2,1:T(8,128)(2,1)S(1)}, u32[]{:S(2)}, u32[]{:S(2)}) %collective-permute-start.11) | collective-permute-done | bytes 49184 | tf_op jit(solution)/shard_map/ppermute | solution.py:15
  53.5 6.7 %collective-permute-done.12 = bf16[2,1,1,16,1536]{4,3,0,2,1:T(8,128)(2,1)S(1)} collective-permute-done((bf16[2,1,1,16,1536]{4,3,0,2,1:T(8,128)(2,1)S(1)}, bf16[2,1,1,16,1536]{4,3,0,2,1:T(8,128)(2,1)S(1)}, u32[]{:S(2)}, u32[]{:S(2)}) %collective-permute-start.12) | collective-permute-done | bytes 98336 | tf_op jit(solution)/shard_map/ppermute | solution.py:15
  64.3 6.0 %collective-permute-start.5 = (bf16[64,1792]{1,0:T(8,128)(2,1)S(1)}, bf16[64,1792]{1,0:T(8,128)(2,1)S(1)}, u32[]{:S(2)}, u32[]{:S(2)}) collective-permute-start(bf16[64,1792]{1,0:T(8,128)(2,1)S(1)} %collective-permute-done.3), channel_id=1, source_target_pairs={{0,4},{1,5},{2,6},{3,7},{4,0},{5,1},{6,2},{7,3},{8,12},{9,13},{10,... | collective-permute-start | bytes 688136 | tf_op jit(solution)/shard_map/ppermute | solution.py:15
  79.7 4.1 %collective-permute-done.6 = bf16[64,1792]{1,0:T(8,128)(2,1)S(1)} collective-permute-done((bf16[64,1792]{1,0:T(8,128)(2,1)S(1)}, bf16[64,1792]{1,0:T(8,128)(2,1)S(1)}, u32[]{:S(2)}, u32[]{:S(2)}) %collective-permute-start.6) | collective-permute-done | bytes 229408 | tf_op jit(solution)/shard_map/ppermute | solution.py:15
  87.7 4.2 %collective-permute-start.15 = (bf16[8,1,2,16,1536]{4,3,0,2,1:T(8,128)(2,1)S(1)}, bf16[8,1,2,16,1536]{4,3,0,2,1:T(8,128)(2,1)S(1)}, u32[]{:S(2)}, u32[]{:S(2)}) collective-permute-start(bf16[8,1,2,16,1536]{4,3,0,2,1:T(8,128)(2,1)S(1)} %maximum_select_fusion.3), channel_id=1, source_target_pairs={{0,256},{128,384},{256,0},{384,128},{1,257},{129,385},{257,1},{385... | collective-permute-start | bytes 2359304 | tf_op jit(solution)/shard_map/ppermute | solution.py:15
  98.2 10.7 %collective-permute-done.15 = bf16[8,1,2,16,1536]{4,3,0,2,1:T(8,128)(2,1)S(1)} collective-permute-done((bf16[8,1,2,16,1536]{4,3,0,2,1:T(8,128)(2,1)S(1)}, bf16[8,1,2,16,1536]{4,3,0,2,1:T(8,128)(2,1)S(1)}, u32[]{:S(2)}, u32[]{:S(2)}) %collective-permute-start.15) | collective-permute-done | bytes 786464 | tf_op jit(solution)/shard_map/ppermute | solution.py:15
  114.7 7.2 %collective-permute-done.8 = bf16[4,32,1024]{2,1,0:T(8,128)(2,1)S(1)} collective-permute-done((bf16[4,32,1024]{2,1,0:T(8,128)(2,1)S(1)}, bf16[4,32,1024]{2,1,0:T(8,128)(2,1)S(1)}, u32[]{:S(2)}, u32[]{:S(2)}) %collective-permute-start.8) | collective-permute-done | bytes 262176 | tf_op jit(solution)/shard_map/ppermute | solution.py:15
  124.1 8.6 %collective-permute-done.9 = bf16[2,32,1024]{2,1,0:T(8,128)(2,1)S(1)} collective-permute-done((bf16[2,32,1024]{2,1,0:T(8,128)(2,1)S(1)}, bf16[2,32,1024]{2,1,0:T(8,128)(2,1)S(1)}, u32[]{:S(2)}, u32[]{:S(2)}) %collective-permute-start.9) | collective-permute-done | bytes 131104 | tf_op jit(solution)/shard_map/ppermute | solution.py:15
  132.8 5.9 %collective-permute-start.10 = (bf16[32,1024]{1,0:T(8,128)(2,1)S(1)}, bf16[32,1024]{1,0:T(8,128)(2,1)S(1)}, u32[]{:S(2)}, u32[]{:S(2)}) collective-permute-start(bf16[32,1024]{1,0:T(8,128)(2,1)S(1)} %dynamic-slice_bitcast_fusion.6), channel_id=1, source_target_pairs={{0,64},{8,72},{16,80},{24,88},{32,96},{40,104},{48,112},{56,120},{... | collective-permute-start | bytes 196616 | tf_op jit(solution)/shard_map/ppermute | solution.py:15
  138.8 5.9 %collective-permute-done.10 = bf16[32,1024]{1,0:T(8,128)(2,1)S(1)} collective-permute-done((bf16[32,1024]{1,0:T(8,128)(2,1)S(1)}, bf16[32,1024]{1,0:T(8,128)(2,1)S(1)}, u32[]{:S(2)}, u32[]{:S(2)}) %collective-permute-start.10) | collective-permute-done | bytes 65568 | tf_op jit(solution)/shard_map/ppermute | solution.py:15
  148.0 5.4 %collective-permute-start.17 = (bf16[32,1536]{1,0:T(8,128)(2,1)S(1)}, bf16[32,1536]{1,0:T(8,128)(2,1)S(1)}, u32[]{:S(2)}, u32[]{:S(2)}) collective-permute-start(bf16[32,1536]{1,0:T(8,128)(2,1)S(1)} %get-tuple-element.16), channel_id=1, source_target_pairs={{0,1},{1,0},{2,3},{3,2},{4,5},{5,4},{6,7},{7,6},{8,9},{9,8},{10,11... | collective-permute-start | bytes 294920 | tf_op jit(solution)/shard_map/ppermute | solution.py:15
  153.7 10.2 %collective-permute-done.17 = bf16[32,1536]{1,0:T(8,128)(2,1)S(1)} collective-permute-done((bf16[32,1536]{1,0:T(8,128)(2,1)S(1)}, bf16[32,1536]{1,0:T(8,128)(2,1)S(1)}, u32[]{:S(2)}, u32[]{:S(2)}) %collective-permute-start.17) | collective-permute-done | bytes 98336 | tf_op jit(solution)/shard_map/ppermute | solution.py:15
  163.9 4.7 %collective-permute-start.20 = (bf16[32,1536]{1,0:T(8,128)(2,1)S(1)}, bf16[32,1536]{1,0:T(8,128)(2,1)S(1)}, u32[]{:S(2)}, u32[]{:S(2)}) collective-permute-start(bf16[32,1536]{1,0:T(8,128)(2,1)S(1)} %fusion.20), channel_id=1, source_target_pairs={{0,6},{1,7},{2,4},{3,5},{4,2},{5,3},{6,0},{7,1},{8,14},{9,15},{10,... | collective-permute-start | bytes 294920 | tf_op jit(solution)/shard_map/ppermute | solution.py:15
  180.2 3.5 %collective-permute-start.21 = (bf16[32,1024]{1,0:T(8,128)(2,1)S(1)}, bf16[32,1024]{1,0:T(8,128)(2,1)S(1)}, u32[]{:S(2)}, u32[]{:S(2)}) collective-permute-start(bf16[32,1024]{1,0:T(8,128)(2,1)S(1)} %fusion.21), channel_id=1, source_target_pairs={{0,128},{128,0},{256,384},{384,256},{1,129},{129,1},{257,385},{385... | collective-permute-start | bytes 196616 | tf_op jit(solution)/shard_map/ppermute | solution.py:15
  190.2 3.5 %collective-permute-start.24 = (bf16[32,384]{1,0:T(8,128)(2,1)S(1)}, bf16[32,384]{1,0:T(8,128)(2,1)S(1)}, u32[]{:S(2)}, u32[]{:S(2)}) collective-permute-start(bf16[32,384]{1,0:T(8,128)(2,1)S(1)} %get-tuple-element.15), channel_id=1, source_target_pairs={{0,128},{128,0},{256,384},{384,256},{1,129},{129,1},{257,385},{385... | collective-permute-start | bytes 73736 | tf_op jit(solution)/shard_map/ppermute | solution.py:15
  202.0 6.9 %collective-permute-done.28 = bf16[4,64,384]{2,1,0:T(8,128)(2,1)S(1)} collective-permute-done((bf16[4,64,384]{2,1,0:T(8,128)(2,1)S(1)}, bf16[4,64,384]{2,1,0:T(8,128)(2,1)S(1)}, u32[]{:S(2)}, u32[]{:S(2)}) %collective-permute-start.28) | collective-permute-done | bytes 196640 | tf_op jit(solution)/shard_map/ppermute | solution.py:15
  211.8 6.2 %collective-permute-done.29 = bf16[2,64,384]{2,1,0:T(8,128)(2,1)S(1)} collective-permute-done((bf16[2,64,384]{2,1,0:T(8,128)(2,1)S(1)}, bf16[2,64,384]{2,1,0:T(8,128)(2,1)S(1)}, u32[]{:S(2)}, u32[]{:S(2)}) %collective-permute-start.29) | collective-permute-done | bytes 98336 | tf_op jit(solution)/shard_map/ppermute | solution.py:15
  218.0 4.7 %collective-permute-start.30 = (bf16[64,384]{1,0:T(8,128)(2,1)S(1)}, bf16[64,384]{1,0:T(8,128)(2,1)S(1)}, u32[]{:S(2)}, u32[]{:S(2)}) collective-permute-start(bf16[64,384]{1,0:T(8,128)(2,1)S(1)} %dynamic-slice_bitcast_fusion.11), channel_id=1, source_target_pairs={{0,64},{8,72},{16,80},{24,88},{32,96},{40,104},{48,112},{56,120},{... | collective-permute-start | bytes 147464 | tf_op jit(solution)/shard_map/ppermute | solution.py:15
  222.7 5.9 %collective-permute-done.30 = bf16[64,384]{1,0:T(8,128)(2,1)S(1)} collective-permute-done((bf16[64,384]{1,0:T(8,128)(2,1)S(1)}, bf16[64,384]{1,0:T(8,128)(2,1)S(1)}, u32[]{:S(2)}, u32[]{:S(2)}) %collective-permute-start.30) | collective-permute-done | bytes 49184 | tf_op jit(solution)/shard_map/ppermute | solution.py:15
  228.6 4.2 %collective-permute-start.33 = (bf16[64,384]{1,0:T(8,128)(2,1)S(1)}, bf16[64,384]{1,0:T(8,128)(2,1)S(1)}, u32[]{:S(2)}, u32[]{:S(2)}) collective-permute-start(bf16[64,384]{1,0:T(8,128)(2,1)S(1)} %fusion.31), channel_id=1, source_target_pairs={{0,384},{128,256},{256,128},{384,0},{1,385},{129,257},{257,129},{3... | collective-permute-start | bytes 147464 | tf_op jit(solution)/shard_map/ppermute | solution.py:15
  (117 shorter events, 83.2 us)
Async XLA Ops:
  0.6 63.7 %collective-permute-start = (bf16[64,1792]{1,0:T(8,128)(2,1)}, bf16[64,1792]{1,0:T(8,128)(2,1)S(1)}, u32[]{:S(2)}, u32[]{:S(2)}) collective-permute-start(bf16[64,1792]{1,0:T(8,128)(2,1)} %param.8), channel_id=1, source_target_pairs={{0,2},{1,3},{2,0},{3,1},{4,6},{5,7},{6,4},{7,5},{8,10},{9,11},{10,... | collective-permute-start | bytes 688136 | tf_op jit(solution)/shard_map/ppermute | solution.py:15
  4.3 66.8 %collective-permute-start.1 = (bf16[64,1792]{1,0:T(8,128)(2,1)}, bf16[64,1792]{1,0:T(8,128)(2,1)S(1)}, u32[]{:S(2)}, u32[]{:S(2)}) collective-permute-start(bf16[64,1792]{1,0:T(8,128)(2,1)} %param.8), channel_id=1, source_target_pairs={{0,4},{1,5},{2,6},{3,7},{4,0},{5,1},{6,2},{7,3},{8,12},{9,13},{10,... | collective-permute-start | bytes 688136 | tf_op jit(solution)/shard_map/ppermute | solution.py:15
  9.1 64.9 %collective-permute-start.2 = (bf16[64,1792]{1,0:T(8,128)(2,1)}, bf16[64,1792]{1,0:T(8,128)(2,1)S(1)}, u32[]{:S(2)}, u32[]{:S(2)}) collective-permute-start(bf16[64,1792]{1,0:T(8,128)(2,1)} %param.8), channel_id=1, source_target_pairs={{0,6},{1,7},{2,4},{3,5},{4,2},{5,3},{6,0},{7,1},{8,14},{9,15},{10,... | collective-permute-start | bytes 688136 | tf_op jit(solution)/shard_map/ppermute | solution.py:15
  11.2 50.9 %collective-permute-start.3 = (bf16[64,1792]{1,0:T(8,128)(2,1)}, bf16[64,1792]{1,0:T(8,128)(2,1)S(1)}, u32[]{:S(2)}, u32[]{:S(2)}) collective-permute-start(bf16[64,1792]{1,0:T(8,128)(2,1)} %param.8), channel_id=1, source_target_pairs={{0,1},{1,0},{2,3},{3,2},{4,5},{5,4},{6,7},{7,6},{8,9},{9,8},{10,11... | collective-permute-start | bytes 688136 | tf_op jit(solution)/shard_map/ppermute | solution.py:15
  27.8 23.7 %collective-permute-start.11 = (bf16[1,1,1,16,1536]{4,3,0,2,1:T(8,128)(2,1)S(1)}, bf16[1,1,1,16,1536]{4,3,0,2,1:T(8,128)(2,1)S(1)}, u32[]{:S(2)}, u32[]{:S(2)}) collective-permute-start(bf16[1,1,1,16,1536]{4,3,0,2,1:T(8,128)(2,1)S(1)} %get-tuple-element.11), channel_id=1, source_target_pairs={{0,64},{8,72},{16,80},{24,88},{32,96},{40,104},{48,112},{56,120},{... | collective-permute-start | bytes 147464 | tf_op jit(solution)/shard_map/ppermute | solution.py:15
  60.2 15.2 %collective-permute-start.13 = (bf16[4,1,1,16,1536]{4,3,0,2,1:T(8,128)(2,1)S(1)}, bf16[4,1,1,16,1536]{4,3,0,2,1:T(8,128)(2,1)S(1)}, u32[]{:S(2)}, u32[]{:S(2)}) collective-permute-start(bf16[4,1,1,16,1536]{4,3,0,2,1:T(8,128)(2,1)S(1)} %bitcast.115), channel_id=1, source_target_pairs={{0,16},{8,24},{16,0},{24,8},{32,48},{40,56},{48,32},{56,40},{64,80... | collective-permute-start | bytes 589832 | tf_op jit(solution)/shard_map/ppermute | solution.py:15
  62.1 15.8 %collective-permute-start.4 = (bf16[64,1792]{1,0:T(8,128)(2,1)S(1)}, bf16[64,1792]{1,0:T(8,128)(2,1)S(1)}, u32[]{:S(2)}, u32[]{:S(2)}) collective-permute-start(bf16[64,1792]{1,0:T(8,128)(2,1)S(1)} %collective-permute-done.3), channel_id=1, source_target_pairs={{0,2},{1,3},{2,0},{3,1},{4,6},{5,7},{6,4},{7,5},{8,10},{9,11},{10,... | collective-permute-start | bytes 688136 | tf_op jit(solution)/shard_map/ppermute | solution.py:15
  64.3 14.6 %collective-permute-start.5 = (bf16[64,1792]{1,0:T(8,128)(2,1)S(1)}, bf16[64,1792]{1,0:T(8,128)(2,1)S(1)}, u32[]{:S(2)}, u32[]{:S(2)}) collective-permute-start(bf16[64,1792]{1,0:T(8,128)(2,1)S(1)} %collective-permute-done.3), channel_id=1, source_target_pairs={{0,4},{1,5},{2,6},{3,7},{4,0},{5,1},{6,2},{7,3},{8,12},{9,13},{10,... | collective-permute-start | bytes 688136 | tf_op jit(solution)/shard_map/ppermute | solution.py:15
  71.1 12.7 %collective-permute-start.6 = (bf16[64,1792]{1,0:T(8,128)(2,1)S(1)}, bf16[64,1792]{1,0:T(8,128)(2,1)S(1)}, u32[]{:S(2)}, u32[]{:S(2)}) collective-permute-start(bf16[64,1792]{1,0:T(8,128)(2,1)S(1)} %collective-permute-done.3), channel_id=1, source_target_pairs={{0,6},{1,7},{2,4},{3,5},{4,2},{5,3},{6,0},{7,1},{8,14},{9,15},{10,... | collective-permute-start | bytes 688136 | tf_op jit(solution)/shard_map/ppermute | solution.py:15
  75.4 12.1 %collective-permute-start.14 = (bf16[8,1,1,16,1536]{4,3,0,2,1:T(8,128)(2,1)S(1)}, bf16[8,1,1,16,1536]{4,3,0,2,1:T(8,128)(2,1)S(1)}, u32[]{:S(2)}, u32[]{:S(2)}) collective-permute-start(bf16[8,1,1,16,1536]{4,3,0,2,1:T(8,128)(2,1)S(1)} %bitcast.105), channel_id=1, source_target_pairs={{0,128},{128,0},{256,384},{384,256},{1,129},{129,1},{257,385},{385... | collective-permute-start | bytes 1179656 | tf_op jit(solution)/shard_map/ppermute | solution.py:15
  87.7 21.2 %collective-permute-start.15 = (bf16[8,1,2,16,1536]{4,3,0,2,1:T(8,128)(2,1)S(1)}, bf16[8,1,2,16,1536]{4,3,0,2,1:T(8,128)(2,1)S(1)}, u32[]{:S(2)}, u32[]{:S(2)}) collective-permute-start(bf16[8,1,2,16,1536]{4,3,0,2,1:T(8,128)(2,1)S(1)} %maximum_select_fusion.3), channel_id=1, source_target_pairs={{0,256},{128,384},{256,0},{384,128},{1,257},{129,385},{257,1},{385... | collective-permute-start | bytes 2359304 | tf_op jit(solution)/shard_map/ppermute | solution.py:15
  96.2 14.9 %collective-permute-start.7 = (bf16[8,32,1024]{2,1,0:T(8,128)(2,1)S(1)}, bf16[8,32,1024]{2,1,0:T(8,128)(2,1)S(1)}, u32[]{:S(2)}, u32[]{:S(2)}) collective-permute-start(bf16[8,32,1024]{2,1,0:T(8,128)(2,1)S(1)} %dynamic-slice_bitcast_fusion), channel_id=1, source_target_pairs={{0,8},{8,0},{16,24},{24,16},{32,40},{40,32},{48,56},{56,48},{64,72... | collective-permute-start | bytes 1572872 | tf_op jit(solution)/shard_map/ppermute | solution.py:15
  109.2 35.5 %collective-permute-start.16 = (bf16[8,1,4,16,1536]{4,3,0,2,1:T(8,128)(2,1)S(1)}, bf16[8,1,4,16,1536]{4,3,0,2,1:T(8,128)(2,1)}, u32[]{:S(2)}, u32[]{:S(2)}) collective-permute-start(bf16[8,1,4,16,1536]{4,3,0,2,1:T(8,128)(2,1)S(1)} %maximum_select_fusion.1), channel_id=1, source_target_pairs={{0,8},{8,0},{16,24},{24,16},{32,40},{40,32},{48,56},{56,48},{64,72... | collective-permute-start | bytes 4718600 | tf_op jit(solution)/shard_map/ppermute | solution.py:15
  122.1 10.7 %collective-permute-start.9 = (bf16[2,32,1024]{2,1,0:T(8,128)(2,1)S(1)}, bf16[2,32,1024]{2,1,0:T(8,128)(2,1)S(1)}, u32[]{:S(2)}, u32[]{:S(2)}) collective-permute-start(bf16[2,32,1024]{2,1,0:T(8,128)(2,1)S(1)} %dynamic-slice_bitcast_fusion.4), channel_id=1, source_target_pairs={{0,32},{8,40},{16,48},{24,56},{32,0},{40,8},{48,16},{56,24},{64,96... | collective-permute-start | bytes 393224 | tf_op jit(solution)/shard_map/ppermute | solution.py:15
  132.8 11.8 %collective-permute-start.10 = (bf16[32,1024]{1,0:T(8,128)(2,1)S(1)}, bf16[32,1024]{1,0:T(8,128)(2,1)S(1)}, u32[]{:S(2)}, u32[]{:S(2)}) collective-permute-start(bf16[32,1024]{1,0:T(8,128)(2,1)S(1)} %dynamic-slice_bitcast_fusion.6), channel_id=1, source_target_pairs={{0,64},{8,72},{16,80},{24,88},{32,96},{40,104},{48,112},{56,120},{... | collective-permute-start | bytes 196616 | tf_op jit(solution)/shard_map/ppermute | solution.py:15
  148.0 15.8 %collective-permute-start.17 = (bf16[32,1536]{1,0:T(8,128)(2,1)S(1)}, bf16[32,1536]{1,0:T(8,128)(2,1)S(1)}, u32[]{:S(2)}, u32[]{:S(2)}) collective-permute-start(bf16[32,1536]{1,0:T(8,128)(2,1)S(1)} %get-tuple-element.16), channel_id=1, source_target_pairs={{0,1},{1,0},{2,3},{3,2},{4,5},{5,4},{6,7},{7,6},{8,9},{9,8},{10,11... | collective-permute-start | bytes 294920 | tf_op jit(solution)/shard_map/ppermute | solution.py:15
  163.9 16.3 %collective-permute-start.20 = (bf16[32,1536]{1,0:T(8,128)(2,1)S(1)}, bf16[32,1536]{1,0:T(8,128)(2,1)S(1)}, u32[]{:S(2)}, u32[]{:S(2)}) collective-permute-start(bf16[32,1536]{1,0:T(8,128)(2,1)S(1)} %fusion.20), channel_id=1, source_target_pairs={{0,6},{1,7},{2,4},{3,5},{4,2},{5,3},{6,0},{7,1},{8,14},{9,15},{10,... | collective-permute-start | bytes 294920 | tf_op jit(solution)/shard_map/ppermute | solution.py:15
  168.6 15.1 %collective-permute-start.19 = (bf16[32,1536]{1,0:T(8,128)(2,1)S(1)}, bf16[32,1536]{1,0:T(8,128)(2,1)S(1)}, u32[]{:S(2)}, u32[]{:S(2)}) collective-permute-start(bf16[32,1536]{1,0:T(8,128)(2,1)S(1)} %fusion.20), channel_id=1, source_target_pairs={{0,4},{1,5},{2,6},{3,7},{4,0},{5,1},{6,2},{7,3},{8,12},{9,13},{10,... | collective-permute-start | bytes 294920 | tf_op jit(solution)/shard_map/ppermute | solution.py:15
  170.5 13.2 %collective-permute-start.18 = (bf16[32,1536]{1,0:T(8,128)(2,1)S(1)}, bf16[32,1536]{1,0:T(8,128)(2,1)S(1)}, u32[]{:S(2)}, u32[]{:S(2)}) collective-permute-start(bf16[32,1536]{1,0:T(8,128)(2,1)S(1)} %fusion.20), channel_id=1, source_target_pairs={{0,2},{1,3},{2,0},{3,1},{4,6},{5,7},{6,4},{7,5},{8,10},{9,11},{10,... | collective-permute-start | bytes 294920 | tf_op jit(solution)/shard_map/ppermute | solution.py:15
  173.8 16.3 %collective-permute-start.23 = (bf16[32,1024]{1,0:T(8,128)(2,1)S(1)}, bf16[32,1024]{1,0:T(8,128)(2,1)S(1)}, u32[]{:S(2)}, u32[]{:S(2)}) collective-permute-start(bf16[32,1024]{1,0:T(8,128)(2,1)S(1)} %fusion.21), channel_id=1, source_target_pairs={{0,384},{128,256},{256,128},{384,0},{1,385},{129,257},{257,129},{3... | collective-permute-start | bytes 196616 | tf_op jit(solution)/shard_map/ppermute | solution.py:15
  177.2 16.4 %collective-permute-start.22 = (bf16[32,1024]{1,0:T(8,128)(2,1)S(1)}, bf16[32,1024]{1,0:T(8,128)(2,1)S(1)}, u32[]{:S(2)}, u32[]{:S(2)}) collective-permute-start(bf16[32,1024]{1,0:T(8,128)(2,1)S(1)} %fusion.21), channel_id=1, source_target_pairs={{0,256},{128,384},{256,0},{384,128},{1,257},{129,385},{257,1},{385... | collective-permute-start | bytes 196616 | tf_op jit(solution)/shard_map/ppermute | solution.py:15
  180.2 13.5 %collective-permute-start.21 = (bf16[32,1024]{1,0:T(8,128)(2,1)S(1)}, bf16[32,1024]{1,0:T(8,128)(2,1)S(1)}, u32[]{:S(2)}, u32[]{:S(2)}) collective-permute-start(bf16[32,1024]{1,0:T(8,128)(2,1)S(1)} %fusion.21), channel_id=1, source_target_pairs={{0,128},{128,0},{256,384},{384,256},{1,129},{129,1},{257,385},{385... | collective-permute-start | bytes 196616 | tf_op jit(solution)/shard_map/ppermute | solution.py:15
  218.0 10.6 %collective-permute-start.30 = (bf16[64,384]{1,0:T(8,128)(2,1)S(1)}, bf16[64,384]{1,0:T(8,128)(2,1)S(1)}, u32[]{:S(2)}, u32[]{:S(2)}) collective-permute-start(bf16[64,384]{1,0:T(8,128)(2,1)S(1)} %dynamic-slice_bitcast_fusion.11), channel_id=1, source_target_pairs={{0,64},{8,72},{16,80},{24,88},{32,96},{40,104},{48,112},{56,120},{... | collective-permute-start | bytes 147464 | tf_op jit(solution)/shard_map/ppermute | solution.py:15
  228.6 10.7 %collective-permute-start.33 = (bf16[64,384]{1,0:T(8,128)(2,1)S(1)}, bf16[64,384]{1,0:T(8,128)(2,1)S(1)}, u32[]{:S(2)}, u32[]{:S(2)}) collective-permute-start(bf16[64,384]{1,0:T(8,128)(2,1)S(1)} %fusion.31), channel_id=1, source_target_pairs={{0,384},{128,256},{256,128},{384,0},{1,385},{129,257},{257,129},{3... | collective-permute-start | bytes 147464 | tf_op jit(solution)/shard_map/ppermute | solution.py:15
  (16 other events, 174.2 us)

commit v2 on v0

v2 whole, which is shorter than its diff:
```python
import math

import jax
import jax.numpy as jnp
from jax import lax
from jax.experimental import pallas as pl
from jax.experimental.pallas import tpu as pltpu
from jax.sharding import Mesh
from jax.sharding import PartitionSpec as P

BLOCK = 128
COUNT = 8
BF = jnp.bfloat16
F32 = jnp.float32


def swap(x, axis, mask):
    return lax.ppermute(x, axis, [(i, i ^ mask) for i in range(lax.axis_size(axis))])


def pick(x, index, axis):
    return lax.dynamic_index_in_dim(x, index, axis, keepdims=False)


def exchange(x, axes):
    return lax.all_to_all(x, axes, 0, 0, tiled=True)


def combine_kernel(c_ref, near_ref, near_got_ref, far_ref, far_got_ref, res_ref, out_ref):
    c = c_ref[0]
    for zs, (keep, got) in enumerate(((near_ref, near_got_ref), (far_ref, far_got_ref))):
        for ys in range(4):
            at = c ^ (2 * ys + zs)
            value = keep[ys].astype(F32) + got[ys].astype(F32) + res_ref[at].astype(F32)
            out_ref[at] = value.astype(BF)


def combine(c, near, near_got, far, far_got, res):
    vmem = pl.BlockSpec(memory_space=pltpu.VMEM)
    return pl.pallas_call(
        combine_kernel,
        out_shape=jax.ShapeDtypeStruct(res.shape, BF),
        in_specs=[pl.BlockSpec(memory_space=pltpu.SMEM)] + [vmem] * 5,
        out_specs=vmem,
        compiler_params=pltpu.CompilerParams(vmem_limit_bytes=16 * 1024 * 1024),
        cost_estimate=pl.CostEstimate(flops=10**6, bytes_accessed=4 * 10**6, transcendentals=0),
    )(c.reshape(1), near, near_got, far, far_got, res)


def shards(hidden_in, down_weight, block_scales, residual, projector, student, segments):
    x, zl, core = lax.axis_index("dp"), lax.axis_index("zl"), lax.axis_index("co")
    y, zh = lax.axis_index("y"), lax.axis_index("zh")
    c = 2 * y + zh
    rows, cols = down_weight.shape
    half = cols // 2

    pg = lax.all_gather(projector, "zl", axis=0, tiled=True)

    far = swap(hidden_in, "zh", 1)
    near_all = [hidden_in] + [swap(hidden_in, "y", k) for k in (1, 2, 3)]
    far_all = [far] + [swap(far, "y", k) for k in (1, 2, 3)]

    effective = (
        (
            down_weight.reshape(rows // BLOCK, BLOCK, cols // BLOCK, BLOCK).astype(F32)
            * block_scales[:, None, :, None]
        )
        .reshape(rows, cols)
        .astype(BF)
    )
    k = jnp.arange(cols)
    source = (k % half) // 64 * 128 + jnp.where(k < half, 1 - core, core) * 64 + k % 64
    order = (jnp.arange(cols)[:, None] == source[None, :]).astype(BF)
    effective = jnp.dot(effective, order, preferred_element_type=F32).astype(BF)
    effective = lax.optimization_barrier(effective)
    place = (jnp.arange(half)[None, :] == zl * 64 + jnp.arange(64)[:, None]).astype(BF)
    res = jnp.dot(residual, place, preferred_element_type=F32).astype(BF).reshape(8, 64, half)

    def bands(pieces):
        part = jnp.dot(jnp.concatenate(pieces, 0), effective, preferred_element_type=F32).astype(BF)
        part = part.reshape(4, 64, cols)
        return part[..., half:], swap(part[..., :half], "co", 1)

    near, near_got = bands(near_all)
    far, far_got = bands(far_all)
    acc = combine(c, near, near_got, far, far_got, res)
    hid = jnp.sum(exchange(acc, "zl").astype(F32), 0).astype(BF)
    hid_all = jnp.stack([hid] + [swap(hid, "dp", k) for k in (1, 2, 3)])
    hid_all = jnp.take(hid_all, x ^ jnp.arange(4), axis=0).reshape(256, half)

    mine = (jnp.arange(64) // 4 == core * 8 + c)[:, None]
    own_student = jnp.where(mine, jnp.tile(student.astype(F32), (16, 1)), 0.0)
    err = jnp.dot(hid, pg, preferred_element_type=F32) - own_student
    err = jnp.sum(exchange(err.astype(BF).reshape(8, 8, -1), ("co", "y")).astype(F32), 0)
    err = err + swap(err.astype(BF), "zh", 1).astype(F32)

    passage = segments[0]
    same = (passage[:, None] == passage[None, :]).astype(F32)
    weight_all = F32(512) / (COUNT * jnp.sum(same, axis=1))
    weight = lax.dynamic_slice_in_dim(weight_all, zl * 64 + core * 32 + y * 8, 8, 0)
    scaled_f = weight[:, None] * err
    student_grad = -lax.dynamic_slice_in_dim(scaled_f, zh * 4, 4, 0)
    scaled = lax.all_gather(scaled_f.astype(BF), "co")

    quarters = jnp.moveaxis(scaled.reshape(2, 8, 4, 384), 2, 0)[:, None]
    quarters = jnp.broadcast_to(quarters, (4, 4, 2, 8, 384)).reshape(16, 2, 8, 384)
    scaled_all = exchange(quarters, ("dp", "y")).reshape(4, 4, 2, 8, 384)
    scaled_all = jnp.swapaxes(scaled_all, 1, 2).reshape(256, 384)
    grad = lax.dot_general(hid_all, scaled_all, (((0,), (0,)), ((), ())), preferred_element_type=F32)
    grad = jnp.sum(exchange(grad.astype(BF).reshape(8, 64, 384), "zl").astype(F32), 0).astype(BF)
    pieces = exchange(jnp.broadcast_to(grad[None], (4, 64, 384)), "dp")
    total = jnp.concatenate([pieces[i] for i in range(4)], 1)
    factor = 1.0 / math.sqrt(512 * lax.axis_size("dp"))
    return (student_grad, total.astype(F32) * factor)


def solution(mesh):
    fine = Mesh(mesh.devices.reshape(4, 8, 2, 4, 2), ("dp", "zl", "co", "y", "zh"))
    trow, tcol = ("zl", "co"), ("y", "zh")
    in_specs = (
        P(("dp",) + tcol, trow),
        P(trow, tcol),
        P(trow, tcol),
        P("dp", tcol + trow),
        P(tcol + trow, None),
        P(("dp",) + trow + tcol, None),
        P("dp", None),
    )
    out_specs = (P(("dp",) + trow + tcol, None), P(tcol + trow, None))
    return jax.shard_map(shards, mesh=fine, in_specs=in_specs, out_specs=out_specs, check_vma=False)
```

time: 1020 us -> 205 us (0.20)
  the two profiles are of different devices: /device:TPU:16 before, /device:TPU:2 now
where the time goes in v2:
time: 205 us; the launch traced here: 204 us
  starting transfers between devices  94.8 us (46%)
  waiting for transfers between devices  70.8 us (35%)
  between operations  14.4 us (7%)
  matrix products  14.2 us (7%)
  local copies, waits for them, and re-layouts  5.15 us (3%)
  other arithmetic  2.07 us (1%)
    all_to_all x5, waiting for transfers between devices, exchange(): return lax.all_to_all(x, axes, 0, 0, tiled=True)  59.2 us
    ppermute x13, starting transfers between devices, swap(): lax.ppermute(x, axis, [(i, i ^ mask) for i in range(lax.axis_size(axis))])  58.1 us
    all_to_all x5, starting transfers between devices, exchange(): return lax.all_to_all(x, axes, 0, 0, tiled=True)  36.6 us
    ppermute x13, waiting for transfers between devices, swap(): lax.ppermute(x, axis, [(i, i ^ mask) for i in range(lax.axis_size(axis))])  11.5 us
    dot_general x1, matrix products, shards(): effective = jnp.dot(effective, order, preferred_element_type=F32).astype(BF)  6.04 us
    dot_general x2, matrix products, bands(): jnp.dot(jnp.concatenate(pieces, 0), effective, preferred_element_type=F32)  4.28 us
  transfers between devices with their start and end apart: 19, of which 7 were waited for; matrix products, arithmetic and copies ran while one was open for 7% of the time, Pallas kernels for 0%

profile of v2, /device:TPU:2, one launch (start us, length us, event | category | flops | bytes accessed | tf_op | source)
XLA Modules:
  0.0 204.3 jit_solution(8982006843662497550)
XLA Ops:
  7.2 15.7 %collective-permute-start.4 = (bf16[64,1792]{1,0:T(8,128)(2,1)}, bf16[64,1792]{1,0:T(8,128)(2,1)S(1)}, u32[]{:S(2)}, u32[]{:S(2)}) collective-permute-start(bf16[64,1792]{1,0:T(8,128)(2,1)} %param.7), channel_id=1, source_target_pairs={{0,1},{1,0},{2,3},{3,2},{4,5},{5,4},{6,7},{7,6},{8,9},{9,8},{10,11... | collective-permute-start | bytes 688136 | tf_op jit(solution)/shard_map/ppermute | solution.py:18
  23.0 3.5 %collective-permute-start = (bf16[64,1792]{1,0:T(8,128)(2,1)}, bf16[64,1792]{1,0:T(8,128)(2,1)S(1)}, u32[]{:S(2)}, u32[]{:S(2)}) collective-permute-start(bf16[64,1792]{1,0:T(8,128)(2,1)} %param.7), channel_id=1, source_target_pairs={{0,2},{2,0},{4,6},{6,4},{1,3},{3,1},{5,7},{7,5},{8,10},{10,8},{12,... | collective-permute-start | bytes 688136 | tf_op jit(solution)/shard_map/ppermute | solution.py:18
  26.5 4.8 %collective-permute-start.1 = (bf16[64,1792]{1,0:T(8,128)(2,1)}, bf16[64,1792]{1,0:T(8,128)(2,1)S(1)}, u32[]{:S(2)}, u32[]{:S(2)}) collective-permute-start(bf16[64,1792]{1,0:T(8,128)(2,1)} %param.7), channel_id=1, source_target_pairs={{0,4},{2,6},{4,0},{6,2},{1,5},{3,7},{5,1},{7,3},{8,12},{10,14},{12... | collective-permute-start | bytes 688136 | tf_op jit(solution)/shard_map/ppermute | solution.py:18
  36.3 6.0 %fusion.2 = bf16[1792,1024]{1,0:T(8,128)(2,1)} fusion(f32[224,8,8,128]{3,2,1,0:T(8,128)S(1)} %bitcast.48, bf16[1792,1024]{1,0:T(8,128)(2,1)S(1)} %copy-done.3, s32[1024]{0:T(1024)S(1)} %fusion.25), kind=kOutput, calls=%fused_computation.5 | convolution fusion | flops 3766484992 | bytes 14684160 | tf_op jit(solution)/shard_map/dot_general | solution.py:74
  42.3 2.5 %collective-permute-start.5 = (bf16[64,1792]{1,0:T(8,128)(2,1)S(1)}, bf16[64,1792]{1,0:T(8,128)(2,1)S(1)}, u32[]{:S(2)}, u32[]{:S(2)}) collective-permute-start(bf16[64,1792]{1,0:T(8,128)(2,1)S(1)} %collective-permute-done.4), channel_id=1, source_target_pairs={{0,2},{2,0},{4,6},{6,4},{1,3},{3,1},{5,7},{7,5},{8,10},{10,8},{12,... | collective-permute-start | bytes 688136 | tf_op jit(solution)/shard_map/ppermute | solution.py:18
  44.9 6.0 %collective-permute-start.6 = (bf16[64,1792]{1,0:T(8,128)(2,1)S(1)}, bf16[64,1792]{1,0:T(8,128)(2,1)S(1)}, u32[]{:S(2)}, u32[]{:S(2)}) collective-permute-start(bf16[64,1792]{1,0:T(8,128)(2,1)S(1)} %collective-permute-done.4), channel_id=1, source_target_pairs={{0,4},{2,6},{4,0},{6,2},{1,5},{3,7},{5,1},{7,3},{8,12},{10,14},{12... | collective-permute-start | bytes 688136 | tf_op jit(solution)/shard_map/ppermute | solution.py:18
  50.9 2.1 %collective-permute-start.7 = (bf16[64,1792]{1,0:T(8,128)(2,1)S(1)}, bf16[64,1792]{1,0:T(8,128)(2,1)S(1)}, u32[]{:S(2)}, u32[]{:S(2)}) collective-permute-start(bf16[64,1792]{1,0:T(8,128)(2,1)S(1)} %collective-permute-done.4), channel_id=1, source_target_pairs={{0,6},{2,4},{4,2},{6,0},{1,7},{3,5},{5,3},{7,1},{8,14},{10,12},{12... | collective-permute-start | bytes 688136 | tf_op jit(solution)/shard_map/ppermute | solution.py:18
  53.1 3.2 %convolution_convert_fusion.2 = bf16[256,1024]{1,0:T(8,128)(2,1)S(1)} fusion(bf16[1792,1024]{1,0:T(8,128)(2,1)} %fusion.2, bf16[64,1792]{1,0:T(8,128)(2,1)S(1)} %collective-permute-done.2, bf16[64,1792]{1,0:T(8,128)(2,1)S(1)} %collective-permute-done.1, bf16[64,1792]{1,0:T(8,128)(2,1)S(1)} %collective-permute-done, bf16[64,1792]{1,0:T(8,128)(2,1)S(1)} %copy-done.4), kind=kOutput, calls=%fused_computation.12 | convolution fusion | flops 943456256 | bytes 5111808 | tf_op jit(solution)/shard_map/dot_general | solution.py:80
  58.2 4.4 %collective-permute-done.7 = bf16[64,1792]{1,0:T(8,128)(2,1)S(1)} collective-permute-done((bf16[64,1792]{1,0:T(8,128)(2,1)S(1)}, bf16[64,1792]{1,0:T(8,128)(2,1)S(1)}, u32[]{:S(2)}, u32[]{:S(2)}) %collective-permute-start.7) | collective-permute-done | bytes 229408 | tf_op jit(solution)/shard_map/ppermute | solution.py:18
  68.2 9.5 %all-to-all-start = ((bf16[8,64,512]{2,1,0:T(8,128)(2,1)}), bf16[8,64,512]{2,1,0:T(8,128)(2,1)S(1)}, u32[]{:S(2)}, u32[]{:S(2)}) async-start(bf16[8,64,512]{2,1,0:T(8,128)(2,1)} %shard_map.86), calls=%async_computation | async-start | bytes 1048576 | tf_op jit(solution)/shard_map/all_to_all | solution.py:26
  78.3 26.4 %all-to-all-done = bf16[8,64,512]{2,1,0:T(8,128)(2,1)S(1)} async-done(((bf16[8,64,512]{2,1,0:T(8,128)(2,1)}), bf16[8,64,512]{2,1,0:T(8,128)(2,1)S(1)}, u32[]{:S(2)}, u32[]{:S(2)}) %all-to-all-start) | async-done | bytes 524320 | tf_op jit(solution)/shard_map/all_to_all | solution.py:26
  104.8 2.5 %fusion.5 = bf16[8,8,1536]{2,1,0:T(8,128)(2,1)} fusion(bf16[64,512]{1,0:T(8,128)(2,1)S(1)} %reduce_sum.43, bf16[512,1536]{1,0:T(8,128)(2,1)} %all-gather.3.cloned.1.call-done, f32[64,1536]{1,0:T(8,128)S(1)} %tile.10, pred[64]{0:T(512)(128)(4,1)S(1)} %fusion.34), kind=kOutput, calls=%fused_computation.8 | convolution fusion | flops 100958208 | bytes 2228288 | tf_op jit(solution)/shard_map/dot_general | solution.py:93
  107.2 9.2 %all-to-all-start.1 = ((bf16[8,8,1536]{2,1,0:T(8,128)(2,1)}), bf16[8,8,1536]{2,1,0:T(8,128)(2,1)S(1)}, u32[]{:S(2)}, u32[]{:S(2)}) async-start(bf16[8,8,1536]{2,1,0:T(8,128)(2,1)} %fusion.5), calls=%async_computation.1 | async-start | bytes 393216 | tf_op jit(solution)/shard_map/all_to_all | solution.py:26
  116.4 3.3 %collective-permute-start.12 = (bf16[64,512]{1,0:T(8,128)(2,1)S(1)}, bf16[64,512]{1,0:T(8,128)(2,1)S(1)}, u32[]{:S(2)}, u32[]{:S(2)}) collective-permute-start(bf16[64,512]{1,0:T(8,128)(2,1)S(1)} %reduce_sum.43), channel_id=1, source_target_pairs={{0,384},{128,256},{256,128},{384,0},{1,385},{129,257},{257,129},{3... | collective-permute-start | bytes 196616 | tf_op jit(solution)/shard_map/ppermute | solution.py:18
  119.7 3.6 %collective-permute-start.10 = (bf16[64,512]{1,0:T(8,128)(2,1)S(1)}, bf16[64,512]{1,0:T(8,128)(2,1)S(1)}, u32[]{:S(2)}, u32[]{:S(2)}) collective-permute-start(bf16[64,512]{1,0:T(8,128)(2,1)S(1)} %reduce_sum.43), channel_id=1, source_target_pairs={{0,128},{128,0},{256,384},{384,256},{1,129},{129,1},{257,385},{385... | collective-permute-start | bytes 196616 | tf_op jit(solution)/shard_map/ppermute | solution.py:18
  123.4 2.3 %collective-permute-start.11 = (bf16[64,512]{1,0:T(8,128)(2,1)S(1)}, bf16[64,512]{1,0:T(8,128)(2,1)S(1)}, u32[]{:S(2)}, u32[]{:S(2)}) collective-permute-start(bf16[64,512]{1,0:T(8,128)(2,1)S(1)} %reduce_sum.43), channel_id=1, source_target_pairs={{0,256},{128,384},{256,0},{384,128},{1,257},{129,385},{257,1},{385... | collective-permute-start | bytes 196616 | tf_op jit(solution)/shard_map/ppermute | solution.py:18
  125.7 8.2 %collective-permute-start.9 = (bf16[8,1536]{1,0:T(8,128)(2,1)S(1)}, bf16[8,1536]{1,0:T(8,128)(2,1)S(1)}, u32[]{:S(2)}, u32[]{:S(2)}) collective-permute-start(bf16[8,1536]{1,0:T(8,128)(2,1)S(1)} %convert_element_type.66), channel_id=1, source_target_pairs={{0,1},{1,0},{2,3},{3,2},{4,5},{5,4},{6,7},{7,6},{8,9},{9,8},{10,11... | collective-permute-start | bytes 73736 | tf_op jit(solution)/shard_map/ppermute | solution.py:18
  134.6 6.0 %collective-permute-done.9 = bf16[8,1536]{1,0:T(8,128)(2,1)S(1)} collective-permute-done((bf16[8,1536]{1,0:T(8,128)(2,1)S(1)}, bf16[8,1536]{1,0:T(8,128)(2,1)S(1)}, u32[]{:S(2)}, u32[]{:S(2)}) %collective-permute-start.9) | collective-permute-done | bytes 24608 | tf_op jit(solution)/shard_map/ppermute | solution.py:18
  143.2 8.4 %all-to-all-start.2 = ((bf16[16,2,8,384]{3,2,1,0:T(8,128)(2,1)}), bf16[16,2,8,384]{3,2,1,0:T(8,128)(2,1)S(1)}, u32[]{:S(2)}, u32[]{:S(2)}) async-start(bf16[16,2,8,384]{3,2,1,0:T(8,128)(2,1)} %bitcast.15), calls=%async_computation.2 | async-start | bytes 393216 | tf_op jit(solution)/shard_map/all_to_all | solution.py:26
  151.7 6.5 %all-to-all-done.2 = bf16[16,2,8,384]{3,2,1,0:T(8,128)(2,1)S(1)} async-done(((bf16[16,2,8,384]{3,2,1,0:T(8,128)(2,1)}), bf16[16,2,8,384]{3,2,1,0:T(8,128)(2,1)S(1)}, u32[]{:S(2)}, u32[]{:S(2)}) %all-to-all-start.2) | async-done | bytes 196640 | tf_op jit(solution)/shard_map/all_to_all | solution.py:26
  159.3 4.7 %all-to-all-start.3 = ((bf16[8,64,384]{2,1,0:T(8,128)(2,1)}), bf16[8,64,384]{2,1,0:T(8,128)(2,1)S(1)}, u32[]{:S(2)}, u32[]{:S(2)}) async-start(bf16[8,64,384]{2,1,0:T(8,128)(2,1)} %bitcast.19), calls=%async_computation.3 | async-start | bytes 786432 | tf_op jit(solution)/shard_map/all_to_all | solution.py:26
  164.0 22.1 %all-to-all-done.3 = bf16[8,64,384]{2,1,0:T(8,128)(2,1)S(1)} async-done(((bf16[8,64,384]{2,1,0:T(8,128)(2,1)}), bf16[8,64,384]{2,1,0:T(8,128)(2,1)S(1)}, u32[]{:S(2)}, u32[]{:S(2)}) %all-to-all-start.3) | async-done | bytes 393248 | tf_op jit(solution)/shard_map/all_to_all | solution.py:26
  186.8 4.9 %all-to-all-start.4 = ((bf16[4,64,384]{2,1,0:T(8,128)(2,1)}), bf16[4,64,384]{2,1,0:T(8,128)(2,1)S(1)}, u32[]{:S(2)}, u32[]{:S(2)}) async-start(bf16[4,64,384]{2,1,0:T(8,128)(2,1)} %broadcast_in_dim.56), calls=%async_computation.4 | async-start | bytes 393216 | tf_op jit(solution)/shard_map/all_to_all | solution.py:26
  192.4 4.3 %all-to-all-done.4 = bf16[4,64,384]{2,1,0:T(8,128)(2,1)S(1)} async-done(((bf16[4,64,384]{2,1,0:T(8,128)(2,1)}), bf16[4,64,384]{2,1,0:T(8,128)(2,1)S(1)}, u32[]{:S(2)}, u32[]{:S(2)}) %all-to-all-start.4) | async-done | bytes 196640 | tf_op jit(solution)/shard_map/all_to_all | solution.py:26
  (65 shorter events, 19.8 us)
Async XLA Ops:
  7.2 58.6 %copy-start = (bf16[512,64]{0,1:T(8,128)(2,1)S(1)}, bf16[512,64]{0,1:T(8,128)(2,1)}, u32[]{:S(2)}) copy-start(bf16[512,64]{0,1:T(8,128)(2,1)} %param.10) | copy-start | bytes 196612
  7.2 97.6 %all-gather.3.cloned.1.call-start = ((), (), s32[]{:S(2)}) async-start(), calls=%async_computation.5 | async-start | bytes 1769472 | tf_op jit(solution)/shard_map/all_gather | solution.py:57
  7.2 35.1 %collective-permute-start.4 = (bf16[64,1792]{1,0:T(8,128)(2,1)}, bf16[64,1792]{1,0:T(8,128)(2,1)S(1)}, u32[]{:S(2)}, u32[]{:S(2)}) collective-permute-start(bf16[64,1792]{1,0:T(8,128)(2,1)} %param.7), channel_id=1, source_target_pairs={{0,1},{1,0},{2,3},{3,2},{4,5},{5,4},{6,7},{7,6},{8,9},{9,8},{10,11... | collective-permute-start | bytes 688136 | tf_op jit(solution)/shard_map/ppermute | solution.py:18
  23.0 27.9 %collective-permute-start = (bf16[64,1792]{1,0:T(8,128)(2,1)}, bf16[64,1792]{1,0:T(8,128)(2,1)S(1)}, u32[]{:S(2)}, u32[]{:S(2)}) collective-permute-start(bf16[64,1792]{1,0:T(8,128)(2,1)} %param.7), channel_id=1, source_target_pairs={{0,2},{2,0},{4,6},{6,4},{1,3},{3,1},{5,7},{7,5},{8,10},{10,8},{12,... | collective-permute-start | bytes 688136 | tf_op jit(solution)/shard_map/ppermute | solution.py:18
  26.5 26.6 %collective-permute-start.1 = (bf16[64,1792]{1,0:T(8,128)(2,1)}, bf16[64,1792]{1,0:T(8,128)(2,1)S(1)}, u32[]{:S(2)}, u32[]{:S(2)}) collective-permute-start(bf16[64,1792]{1,0:T(8,128)(2,1)} %param.7), channel_id=1, source_target_pairs={{0,4},{2,6},{4,0},{6,2},{1,5},{3,7},{5,1},{7,3},{8,12},{10,14},{12... | collective-permute-start | bytes 688136 | tf_op jit(solution)/shard_map/ppermute | solution.py:18
  31.3 21.8 %collective-permute-start.2 = (bf16[64,1792]{1,0:T(8,128)(2,1)}, bf16[64,1792]{1,0:T(8,128)(2,1)S(1)}, u32[]{:S(2)}, u32[]{:S(2)}) collective-permute-start(bf16[64,1792]{1,0:T(8,128)(2,1)} %param.7), channel_id=1, source_target_pairs={{0,6},{2,4},{4,2},{6,0},{1,7},{3,5},{5,3},{7,1},{8,14},{10,12},{12... | collective-permute-start | bytes 688136 | tf_op jit(solution)/shard_map/ppermute | solution.py:18
  36.3 16.8 %copy-start.4 = (bf16[64,1792]{1,0:T(8,128)(2,1)S(1)}, bf16[64,1792]{1,0:T(8,128)(2,1)}, u32[]{:S(2)}) copy-start(bf16[64,1792]{1,0:T(8,128)(2,1)} %param.7) | copy-start | bytes 688132
  42.3 20.3 %copy-start.5 = (bf16[1792,1024]{1,0:T(8,128)(2,1)S(1)}, bf16[1792,1024]{1,0:T(8,128)(2,1)}, u32[]{:S(2)}) copy-start(bf16[1792,1024]{1,0:T(8,128)(2,1)} %fusion.2) | copy-start | bytes 11010052
  42.3 15.9 %collective-permute-start.5 = (bf16[64,1792]{1,0:T(8,128)(2,1)S(1)}, bf16[64,1792]{1,0:T(8,128)(2,1)S(1)}, u32[]{:S(2)}, u32[]{:S(2)}) collective-permute-start(bf16[64,1792]{1,0:T(8,128)(2,1)S(1)} %collective-permute-done.4), channel_id=1, source_target_pairs={{0,2},{2,0},{4,6},{6,4},{1,3},{3,1},{5,7},{7,5},{8,10},{10,8},{12,... | collective-permute-start | bytes 688136 | tf_op jit(solution)/shard_map/ppermute | solution.py:18
  44.9 13.3 %collective-permute-start.6 = (bf16[64,1792]{1,0:T(8,128)(2,1)S(1)}, bf16[64,1792]{1,0:T(8,128)(2,1)S(1)}, u32[]{:S(2)}, u32[]{:S(2)}) collective-permute-start(bf16[64,1792]{1,0:T(8,128)(2,1)S(1)} %collective-permute-done.4), channel_id=1, source_target_pairs={{0,4},{2,6},{4,0},{6,2},{1,5},{3,7},{5,1},{7,3},{8,12},{10,14},{12... | collective-permute-start | bytes 688136 | tf_op jit(solution)/shard_map/ppermute | solution.py:18
  50.9 11.7 %collective-permute-start.7 = (bf16[64,1792]{1,0:T(8,128)(2,1)S(1)}, bf16[64,1792]{1,0:T(8,128)(2,1)S(1)}, u32[]{:S(2)}, u32[]{:S(2)}) collective-permute-start(bf16[64,1792]{1,0:T(8,128)(2,1)S(1)} %collective-permute-done.4), channel_id=1, source_target_pairs={{0,6},{2,4},{4,2},{6,0},{1,7},{3,5},{5,3},{7,1},{8,14},{10,12},{12... | collective-permute-start | bytes 688136 | tf_op jit(solution)/shard_map/ppermute | solution.py:18
  56.3 9.9 %collective-permute-start.3 = (bf16[4,64,512]{2,1,0:T(8,128)(2,1)S(1)}, bf16[4,64,512]{2,1,0:T(8,128)(2,1)S(1)}, u32[]{:S(2)}, u32[]{:S(2)}) collective-permute-start(bf16[4,64,512]{2,1,0:T(8,128)(2,1)S(1)} %get-tuple-element.6), channel_id=1, source_target_pairs={{0,8},{8,0},{1,9},{9,1},{2,10},{10,2},{3,11},{11,3},{4,12},{12,4},... | collective-permute-start | bytes 786440 | tf_op jit(solution)/shard_map/ppermute | solution.py:18
  63.7 14.0 %copy-start.1 = (bf16[4,1536]{1,0:T(4,128)(2,1)S(1)}, bf16[4,1536]{1,0:T(4,128)(2,1)}, u32[]{:S(2)}) copy-start(bf16[4,1536]{1,0:T(4,128)(2,1)} %param.12) | copy-start | bytes 36868
  63.8 14.2 %copy-start.2 = (s32[1,512]{1,0:T(1,128)S(1)}, s32[1,512]{1,0:T(1,128)}, u32[]{:S(2)}) copy-start(s32[1,512]{1,0:T(1,128)} %param.13) | copy-start | bytes 6148
  63.8 3.4 %collective-permute-start.8 = (bf16[4,64,512]{2,1,0:T(8,128)(2,1)S(1)}, bf16[4,64,512]{2,1,0:T(8,128)(2,1)S(1)}, u32[]{:S(2)}, u32[]{:S(2)}) collective-permute-start(bf16[4,64,512]{2,1,0:T(8,128)(2,1)S(1)} %get-tuple-element.4), channel_id=1, source_target_pairs={{0,8},{8,0},{1,9},{9,1},{2,10},{10,2},{3,11},{11,3},{4,12},{12,4},... | collective-permute-start | bytes 786440 | tf_op jit(solution)/shard_map/ppermute | solution.py:18
  68.2 36.4 %all-to-all-start = ((bf16[8,64,512]{2,1,0:T(8,128)(2,1)}), bf16[8,64,512]{2,1,0:T(8,128)(2,1)S(1)}, u32[]{:S(2)}, u32[]{:S(2)}) async-start(bf16[8,64,512]{2,1,0:T(8,128)(2,1)} %shard_map.86), calls=%async_computation | async-start | bytes 1048576 | tf_op jit(solution)/shard_map/all_to_all | solution.py:26
  107.2 18.4 %all-to-all-start.1 = ((bf16[8,8,1536]{2,1,0:T(8,128)(2,1)}), bf16[8,8,1536]{2,1,0:T(8,128)(2,1)S(1)}, u32[]{:S(2)}, u32[]{:S(2)}) async-start(bf16[8,8,1536]{2,1,0:T(8,128)(2,1)} %fusion.5), calls=%async_computation.1 | async-start | bytes 393216 | tf_op jit(solution)/shard_map/all_to_all | solution.py:26
  116.4 17.5 %collective-permute-start.12 = (bf16[64,512]{1,0:T(8,128)(2,1)S(1)}, bf16[64,512]{1,0:T(8,128)(2,1)S(1)}, u32[]{:S(2)}, u32[]{:S(2)}) collective-permute-start(bf16[64,512]{1,0:T(8,128)(2,1)S(1)} %reduce_sum.43), channel_id=1, source_target_pairs={{0,384},{128,256},{256,128},{384,0},{1,385},{129,257},{257,129},{3... | collective-permute-start | bytes 196616 | tf_op jit(solution)/shard_map/ppermute | solution.py:18
  119.7 14.3 %collective-permute-start.10 = (bf16[64,512]{1,0:T(8,128)(2,1)S(1)}, bf16[64,512]{1,0:T(8,128)(2,1)S(1)}, u32[]{:S(2)}, u32[]{:S(2)}) collective-permute-start(bf16[64,512]{1,0:T(8,128)(2,1)S(1)} %reduce_sum.43), channel_id=1, source_target_pairs={{0,128},{128,0},{256,384},{384,256},{1,129},{129,1},{257,385},{385... | collective-permute-start | bytes 196616 | tf_op jit(solution)/shard_map/ppermute | solution.py:18
  123.4 10.6 %collective-permute-start.11 = (bf16[64,512]{1,0:T(8,128)(2,1)S(1)}, bf16[64,512]{1,0:T(8,128)(2,1)S(1)}, u32[]{:S(2)}, u32[]{:S(2)}) collective-permute-start(bf16[64,512]{1,0:T(8,128)(2,1)S(1)} %reduce_sum.43), channel_id=1, source_target_pairs={{0,256},{128,384},{256,0},{384,128},{1,257},{129,385},{257,1},{385... | collective-permute-start | bytes 196616 | tf_op jit(solution)/shard_map/ppermute | solution.py:18
  125.7 14.9 %collective-permute-start.9 = (bf16[8,1536]{1,0:T(8,128)(2,1)S(1)}, bf16[8,1536]{1,0:T(8,128)(2,1)S(1)}, u32[]{:S(2)}, u32[]{:S(2)}) collective-permute-start(bf16[8,1536]{1,0:T(8,128)(2,1)S(1)} %convert_element_type.66), channel_id=1, source_target_pairs={{0,1},{1,0},{2,3},{3,2},{4,5},{5,4},{6,7},{7,6},{8,9},{9,8},{10,11... | collective-permute-start | bytes 73736 | tf_op jit(solution)/shard_map/ppermute | solution.py:18
  143.2 14.9 %all-to-all-start.2 = ((bf16[16,2,8,384]{3,2,1,0:T(8,128)(2,1)}), bf16[16,2,8,384]{3,2,1,0:T(8,128)(2,1)S(1)}, u32[]{:S(2)}, u32[]{:S(2)}) async-start(bf16[16,2,8,384]{3,2,1,0:T(8,128)(2,1)} %bitcast.15), calls=%async_computation.2 | async-start | bytes 393216 | tf_op jit(solution)/shard_map/all_to_all | solution.py:26
  159.3 26.8 %all-to-all-start.3 = ((bf16[8,64,384]{2,1,0:T(8,128)(2,1)}), bf16[8,64,384]{2,1,0:T(8,128)(2,1)S(1)}, u32[]{:S(2)}, u32[]{:S(2)}) async-start(bf16[8,64,384]{2,1,0:T(8,128)(2,1)} %bitcast.19), calls=%async_computation.3 | async-start | bytes 786432 | tf_op jit(solution)/shard_map/all_to_all | solution.py:26
  186.8 9.8 %all-to-all-start.4 = ((bf16[4,64,384]{2,1,0:T(8,128)(2,1)}), bf16[4,64,384]{2,1,0:T(8,128)(2,1)S(1)}, u32[]{:S(2)}, u32[]{:S(2)}) async-start(bf16[4,64,384]{2,1,0:T(8,128)(2,1)} %broadcast_in_dim.56), calls=%async_computation.4 | async-start | bytes 393216 | tf_op jit(solution)/shard_map/all_to_all | solution.py:26
  (1 other events, 2.0 us)
Sparse Core Ops, SparseCore 0:
  33.6 65.7 all-gather.2

commit v3 on v2

v3 whole, which is shorter than its diff:
```python
import math

import jax
import jax.numpy as jnp
from jax import lax
from jax.experimental import pallas as pl
from jax.experimental.pallas import tpu as pltpu
from jax.sharding import Mesh
from jax.sharding import PartitionSpec as P

BLOCK = 128
COUNT = 8
BF = jnp.bfloat16
F32 = jnp.float32
MIB = 1024 * 1024
VMEM = pl.BlockSpec(memory_space=pltpu.VMEM)
SMEM = pl.BlockSpec(memory_space=pltpu.SMEM)


def swap(x, axis, mask):
    return lax.ppermute(x, axis, [(i, i ^ mask) for i in range(lax.axis_size(axis))])


def pick(x, index, axis):
    return lax.dynamic_index_in_dim(x, index, axis, keepdims=False)


def exchange(x, axes):
    return lax.all_to_all(x, axes, 0, 0, tiled=True)


def gather(x, axis):
    return exchange(jnp.broadcast_to(x[None], (lax.axis_size(axis),) + x.shape), axis)


def join(x, axis, mask, bit, at):
    got = swap(x, axis, mask)
    return jnp.where(bit == 0, jnp.concatenate([x, got], at), jnp.concatenate([got, x], at))


def after(x, *others):
    return lax.optimization_barrier((x,) + others)[0]


def band_kernel(core_ref, scales_ref, weight_ref, *refs):
    *token_refs, send_ref, keep_ref, total_ref = refs
    step = pl.program_id(0)
    depth, cols = weight_ref.shape
    tokens = jnp.concatenate([r[...] for r in token_refs], 0)
    first = lax.broadcasted_iota(jnp.int32, (1, BLOCK), 1) < 64
    is_one = core_ref[0] == 1
    for m in range(2):
        tiles = []
        for j in range(4 * m, 4 * m + 4):
            column = []
            for i in range(depth // BLOCK):
                block = weight_ref[i * BLOCK : i * BLOCK + BLOCK, j * BLOCK : j * BLOCK + BLOCK].astype(F32)
                column.append((block * scales_ref[step * (depth // BLOCK) + i, j]).astype(BF))
            tiles.append(jnp.concatenate(column, 0))
        part = jnp.dot(tokens, jnp.concatenate(tiles, 1), preferred_element_type=F32)

        @pl.when(step == 0)
        def _():
            total_ref[:, 512 * m : 512 * m + 512] = part

        @pl.when(step == 1)
        def _():
            whole = total_ref[:, 512 * m : 512 * m + 512] + part
            for zp in range(2):
                a = whole[:, BLOCK * zp : BLOCK * zp + BLOCK]
                b = whole[:, BLOCK * zp + 256 : BLOCK * zp + 256 + BLOCK]
                zero = jnp.where(first, a, pltpu.roll(b, 64, 1)).astype(BF)
                one = jnp.where(first, pltpu.roll(a, 64, 1), b).astype(BF)
                at = (slice(None), pl.ds(256 * zp + BLOCK * m, BLOCK))
                send_ref[at] = jnp.where(is_one, zero, one)
                keep_ref[at] = jnp.where(is_one, one, zero)


def band(core, scales, weight, tokens):
    count, (depth, cols) = sum(v.shape[0] for v in tokens), weight.shape
    half = jax.ShapeDtypeStruct((count, cols // 2), BF)
    whole = pl.BlockSpec(half.shape, lambda k: (0, 0))
    return pl.pallas_call(
        band_kernel,
        grid=(2,),
        out_shape=(half, half),
        in_specs=[SMEM, SMEM, pl.BlockSpec((depth // 2, cols), lambda k: (k, 0))]
        + [pl.BlockSpec((v.shape[0], depth // 2), lambda k: (0, k)) for v in tokens],
        out_specs=(whole, whole),
        scratch_shapes=[pltpu.VMEM((count, cols), F32)],
        compiler_params=pltpu.CompilerParams(vmem_limit_bytes=32 * MIB),
        cost_estimate=pl.CostEstimate(flops=10**4, bytes_accessed=10**4, transcendentals=0),
    )(core.reshape(1), scales, weight, *tokens)


def combine_kernel(at_ref, near_ref, near_got_ref, far_ref, far_got_ref, res_ref, out_ref):
    y, zh = at_ref[0], at_ref[1]
    for far, (keep, got) in enumerate(((near_ref, near_got_ref), (far_ref, far_got_ref))):
        for k in range(4):
            to_y, to_z = (k, 1 - zh) if far else (y ^ k, zh)
            value = keep[k].astype(F32) + got[k].astype(F32) + res_ref[2 * to_y + to_z].astype(F32)
            for zp in range(2):
                out_ref[to_y, zp, to_z] = value[:, 256 * zp : 256 * zp + 256].astype(BF)


def combine(at, near, near_got, far, far_got, res):
    return pl.pallas_call(
        combine_kernel,
        out_shape=jax.ShapeDtypeStruct((4, 2, 2, 64, 256), BF),
        in_specs=[SMEM] + [VMEM] * 5,
        out_specs=VMEM,
        compiler_params=pltpu.CompilerParams(vmem_limit_bytes=16 * MIB),
        cost_estimate=pl.CostEstimate(flops=10**4, bytes_accessed=10**4, transcendentals=0),
    )(at, near, near_got, far, far_got, res)


def shards(hidden_in, down_weight, block_scales, residual, projector, student, segments):
    x, zq, zp, core = (lax.axis_index(name) for name in ("dp", "zq", "zp", "co"))
    y, zh = lax.axis_index("y"), lax.axis_index("zh")
    rows, cols = down_weight.shape
    half = cols // 2

    far = swap(hidden_in, "zh", 1)
    near = [hidden_in] + [swap(hidden_in, "y", k) for k in (1, 2, 3)]
    pg = join(pick(projector.reshape(4, 16, -1), x, 0)[None, None], "zq", 2, zq >> 1, 0)
    far, pg, *near = lax.optimization_barrier((far, pg, *near))
    pg = join(pg.reshape(2, 1, 16, -1), "zq", 1, zq & 1, 1).reshape(4, 1, 1, 16, -1)

    send, near = band(core, block_scales, down_weight, near)
    near_got = swap(send, "co", 1)
    far, pg = lax.optimization_barrier((gather(far, "y").reshape(256, rows), pg))
    send, far = band(core, block_scales, down_weight, [far])
    far_got = swap(send, "co", 1)

    pg = join(pg, "dp", 1, x & 1, 2)
    pg = join(pg, "dp", 2, x >> 1, 1).reshape(256, -1)

    column = jnp.arange(half)[None, :]
    place = (column == zp * 256 + zq * 64 + jnp.arange(64)[:, None]).astype(BF)
    res = jnp.dot(residual, place, preferred_element_type=F32).astype(BF).reshape(8, 64, half)
    blocks = lambda v: v.reshape(4, 64, half)
    acc = combine(jnp.stack([y, zh]), blocks(near), blocks(near_got), blocks(far), blocks(far_got), res)
    hid = exchange(acc.reshape(8, BLOCK, 256), ("zq", "zp"))
    hid = jnp.sum(hid.astype(F32), 0).astype(BF)

    mine = (jnp.arange(BLOCK) // 4 == zp * 16 + core * 8 + y * 2 + zh)[:, None]
    own_student = jnp.where(mine, jnp.tile(student.astype(F32), (32, 1)), 0.0)
    err = jnp.dot(hid, pg, preferred_element_type=F32) - own_student
    err = jnp.sum(exchange(err.astype(BF).reshape(16, 8, -1), ("zp", "co", "y")).astype(F32), 0)
    hid_two = after(jnp.stack([hid, swap(hid, "dp", 1)]), err)
    hid_all = jnp.concatenate([hid_two, swap(hid_two, "dp", 2)])
    hid_all = jnp.take(hid_all, x ^ jnp.arange(4), axis=0).reshape(512, 256)
    err = err + swap(err.astype(BF), "zh", 1).astype(F32)

    passage = segments[0]
    same = (passage[:, None] == passage[None, :]).astype(F32)
    weight_all = F32(512) / (COUNT * jnp.sum(same, axis=1))
    weight = lax.dynamic_slice_in_dim(weight_all, zq * 128 + zp * 64 + core * 32 + y * 8, 8, 0)
    scaled_f = weight[:, None] * err
    student_grad = -lax.dynamic_slice_in_dim(scaled_f, zh * 4, 4, 0)
    scaled = lax.all_gather(scaled_f.astype(BF), ("zp", "co"))

    quarters = jnp.moveaxis(scaled.reshape(4, 8, 4, 384), 2, 0)[:, None]
    quarters = jnp.broadcast_to(quarters, (4, 4, 4, 8, 384)).reshape(16, 4, 8, 384)
    scaled_all = exchange(quarters, ("dp", "y")).reshape(4, 4, 4, 8, 384)
    scaled_all = jnp.swapaxes(scaled_all, 1, 2).reshape(512, 384)
    grad = lax.dot_general(hid_all, scaled_all, (((0,), (0,)), ((), ())), preferred_element_type=F32)
    grad = jnp.sum(exchange(grad.astype(BF).reshape(4, 64, 384), "zq").astype(F32), 0).astype(BF)
    pieces = gather(grad, "dp").reshape(4, 64, 384)
    total = jnp.concatenate([pieces[i] for i in range(4)], 1)
    factor = 1.0 / math.sqrt(512 * lax.axis_size("dp"))
    return (student_grad, total.astype(F32) * factor)


def solution(mesh):
    names = ("dp", "zq", "zp", "co", "y", "zh")
    fine = Mesh(mesh.devices.reshape(4, 4, 2, 2, 4, 2), names)
    trow, tcol = names[1:4], names[4:]
    in_specs = (
        P(("dp",) + tcol, trow),
        P(trow, tcol),
        P(trow, tcol),
        P("dp", tcol + trow),
        P(tcol + trow, None),
        P(("dp",) + trow + tcol, None),
        P("dp", None),
    )
    out_specs = (P(("dp",) + trow + tcol, None), P(tcol + trow, None))
    return jax.shard_map(shards, mesh=fine, in_specs=in_specs, out_specs=out_specs, check_vma=False)
```

time: 205 us -> 187 us (0.912)
  between operations: 14.4 us -> 1.07 us
  matrix products: 14.2 us -> 2.4 us
  Pallas kernels: 1 us -> 7.48 us
  starting transfers between devices: 94.8 us -> 89.4 us
  local copies, waits for them, and re-layouts: 5.15 us -> 10.2 us
  blocking collectives: 1.83 us -> 5.32 us
  waiting for transfers between devices: 70.8 us -> 67.9 us
    all_to_all x5 -> x6, waiting for transfers between devices: 59.2 us -> 41 us  [exchange(): return lax.all_to_all(x, axes, 0, 0, tiled=True)]
    ppermute x13, waiting for transfers between devices: 11.5 us -> 26.8 us  [swap(): lax.ppermute(x, axis, [(i, i ^ mask) for i in range(lax.axis_size(axis))])]
    dot_general x3 -> x0, matrix products: 10.3 us -> none  [the longest x1 6.04 us: shards(): effective = jnp.dot(effective, order, preferred_element_type=F32).astype(BF)]
    all_to_all x5 -> x6, starting transfers between devices: 36.6 us -> 28.6 us  [exchange(): return lax.all_to_all(x, axes, 0, 0, tiled=True)]
    pallas_call x1 -> x3, Pallas kernels: 1 us -> 7.48 us  [the longest x2 5.88 us: band(): pl.pallas_call(band_kernel, grid=(2,), out_shape=(half, half), in_specs=[...]
    unnamed x13 -> x15, local copies, waits for them, and re-layouts: 2.3 us -> 6.71 us
    all_gather x1, blocking collectives: 1.83 us -> 5.32 us  [shards(): scaled = lax.all_gather(scaled_f.astype(BF), ('zp', 'co'))]
    ppermute x13, starting transfers between devices: 58.1 us -> 60.8 us  [swap(): lax.ppermute(x, axis, [(i, i ^ mask) for i in range(lax.axis_size(axis))])]
  transfers between devices with their start and end apart: 19 -> 19, of which waited for: 7 -> 12; matrix products, arithmetic and copies ran while one was open for 7% -> 2% of each run, Pallas kernels for 0% -> 3%
where the time goes in v3:
time: 187 us; the launch traced here: 186 us
  starting transfers between devices  89.4 us (48%)
  waiting for transfers between devices  67.9 us (36%)
  local copies, waits for them, and re-layouts  10.2 us (5%)
  Pallas kernels  7.48 us (4%)
  blocking collectives  5.32 us (3%)
  matrix products  2.4 us (1%)
  other arithmetic  2.3 us (1%)
    ppermute x13, starting transfers between devices, swap(): lax.ppermute(x, axis, [(i, i ^ mask) for i in range(lax.axis_size(axis))])  60.8 us
    all_to_all x6, waiting for transfers between devices, exchange(): return lax.all_to_all(x, axes, 0, 0, tiled=True)  41 us
    all_to_all x6, starting transfers between devices, exchange(): return lax.all_to_all(x, axes, 0, 0, tiled=True)  28.6 us
    ppermute x13, waiting for transfers between devices, swap(): lax.ppermute(x, axis, [(i, i ^ mask) for i in range(lax.axis_size(axis))])  26.8 us
    unnamed x15, local copies, waits for them, and re-layouts  6.71 us
    pallas_call x2, Pallas kernels, band(): pl.pallas_call(band_kernel, grid=(2,), out_shape=(half, half), in_specs=[...  5.88 us
    all_gather x1, blocking collectives, shards(): scaled = lax.all_gather(scaled_f.astype(BF), ('zp', 'co'))  5.32 us
  transfers between devices with their start and end apart: 19, of which 12 were waited for; matrix products, arithmetic and copies ran while one was open for 2% of the time, Pallas kernels for 3%

profile of v3, /device:TPU:2, one launch (start us, length us, event | category | flops | bytes accessed | tf_op | source)
XLA Modules:
  0.0 186.0 jit_solution(2058278236342569103)
XLA Ops:
  1.6 9.1 %collective-permute-start.1 = (bf16[1,1,16,1536]{3,2,1,0:T(8,128)(2,1)S(1)}, bf16[1,1,16,1536]{3,2,1,0:T(8,128)(2,1)S(1)}, u32[]{:S(2)}, u32[]{:S(2)}) collective-permute-start(bf16[1,1,16,1536]{3,2,1,0:T(8,128)(2,1)S(1)} %dynamic-slice_bitcast_fusion), channel_id=1, source_target_pairs={{0,64},{32,96},{64,0},{96,32},{1,65},{33,97},{65,1},{97,33},{2,66}... | collective-permute-start | bytes 147464 | tf_op jit(solution)/shard_map/ppermute | solution.py:21
  10.7 10.9 %collective-permute-start = (bf16[64,1792]{1,0:T(8,128)(2,1)}, bf16[64,1792]{1,0:T(8,128)(2,1)S(1)}, u32[]{:S(2)}, u32[]{:S(2)}) collective-permute-start(bf16[64,1792]{1,0:T(8,128)(2,1)} %refs_0_), channel_id=1, source_target_pairs={{0,1},{1,0},{2,3},{3,2},{4,5},{5,4},{6,7},{7,6},{8,9},{9,8},{10,11... | collective-permute-start | bytes 688136 | tf_op jit(solution)/shard_map/ppermute | solution.py:21
  21.6 3.5 %collective-permute-start.2 = (bf16[64,1792]{1,0:T(8,128)(2,1)}, bf16[64,1792]{1,0:T(8,128)(2,1)S(1)}, u32[]{:S(2)}, u32[]{:S(2)}) collective-permute-start(bf16[64,1792]{1,0:T(8,128)(2,1)} %refs_0_), channel_id=1, source_target_pairs={{0,2},{2,0},{4,6},{6,4},{1,3},{3,1},{5,7},{7,5},{8,10},{10,8},{12,... | collective-permute-start | bytes 688136 | tf_op jit(solution)/shard_map/ppermute | solution.py:21
  25.1 4.8 %collective-permute-start.3 = (bf16[64,1792]{1,0:T(8,128)(2,1)}, bf16[64,1792]{1,0:T(8,128)(2,1)S(1)}, u32[]{:S(2)}, u32[]{:S(2)}) collective-permute-start(bf16[64,1792]{1,0:T(8,128)(2,1)} %refs_0_), channel_id=1, source_target_pairs={{0,4},{2,6},{4,0},{6,2},{1,5},{3,7},{5,1},{7,3},{8,12},{10,14},{12... | collective-permute-start | bytes 688136 | tf_op jit(solution)/shard_map/ppermute | solution.py:21
  32.1 5.8 %collective-permute-done.3.refs_2_ = bf16[64,1792]{1,0:T(8,128)(2,1)S(1)} collective-permute-done((bf16[64,1792]{1,0:T(8,128)(2,1)}, bf16[64,1792]{1,0:T(8,128)(2,1)S(1)}, u32[]{:S(2)}, u32[]{:S(2)}) %collective-permute-start.3) | collective-permute-done | bytes 229408 | tf_op jit(solution)/shard_map/ppermute | solution.py:21
  37.9 4.7 %collective-permute-done.4.refs_3_ = bf16[64,1792]{1,0:T(8,128)(2,1)S(1)} collective-permute-done((bf16[64,1792]{1,0:T(8,128)(2,1)}, bf16[64,1792]{1,0:T(8,128)(2,1)S(1)}, u32[]{:S(2)}, u32[]{:S(2)}) %collective-permute-start.4) | collective-permute-done | bytes 229408 | tf_op jit(solution)/shard_map/ppermute | solution.py:21
  43.7 3.5 %all-to-all-start = ((bf16[4,64,1792]{2,1,0:T(8,128)(2,1)}), bf16[4,64,1792]{2,1,0:T(8,128)(2,1)S(1)}, u32[]{:S(2)}, u32[]{:S(2)}) async-start(bf16[4,64,1792]{2,1,0:T(8,128)(2,1)} %broadcast_in_dim.28), calls=%async_computation | async-start | bytes 1835008 | tf_op jit(solution)/shard_map/all_to_all | solution.py:29
  48.0 3.4 %collective-permute-start.6 = (bf16[2,1,16,1536]{3,2,1,0:T(8,128)(2,1)S(1)}, bf16[2,1,16,1536]{3,2,1,0:T(8,128)(2,1)S(1)}, u32[]{:S(2)}, u32[]{:S(2)}) collective-permute-start(bf16[2,1,16,1536]{3,2,1,0:T(8,128)(2,1)S(1)} %maximum_select_fusion.3), channel_id=1, source_target_pairs={{0,32},{32,0},{64,96},{96,64},{1,33},{33,1},{65,97},{97,65},{2,34}... | collective-permute-start | bytes 294920 | tf_op jit(solution)/shard_map/ppermute | solution.py:21
  71.2 6.9 %all-to-all-start.1 = ((bf16[8,128,256]{2,1,0:T(8,128)(2,1)}), bf16[8,128,256]{2,1,0:T(8,128)(2,1)S(1)}, u32[]{:S(2)}, u32[]{:S(2)}) async-start(bf16[8,128,256]{2,1,0:T(8,128)(2,1)} %bitcast.14), calls=%async_computation.1 | async-start | bytes 1048576 | tf_op jit(solution)/shard_map/all_to_all | solution.py:29
  80.6 6.1 %collective-permute-done.8 = bf16[4,1,1,16,1536]{4,3,2,1,0:T(8,128)(2,1)S(1)} collective-permute-done((bf16[4,1,1,16,1536]{4,3,2,1,0:T(8,128)(2,1)S(1)}, bf16[4,1,1,16,1536]{4,3,2,1,0:T(8,128)(2,1)S(1)}, u32[]{:S(2)}, u32[]{:S(2)}) %collective-permute-start.8) | collective-permute-done | bytes 196640 | tf_op jit(solution)/shard_map/ppermute | solution.py:21
  86.7 4.0 %collective-permute-start.9 = (bf16[4,1,2,16,1536]{4,3,2,1,0:T(8,128)(2,1)S(1)}, bf16[4,1,2,16,1536]{4,3,2,1,0:T(8,128)(2,1)S(1)}, u32[]{:S(2)}, u32[]{:S(2)}) collective-permute-start(bf16[4,1,2,16,1536]{4,3,2,1,0:T(8,128)(2,1)S(1)} %maximum_select_fusion.1), channel_id=1, source_target_pairs={{0,256},{128,384},{256,0},{384,128},{1,257},{129,385},{257,1},{385... | collective-permute-start | bytes 1179656 | tf_op jit(solution)/shard_map/ppermute | solution.py:21
  91.2 9.0 %collective-permute-done.9 = bf16[4,1,2,16,1536]{4,3,2,1,0:T(8,128)(2,1)S(1)} collective-permute-done((bf16[4,1,2,16,1536]{4,3,2,1,0:T(8,128)(2,1)S(1)}, bf16[4,1,2,16,1536]{4,3,2,1,0:T(8,128)(2,1)S(1)}, u32[]{:S(2)}, u32[]{:S(2)}) %collective-permute-start.9) | collective-permute-done | bytes 393248 | tf_op jit(solution)/shard_map/ppermute | solution.py:21
  100.2 7.0 %all-to-all-done.1 = bf16[8,128,256]{2,1,0:T(8,128)(2,1)S(1)} async-done(((bf16[8,128,256]{2,1,0:T(8,128)(2,1)}), bf16[8,128,256]{2,1,0:T(8,128)(2,1)S(1)}, u32[]{:S(2)}, u32[]{:S(2)}) %all-to-all-start.1) | async-done | bytes 524320 | tf_op jit(solution)/shard_map/all_to_all | solution.py:29
  108.3 3.6 %all-to-all-start.2 = ((bf16[16,8,1536]{2,1,0:T(8,128)(2,1)}), bf16[16,8,1536]{2,1,0:T(8,128)(2,1)S(1)}, u32[]{:S(2)}, u32[]{:S(2)}) async-start(bf16[16,8,1536]{2,1,0:T(8,128)(2,1)} %fusion.1), calls=%async_computation.2 | async-start | bytes 786432 | tf_op jit(solution)/shard_map/all_to_all | solution.py:29
  114.7 6.5 %all-to-all-done.2 = bf16[16,8,1536]{2,1,0:T(8,128)(2,1)S(1)} async-done(((bf16[16,8,1536]{2,1,0:T(8,128)(2,1)}), bf16[16,8,1536]{2,1,0:T(8,128)(2,1)S(1)}, u32[]{:S(2)}, u32[]{:S(2)}) %all-to-all-start.2) | async-done | bytes 393248 | tf_op jit(solution)/shard_map/all_to_all | solution.py:29
  121.2 10.2 %collective-permute-start.10 = (bf16[8,1536]{1,0:T(8,128)(2,1)S(1)}, bf16[8,1536]{1,0:T(8,128)(2,1)S(1)}, u32[]{:S(2)}, u32[]{:S(2)}) collective-permute-start(bf16[8,1536]{1,0:T(8,128)(2,1)S(1)} %convert_element_type.44), channel_id=1, source_target_pairs={{0,1},{1,0},{2,3},{3,2},{4,5},{5,4},{6,7},{7,6},{8,9},{9,8},{10,11... | collective-permute-start | bytes 73736 | tf_op jit(solution)/shard_map/ppermute | solution.py:21
  131.5 4.0 %collective-permute-start.12 = (bf16[2,128,256]{2,1,0:T(8,128)(2,1)S(1)}, bf16[2,128,256]{2,1,0:T(8,128)(2,1)S(1)}, u32[]{:S(2)}, u32[]{:S(2)}) collective-permute-start(bf16[2,128,256]{2,1,0:T(8,128)(2,1)S(1)} %pad_maximum_fusion.1), channel_id=1, source_target_pairs={{0,256},{128,384},{256,0},{384,128},{1,257},{129,385},{257,1},{385... | collective-permute-start | bytes 393224 | tf_op jit(solution)/shard_map/ppermute | solution.py:21
  135.7 5.3 %all-gather = bf16[32,1536]{1,0:T(8,128)(2,1)S(1)} all-gather(bf16[8,1536]{1,0:T(8,128)(2,1)S(1)} %get-tuple-element.28), channel_id=2, replica_groups=mesh['dp'=4,'zq'=4,'zp'=2,'co'=2,'y'=4,'zh'=2] {'zp','co'}, dimensions={0}, use_global_device_ids=true | all-gather | bytes 122880 | tf_op jit(solution)/shard_map/all_gather | solution.py:161
  141.8 5.3 %all-to-all-start.3 = ((bf16[16,4,8,384]{3,2,1,0:T(8,128)(2,1)}), bf16[16,4,8,384]{3,2,1,0:T(8,128)(2,1)S(1)}, u32[]{:S(2)}, u32[]{:S(2)}) async-start(bf16[16,4,8,384]{3,2,1,0:T(8,128)(2,1)} %bitcast.23), calls=%async_computation.3 | async-start | bytes 786432 | tf_op jit(solution)/shard_map/all_to_all | solution.py:29
  147.8 7.7 %all-to-all-done.3 = bf16[16,4,8,384]{3,2,1,0:T(8,128)(2,1)S(1)} async-done(((bf16[16,4,8,384]{3,2,1,0:T(8,128)(2,1)}), bf16[16,4,8,384]{3,2,1,0:T(8,128)(2,1)S(1)}, u32[]{:S(2)}, u32[]{:S(2)}) %all-to-all-start.3) | async-done | bytes 393248 | tf_op jit(solution)/shard_map/all_to_all | solution.py:29
  156.6 3.9 %all-to-all-start.4 = ((bf16[4,64,384]{2,1,0:T(8,128)(2,1)}), bf16[4,64,384]{2,1,0:T(8,128)(2,1)S(1)}, u32[]{:S(2)}, u32[]{:S(2)}) async-start(bf16[4,64,384]{2,1,0:T(8,128)(2,1)} %bitcast.27), calls=%async_computation.4 | async-start | bytes 393216 | tf_op jit(solution)/shard_map/all_to_all | solution.py:29
  160.5 13.7 %all-to-all-done.4 = bf16[4,64,384]{2,1,0:T(8,128)(2,1)S(1)} async-done(((bf16[4,64,384]{2,1,0:T(8,128)(2,1)}), bf16[4,64,384]{2,1,0:T(8,128)(2,1)S(1)}, u32[]{:S(2)}, u32[]{:S(2)}) %all-to-all-start.4) | async-done | bytes 196640 | tf_op jit(solution)/shard_map/all_to_all | solution.py:29
  175.0 5.4 %all-to-all-start.5 = ((bf16[4,64,384]{2,1,0:T(8,128)(2,1)}), bf16[4,64,384]{2,1,0:T(8,128)(2,1)S(1)}, u32[]{:S(2)}, u32[]{:S(2)}) async-start(bf16[4,64,384]{2,1,0:T(8,128)(2,1)} %broadcast_in_dim.51), calls=%async_computation.5 | async-start | bytes 393216 | tf_op jit(solution)/shard_map/all_to_all | solution.py:29
  181.0 4.3 %all-to-all-done.5 = bf16[4,64,384]{2,1,0:T(8,128)(2,1)S(1)} async-done(((bf16[4,64,384]{2,1,0:T(8,128)(2,1)}), bf16[4,64,384]{2,1,0:T(8,128)(2,1)S(1)}, u32[]{:S(2)}, u32[]{:S(2)}) %all-to-all-start.5) | async-done | bytes 196640 | tf_op jit(solution)/shard_map/all_to_all | solution.py:29
  (69 shorter events, 36.4 us)
Async XLA Ops:
  1.6 30.5 %collective-permute-start.1 = (bf16[1,1,16,1536]{3,2,1,0:T(8,128)(2,1)S(1)}, bf16[1,1,16,1536]{3,2,1,0:T(8,128)(2,1)S(1)}, u32[]{:S(2)}, u32[]{:S(2)}) collective-permute-start(bf16[1,1,16,1536]{3,2,1,0:T(8,128)(2,1)S(1)} %dynamic-slice_bitcast_fusion), channel_id=1, source_target_pairs={{0,64},{32,96},{64,0},{96,32},{1,65},{33,97},{65,1},{97,33},{2,66}... | collective-permute-start | bytes 147464 | tf_op jit(solution)/shard_map/ppermute | solution.py:21
  10.7 21.4 %collective-permute-start = (bf16[64,1792]{1,0:T(8,128)(2,1)}, bf16[64,1792]{1,0:T(8,128)(2,1)S(1)}, u32[]{:S(2)}, u32[]{:S(2)}) collective-permute-start(bf16[64,1792]{1,0:T(8,128)(2,1)} %refs_0_), channel_id=1, source_target_pairs={{0,1},{1,0},{2,3},{3,2},{4,5},{5,4},{6,7},{7,6},{8,9},{9,8},{10,11... | collective-permute-start | bytes 688136 | tf_op jit(solution)/shard_map/ppermute | solution.py:21
  21.6 10.5 %collective-permute-start.2 = (bf16[64,1792]{1,0:T(8,128)(2,1)}, bf16[64,1792]{1,0:T(8,128)(2,1)S(1)}, u32[]{:S(2)}, u32[]{:S(2)}) collective-permute-start(bf16[64,1792]{1,0:T(8,128)(2,1)} %refs_0_), channel_id=1, source_target_pairs={{0,2},{2,0},{4,6},{6,4},{1,3},{3,1},{5,7},{7,5},{8,10},{10,8},{12,... | collective-permute-start | bytes 688136 | tf_op jit(solution)/shard_map/ppermute | solution.py:21
  25.1 12.9 %collective-permute-start.3 = (bf16[64,1792]{1,0:T(8,128)(2,1)}, bf16[64,1792]{1,0:T(8,128)(2,1)S(1)}, u32[]{:S(2)}, u32[]{:S(2)}) collective-permute-start(bf16[64,1792]{1,0:T(8,128)(2,1)} %refs_0_), channel_id=1, source_target_pairs={{0,4},{2,6},{4,0},{6,2},{1,5},{3,7},{5,1},{7,3},{8,12},{10,14},{12... | collective-permute-start | bytes 688136 | tf_op jit(solution)/shard_map/ppermute | solution.py:21
  29.9 12.8 %collective-permute-start.4 = (bf16[64,1792]{1,0:T(8,128)(2,1)}, bf16[64,1792]{1,0:T(8,128)(2,1)S(1)}, u32[]{:S(2)}, u32[]{:S(2)}) collective-permute-start(bf16[64,1792]{1,0:T(8,128)(2,1)} %refs_0_), channel_id=1, source_target_pairs={{0,6},{2,4},{4,2},{6,0},{1,7},{3,5},{5,3},{7,1},{8,14},{10,12},{12... | collective-permute-start | bytes 688136 | tf_op jit(solution)/shard_map/ppermute | solution.py:21
  43.7 17.5 %all-to-all-start = ((bf16[4,64,1792]{2,1,0:T(8,128)(2,1)}), bf16[4,64,1792]{2,1,0:T(8,128)(2,1)S(1)}, u32[]{:S(2)}, u32[]{:S(2)}) async-start(bf16[4,64,1792]{2,1,0:T(8,128)(2,1)} %broadcast_in_dim.28), calls=%async_computation | async-start | bytes 1835008 | tf_op jit(solution)/shard_map/all_to_all | solution.py:29
  48.0 11.3 %collective-permute-start.6 = (bf16[2,1,16,1536]{3,2,1,0:T(8,128)(2,1)S(1)}, bf16[2,1,16,1536]{3,2,1,0:T(8,128)(2,1)S(1)}, u32[]{:S(2)}, u32[]{:S(2)}) collective-permute-start(bf16[2,1,16,1536]{3,2,1,0:T(8,128)(2,1)S(1)} %maximum_select_fusion.3), channel_id=1, source_target_pairs={{0,32},{32,0},{64,96},{96,64},{1,33},{33,1},{65,97},{97,65},{2,34}... | collective-permute-start | bytes 294920 | tf_op jit(solution)/shard_map/ppermute | solution.py:21
  51.4 2.0 %copy-start.1 = (bf16[1792,1024]{1,0:T(8,128)(2,1)S(1)}, bf16[1792,1024]{1,0:T(8,128)(2,1)}, u32[]{:S(2)}) copy-start(bf16[1792,1024]{1,0:T(8,128)(2,1)} %weight_ref.3) | copy-start | bytes 11010052
  54.3 13.9 %copy-start.4 = (bf16[512,64]{0,1:T(8,128)(2,1)S(1)}, bf16[512,64]{0,1:T(8,128)(2,1)}, u32[]{:S(2)}) copy-start(bf16[512,64]{0,1:T(8,128)(2,1)} %param.10) | copy-start | bytes 196612
  57.3 11.3 %collective-permute-start.5 = (bf16[256,512]{1,0:T(8,128)(2,1)S(1)}, bf16[256,512]{1,0:T(8,128)(2,1)S(1)}, u32[]{:S(2)}, u32[]{:S(2)}) collective-permute-start(bf16[256,512]{1,0:T(8,128)(2,1)S(1)} %get-tuple-element.20), channel_id=1, source_target_pairs={{0,8},{8,0},{1,9},{9,1},{2,10},{10,2},{3,11},{11,3},{4,12},{12,4},... | collective-permute-start | bytes 786440 | tf_op jit(solution)/shard_map/ppermute | solution.py:21
  61.2 2.0 %copy-start.2 = (bf16[1792,1024]{1,0:T(8,128)(2,1)S(1)}, bf16[1792,1024]{1,0:T(8,128)(2,1)}, u32[]{:S(2)}) copy-start(bf16[1792,1024]{1,0:T(8,128)(2,1)} %weight_ref.3) | copy-start | bytes 11010052
  63.3 27.5 %copy-start.5 = (bf16[4,1536]{1,0:T(4,128)(2,1)S(1)}, bf16[4,1536]{1,0:T(4,128)(2,1)}, u32[]{:S(2)}) copy-start(bf16[4,1536]{1,0:T(4,128)(2,1)} %param.12) | copy-start | bytes 36868
  66.2 3.4 %collective-permute-start.7 = (bf16[256,512]{1,0:T(8,128)(2,1)S(1)}, bf16[256,512]{1,0:T(8,128)(2,1)S(1)}, u32[]{:S(2)}, u32[]{:S(2)}) collective-permute-start(bf16[256,512]{1,0:T(8,128)(2,1)S(1)} %get-tuple-element.25), channel_id=1, source_target_pairs={{0,8},{8,0},{1,9},{9,1},{2,10},{10,2},{3,11},{11,3},{4,12},{12,4},... | collective-permute-start | bytes 786440 | tf_op jit(solution)/shard_map/ppermute | solution.py:21
  71.2 35.9 %all-to-all-start.1 = ((bf16[8,128,256]{2,1,0:T(8,128)(2,1)}), bf16[8,128,256]{2,1,0:T(8,128)(2,1)S(1)}, u32[]{:S(2)}, u32[]{:S(2)}) async-start(bf16[8,128,256]{2,1,0:T(8,128)(2,1)} %bitcast.14), calls=%async_computation.1 | async-start | bytes 1048576 | tf_op jit(solution)/shard_map/all_to_all | solution.py:29
  78.1 8.5 %collective-permute-start.8 = (bf16[4,1,1,16,1536]{4,3,2,1,0:T(8,128)(2,1)S(1)}, bf16[4,1,1,16,1536]{4,3,2,1,0:T(8,128)(2,1)S(1)}, u32[]{:S(2)}, u32[]{:S(2)}) collective-permute-start(bf16[4,1,1,16,1536]{4,3,2,1,0:T(8,128)(2,1)S(1)} %bitcast.58), channel_id=1, source_target_pairs={{0,128},{128,0},{256,384},{384,256},{1,129},{129,1},{257,385},{385... | collective-permute-start | bytes 589832 | tf_op jit(solution)/shard_map/ppermute | solution.py:21
  86.7 13.4 %collective-permute-start.9 = (bf16[4,1,2,16,1536]{4,3,2,1,0:T(8,128)(2,1)S(1)}, bf16[4,1,2,16,1536]{4,3,2,1,0:T(8,128)(2,1)S(1)}, u32[]{:S(2)}, u32[]{:S(2)}) collective-permute-start(bf16[4,1,2,16,1536]{4,3,2,1,0:T(8,128)(2,1)S(1)} %maximum_select_fusion.1), channel_id=1, source_target_pairs={{0,256},{128,384},{256,0},{384,128},{1,257},{129,385},{257,1},{385... | collective-permute-start | bytes 1179656 | tf_op jit(solution)/shard_map/ppermute | solution.py:21
  90.8 21.1 %copy-start.6 = (s32[1,512]{1,0:T(1,128)S(1)}, s32[1,512]{1,0:T(1,128)}, u32[]{:S(2)}) copy-start(s32[1,512]{1,0:T(1,128)} %param.13) | copy-start | bytes 6148
  108.3 12.8 %all-to-all-start.2 = ((bf16[16,8,1536]{2,1,0:T(8,128)(2,1)}), bf16[16,8,1536]{2,1,0:T(8,128)(2,1)S(1)}, u32[]{:S(2)}, u32[]{:S(2)}) async-start(bf16[16,8,1536]{2,1,0:T(8,128)(2,1)} %fusion.1), calls=%async_computation.2 | async-start | bytes 786432 | tf_op jit(solution)/shard_map/all_to_all | solution.py:29
  112.2 19.2 %collective-permute-start.11 = (bf16[128,256]{1,0:T(8,128)(2,1)S(1)}, bf16[128,256]{1,0:T(8,128)(2,1)S(1)}, u32[]{:S(2)}, u32[]{:S(2)}) collective-permute-start(bf16[128,256]{1,0:T(8,128)(2,1)S(1)} %reduce_sum.43), channel_id=1, source_target_pairs={{0,128},{128,0},{256,384},{384,256},{1,129},{129,1},{257,385},{385... | collective-permute-start | bytes 196616 | tf_op jit(solution)/shard_map/ppermute | solution.py:21
  121.2 14.4 %collective-permute-start.10 = (bf16[8,1536]{1,0:T(8,128)(2,1)S(1)}, bf16[8,1536]{1,0:T(8,128)(2,1)S(1)}, u32[]{:S(2)}, u32[]{:S(2)}) collective-permute-start(bf16[8,1536]{1,0:T(8,128)(2,1)S(1)} %convert_element_type.44), channel_id=1, source_target_pairs={{0,1},{1,0},{2,3},{3,2},{4,5},{5,4},{6,7},{7,6},{8,9},{9,8},{10,11... | collective-permute-start | bytes 73736 | tf_op jit(solution)/shard_map/ppermute | solution.py:21
  131.5 15.7 %collective-permute-start.12 = (bf16[2,128,256]{2,1,0:T(8,128)(2,1)S(1)}, bf16[2,128,256]{2,1,0:T(8,128)(2,1)S(1)}, u32[]{:S(2)}, u32[]{:S(2)}) collective-permute-start(bf16[2,128,256]{2,1,0:T(8,128)(2,1)S(1)} %pad_maximum_fusion.1), channel_id=1, source_target_pairs={{0,256},{128,384},{256,0},{384,128},{1,257},{129,385},{257,1},{385... | collective-permute-start | bytes 393224 | tf_op jit(solution)/shard_map/ppermute | solution.py:21
  141.8 13.7 %all-to-all-start.3 = ((bf16[16,4,8,384]{3,2,1,0:T(8,128)(2,1)}), bf16[16,4,8,384]{3,2,1,0:T(8,128)(2,1)S(1)}, u32[]{:S(2)}, u32[]{:S(2)}) async-start(bf16[16,4,8,384]{3,2,1,0:T(8,128)(2,1)} %bitcast.23), calls=%async_computation.3 | async-start | bytes 786432 | tf_op jit(solution)/shard_map/all_to_all | solution.py:29
  156.6 17.6 %all-to-all-start.4 = ((bf16[4,64,384]{2,1,0:T(8,128)(2,1)}), bf16[4,64,384]{2,1,0:T(8,128)(2,1)S(1)}, u32[]{:S(2)}, u32[]{:S(2)}) async-start(bf16[4,64,384]{2,1,0:T(8,128)(2,1)} %bitcast.27), calls=%async_computation.4 | async-start | bytes 393216 | tf_op jit(solution)/shard_map/all_to_all | solution.py:29
  175.0 10.2 %all-to-all-start.5 = ((bf16[4,64,384]{2,1,0:T(8,128)(2,1)}), bf16[4,64,384]{2,1,0:T(8,128)(2,1)S(1)}, u32[]{:S(2)}, u32[]{:S(2)}) async-start(bf16[4,64,384]{2,1,0:T(8,128)(2,1)} %broadcast_in_dim.51), calls=%async_computation.5 | async-start | bytes 393216 | tf_op jit(solution)/shard_map/all_to_all | solution.py:29
  (2 other events, 1.9 us)

commit v4 on v3

--- a/solution.py
+++ b/solution.py
@@ -15,6 +15,7 @@
 MIB = 1024 * 1024
 VMEM = pl.BlockSpec(memory_space=pltpu.VMEM)
 SMEM = pl.BlockSpec(memory_space=pltpu.SMEM)
+COST = pl.CostEstimate(flops=10**4, bytes_accessed=10**4, transcendentals=0)
 
 
 def swap(x, axis, mask):
@@ -33,64 +34,65 @@
     return exchange(jnp.broadcast_to(x[None], (lax.axis_size(axis),) + x.shape), axis)
 
 
+def placed(x, got, bit, at):
+    return jnp.where(bit == 0, jnp.concatenate([x, got], at), jnp.concatenate([got, x], at))
+
+
 def join(x, axis, mask, bit, at):
-    got = swap(x, axis, mask)
-    return jnp.where(bit == 0, jnp.concatenate([x, got], at), jnp.concatenate([got, x], at))
+    return placed(x, swap(x, axis, mask), bit, at)
 
 
 def after(x, *others):
     return lax.optimization_barrier((x,) + others)[0]
 
 
-def band_kernel(core_ref, scales_ref, weight_ref, *refs):
-    *token_refs, send_ref, keep_ref, total_ref = refs
-    step = pl.program_id(0)
-    depth, cols = weight_ref.shape
+def scale_kernel(scales_ref, weight_ref, out_ref):
+    rows, cols = weight_ref.shape
+    for j in range(cols // BLOCK):
+        for i in range(rows // BLOCK):
+            at = (pl.ds(i * BLOCK, BLOCK), pl.ds(j * BLOCK, BLOCK))
+            out_ref[at] = (weight_ref[at].astype(F32) * scales_ref[j, i]).astype(BF)
+
+
+def scale(weight, scales):
+    return pl.pallas_call(
+        scale_kernel,
+        out_shape=jax.ShapeDtypeStruct(weight.shape, BF),
+        in_specs=[SMEM, VMEM],
+        out_specs=VMEM,
+        compiler_params=pltpu.CompilerParams(vmem_limit_bytes=24 * MIB),
+        cost_estimate=COST,
+    )(scales, weight)
+
+
+def band_kernel(core_ref, weight_ref, *refs):
+    *token_refs, send_ref, keep_ref = refs
     tokens = jnp.concatenate([r[...] for r in token_refs], 0)
     first = lax.broadcasted_iota(jnp.int32, (1, BLOCK), 1) < 64
     is_one = core_ref[0] == 1
     for m in range(2):
-        tiles = []
-        for j in range(4 * m, 4 * m + 4):
-            column = []
-            for i in range(depth // BLOCK):
-                block = weight_ref[i * BLOCK : i * BLOCK + BLOCK, j * BLOCK : j * BLOCK + BLOCK].astype(F32)
-                column.append((block * scales_ref[step * (depth // BLOCK) + i, j]).astype(BF))
-            tiles.append(jnp.concatenate(column, 0))
-        part = jnp.dot(tokens, jnp.concatenate(tiles, 1), preferred_element_type=F32)
-
-        @pl.when(step == 0)
-        def _():
-            total_ref[:, 512 * m : 512 * m + 512] = part
-
-        @pl.when(step == 1)
-        def _():
-            whole = total_ref[:, 512 * m : 512 * m + 512] + part
-            for zp in range(2):
-                a = whole[:, BLOCK * zp : BLOCK * zp + BLOCK]
-                b = whole[:, BLOCK * zp + 256 : BLOCK * zp + 256 + BLOCK]
-                zero = jnp.where(first, a, pltpu.roll(b, 64, 1)).astype(BF)
-                one = jnp.where(first, pltpu.roll(a, 64, 1), b).astype(BF)
-                at = (slice(None), pl.ds(256 * zp + BLOCK * m, BLOCK))
-                send_ref[at] = jnp.where(is_one, zero, one)
-                keep_ref[at] = jnp.where(is_one, one, zero)
+        part = jnp.dot(tokens, weight_ref[:, 512 * m : 512 * m + 512], preferred_element_type=F32)
+        for zp in range(2):
+            a = part[:, BLOCK * zp : BLOCK * zp + BLOCK]
+            b = part[:, BLOCK * zp + 256 : BLOCK * zp + 256 + BLOCK]
+            zero = jnp.where(first, a, pltpu.roll(b, 64, 1)).astype(BF)
+            one = jnp.where(first, pltpu.roll(a, 64, 1), b).astype(BF)
+            at = (slice(None), pl.ds(256 * zp + BLOCK * m, BLOCK))
+            send_ref[at] = jnp.where(is_one, zero, one)
+            keep_ref[at] = jnp.where(is_one, one, zero)
 
 
-def band(core, scales, weight, tokens):
-    count, (depth, cols) = sum(v.shape[0] for v in tokens), weight.shape
-    half = jax.ShapeDtypeStruct((count, cols // 2), BF)
-    whole = pl.BlockSpec(half.shape, lambda k: (0, 0))
+def band(core, weight, tokens):
+    rows = sum(v.shape[0] for v in tokens)
+    half = jax.ShapeDtypeStruct((rows, weight.shape[1] // 2), BF)
     return pl.pallas_call(
         band_kernel,
-        grid=(2,),
         out_shape=(half, half),
-        in_specs=[SMEM, SMEM, pl.BlockSpec((depth // 2, cols), lambda k: (k, 0))]
-        + [pl.BlockSpec((v.shape[0], depth // 2), lambda k: (0, k)) for v in tokens],
-        out_specs=(whole, whole),
-        scratch_shapes=[pltpu.VMEM((count, cols), F32)],
-        compiler_params=pltpu.CompilerParams(vmem_limit_bytes=32 * MIB),
-        cost_estimate=pl.CostEstimate(flops=10**4, bytes_accessed=10**4, transcendentals=0),
-    )(core.reshape(1), scales, weight, *tokens)
+        in_specs=[SMEM] + [VMEM] * (1 + len(tokens)),
+        out_specs=(VMEM, VMEM),
+        compiler_params=pltpu.CompilerParams(vmem_limit_bytes=24 * MIB),
+        cost_estimate=COST,
+    )(core.reshape(1), weight, *tokens)
 
 
 def combine_kernel(at_ref, near_ref, near_got_ref, far_ref, far_got_ref, res_ref, out_ref):
@@ -110,7 +112,7 @@
         in_specs=[SMEM] + [VMEM] * 5,
         out_specs=VMEM,
         compiler_params=pltpu.CompilerParams(vmem_limit_bytes=16 * MIB),
-        cost_estimate=pl.CostEstimate(flops=10**4, bytes_accessed=10**4, transcendentals=0),
+        cost_estimate=COST,
     )(at, near, near_got, far, far_got, res)
 
 
@@ -122,14 +124,18 @@
 
     far = swap(hidden_in, "zh", 1)
     near = [hidden_in] + [swap(hidden_in, "y", k) for k in (1, 2, 3)]
-    pg = join(pick(projector.reshape(4, 16, -1), x, 0)[None, None], "zq", 2, zq >> 1, 0)
-    far, pg, *near = lax.optimization_barrier((far, pg, *near))
+    effective = scale(down_weight, block_scales.T)
+
+    pg = pick(projector.reshape(4, 16, -1), x, 0)[None, None]
+    got = swap(pg, "zq", 2)
+    far, got, effective, *near = lax.optimization_barrier((far, got, effective, *near))
+    pg = placed(pg, got, zq >> 1, 0)
     pg = join(pg.reshape(2, 1, 16, -1), "zq", 1, zq & 1, 1).reshape(4, 1, 1, 16, -1)
 
-    send, near = band(core, block_scales, down_weight, near)
+    send, near = band(core, effective, near)
     near_got = swap(send, "co", 1)
     far, pg = lax.optimization_barrier((gather(far, "y").reshape(256, rows), pg))
-    send, far = band(core, block_scales, down_weight, [far])
+    send, far = band(core, effective, [far])
     far_got = swap(send, "co", 1)
 
     pg = join(pg, "dp", 1, x & 1, 2)

time: 187 us -> 186 us (level)
  starting transfers between devices: 89.4 us -> 84.6 us
  waiting for transfers between devices: 67.9 us -> 71.6 us
  local copies, waits for them, and re-layouts: 10.2 us -> 12.1 us
    ppermute x13, starting transfers between devices: 60.8 us -> 54.8 us  [swap(): lax.ppermute(x, axis, [(i, i ^ mask) for i in range(lax.axis_size(axis))])]
    all_to_all x6, waiting for transfers between devices: 41 us -> 44.8 us  [exchange(): return lax.all_to_all(x, axes, 0, 0, tiled=True)]
    unnamed x15 -> x20, local copies, waits for them, and re-layouts: 6.71 us -> 8.6 us
    pallas_call x2 -> x3, Pallas kernels: 5.88 us -> 4.06 us  [the longest x2 2.4 us: band(): pl.pallas_call(band_kernel, out_shape=(half, half), in_specs=[SMEM] + [VM...]
  transfers between devices with their start and end apart: 19 -> 19, of which waited for: 12 -> 12; matrix products, arithmetic and copies ran while one was open for 2% -> 2% of each run, Pallas kernels for 3% -> 2%
where the time goes in v4:
time: 186 us; the launch traced here: 185 us
  starting transfers between devices  84.6 us (45%)
  waiting for transfers between devices  71.6 us (38%)
  local copies, waits for them, and re-layouts  12.1 us (7%)
  Pallas kernels  5.66 us (3%)
  blocking collectives  5.32 us (3%)
  matrix products  2.4 us (1%)
  other arithmetic  2.29 us (1%)
    ppermute x13, starting transfers between devices, swap(): lax.ppermute(x, axis, [(i, i ^ mask) for i in range(lax.axis_size(axis))])  54.8 us
    all_to_all x6, waiting for transfers between devices, exchange(): return lax.all_to_all(x, axes, 0, 0, tiled=True)  44.8 us
    all_to_all x6, starting transfers between devices, exchange(): return lax.all_to_all(x, axes, 0, 0, tiled=True)  29.8 us
    ppermute x13, waiting for transfers between devices, swap(): lax.ppermute(x, axis, [(i, i ^ mask) for i in range(lax.axis_size(axis))])  26.8 us
    unnamed x20, local copies, waits for them, and re-layouts  8.6 us
    all_gather x1, blocking collectives, shards(): scaled = lax.all_gather(scaled_f.astype(BF), ('zp', 'co'))  5.32 us
  transfers between devices with their start and end apart: 19, of which 12 were waited for; matrix products, arithmetic and copies ran while one was open for 2% of the time, Pallas kernels for 2%

profile of v4, /device:TPU:2, one launch (start us, length us, event | category | flops | bytes accessed | tf_op | source)
XLA Modules:
  0.0 185.0 jit_solution(11931618413591471083)
XLA Ops:
  0.6 15.9 %collective-permute-start = (bf16[64,1792]{1,0:T(8,128)(2,1)}, bf16[64,1792]{1,0:T(8,128)(2,1)S(1)}, u32[]{:S(2)}, u32[]{:S(2)}) collective-permute-start(bf16[64,1792]{1,0:T(8,128)(2,1)} %refs_0_), channel_id=1, source_target_pairs={{0,1},{1,0},{2,3},{3,2},{4,5},{5,4},{6,7},{7,6},{8,9},{9,8},{10,11... | collective-permute-start | bytes 688136 | tf_op jit(solution)/shard_map/ppermute | solution.py:22
  16.5 3.5 %collective-permute-start.2 = (bf16[64,1792]{1,0:T(8,128)(2,1)}, bf16[64,1792]{1,0:T(8,128)(2,1)S(1)}, u32[]{:S(2)}, u32[]{:S(2)}) collective-permute-start(bf16[64,1792]{1,0:T(8,128)(2,1)} %refs_0_), channel_id=1, source_target_pairs={{0,2},{2,0},{4,6},{6,4},{1,3},{3,1},{5,7},{7,5},{8,10},{10,8},{12,... | collective-permute-start | bytes 688136 | tf_op jit(solution)/shard_map/ppermute | solution.py:22
  20.0 4.8 %collective-permute-start.3 = (bf16[64,1792]{1,0:T(8,128)(2,1)}, bf16[64,1792]{1,0:T(8,128)(2,1)S(1)}, u32[]{:S(2)}, u32[]{:S(2)}) collective-permute-start(bf16[64,1792]{1,0:T(8,128)(2,1)} %refs_0_), channel_id=1, source_target_pairs={{0,4},{2,6},{4,0},{6,2},{1,5},{3,7},{5,1},{7,3},{8,12},{10,14},{12... | collective-permute-start | bytes 688136 | tf_op jit(solution)/shard_map/ppermute | solution.py:22
  27.0 4.3 %collective-permute-start.1 = (bf16[1,1,16,1536]{3,2,1,0:T(8,128)(2,1)S(1)}, bf16[1,1,16,1536]{3,2,1,0:T(8,128)(2,1)S(1)}, u32[]{:S(2)}, u32[]{:S(2)}) collective-permute-start(bf16[1,1,16,1536]{3,2,1,0:T(8,128)(2,1)S(1)} %dynamic-slice_bitcast_fusion), channel_id=1, source_target_pairs={{0,64},{32,96},{64,0},{96,32},{1,65},{33,97},{65,1},{97,33},{2,66}... | collective-permute-start | bytes 147464 | tf_op jit(solution)/shard_map/ppermute | solution.py:22
  37.5 4.3 %collective-permute-done.1 = bf16[1,1,16,1536]{3,2,1,0:T(8,128)(2,1)S(1)} collective-permute-done((bf16[1,1,16,1536]{3,2,1,0:T(8,128)(2,1)S(1)}, bf16[1,1,16,1536]{3,2,1,0:T(8,128)(2,1)S(1)}, u32[]{:S(2)}, u32[]{:S(2)}) %collective-permute-start.1) | collective-permute-done | bytes 49184 | tf_op jit(solution)/shard_map/ppermute | solution.py:22
  42.8 4.5 %all-to-all-start = ((bf16[4,64,1792]{2,1,0:T(8,128)(2,1)}), bf16[4,64,1792]{2,1,0:T(8,128)(2,1)S(1)}, u32[]{:S(2)}, u32[]{:S(2)}) async-start(bf16[4,64,1792]{2,1,0:T(8,128)(2,1)} %broadcast_in_dim.48), calls=%async_computation | async-start | bytes 1835008 | tf_op jit(solution)/shard_map/all_to_all | solution.py:30
  55.6 5.5 %all-to-all-done = bf16[4,64,1792]{2,1,0:T(8,128)(2,1)S(1)} async-done(((bf16[4,64,1792]{2,1,0:T(8,128)(2,1)}), bf16[4,64,1792]{2,1,0:T(8,128)(2,1)S(1)}, u32[]{:S(2)}, u32[]{:S(2)}) %all-to-all-start) | async-done | bytes 917536 | tf_op jit(solution)/shard_map/all_to_all | solution.py:30
  69.4 7.6 %all-to-all-start.1 = ((bf16[8,128,256]{2,1,0:T(8,128)(2,1)}), bf16[8,128,256]{2,1,0:T(8,128)(2,1)S(1)}, u32[]{:S(2)}, u32[]{:S(2)}) async-start(bf16[8,128,256]{2,1,0:T(8,128)(2,1)} %bitcast.15), calls=%async_computation.1 | async-start | bytes 1048576 | tf_op jit(solution)/shard_map/all_to_all | solution.py:30
  79.4 6.1 %collective-permute-done.8 = bf16[4,1,1,16,1536]{4,3,2,1,0:T(8,128)(2,1)S(1)} collective-permute-done((bf16[4,1,1,16,1536]{4,3,2,1,0:T(8,128)(2,1)S(1)}, bf16[4,1,1,16,1536]{4,3,2,1,0:T(8,128)(2,1)S(1)}, u32[]{:S(2)}, u32[]{:S(2)}) %collective-permute-start.8) | collective-permute-done | bytes 196640 | tf_op jit(solution)/shard_map/ppermute | solution.py:22
  85.5 4.0 %collective-permute-start.9 = (bf16[4,1,2,16,1536]{4,3,2,1,0:T(8,128)(2,1)S(1)}, bf16[4,1,2,16,1536]{4,3,2,1,0:T(8,128)(2,1)S(1)}, u32[]{:S(2)}, u32[]{:S(2)}) collective-permute-start(bf16[4,1,2,16,1536]{4,3,2,1,0:T(8,128)(2,1)S(1)} %maximum_select_fusion.1), channel_id=1, source_target_pairs={{0,256},{128,384},{256,0},{384,128},{1,257},{129,385},{257,1},{385... | collective-permute-start | bytes 1179656 | tf_op jit(solution)/shard_map/ppermute | solution.py:22
  90.0 9.0 %collective-permute-done.9 = bf16[4,1,2,16,1536]{4,3,2,1,0:T(8,128)(2,1)S(1)} collective-permute-done((bf16[4,1,2,16,1536]{4,3,2,1,0:T(8,128)(2,1)S(1)}, bf16[4,1,2,16,1536]{4,3,2,1,0:T(8,128)(2,1)S(1)}, u32[]{:S(2)}, u32[]{:S(2)}) %collective-permute-start.9) | collective-permute-done | bytes 393248 | tf_op jit(solution)/shard_map/ppermute | solution.py:22
  99.0 7.0 %all-to-all-done.1 = bf16[8,128,256]{2,1,0:T(8,128)(2,1)S(1)} async-done(((bf16[8,128,256]{2,1,0:T(8,128)(2,1)}), bf16[8,128,256]{2,1,0:T(8,128)(2,1)S(1)}, u32[]{:S(2)}, u32[]{:S(2)}) %all-to-all-start.1) | async-done | bytes 524320 | tf_op jit(solution)/shard_map/all_to_all | solution.py:30
  107.1 3.6 %all-to-all-start.2 = ((bf16[16,8,1536]{2,1,0:T(8,128)(2,1)}), bf16[16,8,1536]{2,1,0:T(8,128)(2,1)S(1)}, u32[]{:S(2)}, u32[]{:S(2)}) async-start(bf16[16,8,1536]{2,1,0:T(8,128)(2,1)} %fusion.1), calls=%async_computation.2 | async-start | bytes 786432 | tf_op jit(solution)/shard_map/all_to_all | solution.py:30
  113.5 6.5 %all-to-all-done.2 = bf16[16,8,1536]{2,1,0:T(8,128)(2,1)S(1)} async-done(((bf16[16,8,1536]{2,1,0:T(8,128)(2,1)}), bf16[16,8,1536]{2,1,0:T(8,128)(2,1)S(1)}, u32[]{:S(2)}, u32[]{:S(2)}) %all-to-all-start.2) | async-done | bytes 393248 | tf_op jit(solution)/shard_map/all_to_all | solution.py:30
  120.0 5.5 %collective-permute-start.10 = (bf16[8,1536]{1,0:T(8,128)(2,1)S(1)}, bf16[8,1536]{1,0:T(8,128)(2,1)S(1)}, u32[]{:S(2)}, u32[]{:S(2)}) collective-permute-start(bf16[8,1536]{1,0:T(8,128)(2,1)S(1)} %convert_element_type.44), channel_id=1, source_target_pairs={{0,1},{1,0},{2,3},{3,2},{4,5},{5,4},{6,7},{7,6},{8,9},{9,8},{10,11... | collective-permute-start | bytes 73736 | tf_op jit(solution)/shard_map/ppermute | solution.py:22
  125.5 4.0 %collective-permute-start.12 = (bf16[2,128,256]{2,1,0:T(8,128)(2,1)S(1)}, bf16[2,128,256]{2,1,0:T(8,128)(2,1)S(1)}, u32[]{:S(2)}, u32[]{:S(2)}) collective-permute-start(bf16[2,128,256]{2,1,0:T(8,128)(2,1)S(1)} %pad_maximum_fusion.1), channel_id=1, source_target_pairs={{0,256},{128,384},{256,0},{384,128},{1,257},{129,385},{257,1},{385... | collective-permute-start | bytes 393224 | tf_op jit(solution)/shard_map/ppermute | solution.py:22
  129.6 5.2 %collective-permute-done.10 = bf16[8,1536]{1,0:T(8,128)(2,1)S(1)} collective-permute-done((bf16[8,1536]{1,0:T(8,128)(2,1)S(1)}, bf16[8,1536]{1,0:T(8,128)(2,1)S(1)}, u32[]{:S(2)}, u32[]{:S(2)}) %collective-permute-start.10) | collective-permute-done | bytes 24608 | tf_op jit(solution)/shard_map/ppermute | solution.py:22
  134.9 5.3 %all-gather = bf16[32,1536]{1,0:T(8,128)(2,1)S(1)} all-gather(bf16[8,1536]{1,0:T(8,128)(2,1)S(1)} %get-tuple-element.30), channel_id=2, replica_groups=mesh['dp'=4,'zq'=4,'zp'=2,'co'=2,'y'=4,'zh'=2] {'zp','co'}, dimensions={0}, use_global_device_ids=true | all-gather | bytes 122880 | tf_op jit(solution)/shard_map/all_gather | solution.py:167
  141.0 5.3 %all-to-all-start.3 = ((bf16[16,4,8,384]{3,2,1,0:T(8,128)(2,1)}), bf16[16,4,8,384]{3,2,1,0:T(8,128)(2,1)S(1)}, u32[]{:S(2)}, u32[]{:S(2)}) async-start(bf16[16,4,8,384]{3,2,1,0:T(8,128)(2,1)} %bitcast.24), calls=%async_computation.3 | async-start | bytes 786432 | tf_op jit(solution)/shard_map/all_to_all | solution.py:30
  147.0 7.7 %all-to-all-done.3 = bf16[16,4,8,384]{3,2,1,0:T(8,128)(2,1)S(1)} async-done(((bf16[16,4,8,384]{3,2,1,0:T(8,128)(2,1)}), bf16[16,4,8,384]{3,2,1,0:T(8,128)(2,1)S(1)}, u32[]{:S(2)}, u32[]{:S(2)}) %all-to-all-start.3) | async-done | bytes 393248 | tf_op jit(solution)/shard_map/all_to_all | solution.py:30
  155.8 3.4 %all-to-all-start.4 = ((bf16[4,64,384]{2,1,0:T(8,128)(2,1)}), bf16[4,64,384]{2,1,0:T(8,128)(2,1)S(1)}, u32[]{:S(2)}, u32[]{:S(2)}) async-start(bf16[4,64,384]{2,1,0:T(8,128)(2,1)} %bitcast.28), calls=%async_computation.4 | async-start | bytes 393216 | tf_op jit(solution)/shard_map/all_to_all | solution.py:30
  159.1 13.9 %all-to-all-done.4 = bf16[4,64,384]{2,1,0:T(8,128)(2,1)S(1)} async-done(((bf16[4,64,384]{2,1,0:T(8,128)(2,1)}), bf16[4,64,384]{2,1,0:T(8,128)(2,1)S(1)}, u32[]{:S(2)}, u32[]{:S(2)}) %all-to-all-start.4) | async-done | bytes 196640 | tf_op jit(solution)/shard_map/all_to_all | solution.py:30
  173.8 5.6 %all-to-all-start.5 = ((bf16[4,64,384]{2,1,0:T(8,128)(2,1)}), bf16[4,64,384]{2,1,0:T(8,128)(2,1)S(1)}, u32[]{:S(2)}, u32[]{:S(2)}) async-start(bf16[4,64,384]{2,1,0:T(8,128)(2,1)} %broadcast_in_dim.54), calls=%async_computation.5 | async-start | bytes 393216 | tf_op jit(solution)/shard_map/all_to_all | solution.py:30
  180.0 4.3 %all-to-all-done.5 = bf16[4,64,384]{2,1,0:T(8,128)(2,1)S(1)} async-done(((bf16[4,64,384]{2,1,0:T(8,128)(2,1)}), bf16[4,64,384]{2,1,0:T(8,128)(2,1)S(1)}, u32[]{:S(2)}, u32[]{:S(2)}) %all-to-all-start.5) | async-done | bytes 196640 | tf_op jit(solution)/shard_map/all_to_all | solution.py:30
  (75 shorter events, 37.5 us)
Async XLA Ops:
  0.6 26.3 %copy-start = (bf16[64,1536]{1,0:T(8,128)(2,1)S(1)}, bf16[64,1536]{1,0:T(8,128)(2,1)}, u32[]{:S(2)}) copy-start(bf16[64,1536]{1,0:T(8,128)(2,1)} %param.11) | copy-start | bytes 589828
  0.6 41.1 %collective-permute-start = (bf16[64,1792]{1,0:T(8,128)(2,1)}, bf16[64,1792]{1,0:T(8,128)(2,1)S(1)}, u32[]{:S(2)}, u32[]{:S(2)}) collective-permute-start(bf16[64,1792]{1,0:T(8,128)(2,1)} %refs_0_), channel_id=1, source_target_pairs={{0,1},{1,0},{2,3},{3,2},{4,5},{5,4},{6,7},{7,6},{8,9},{9,8},{10,11... | collective-permute-start | bytes 688136 | tf_op jit(solution)/shard_map/ppermute | solution.py:22
  16.5 25.3 %collective-permute-start.2 = (bf16[64,1792]{1,0:T(8,128)(2,1)}, bf16[64,1792]{1,0:T(8,128)(2,1)S(1)}, u32[]{:S(2)}, u32[]{:S(2)}) collective-permute-start(bf16[64,1792]{1,0:T(8,128)(2,1)} %refs_0_), channel_id=1, source_target_pairs={{0,2},{2,0},{4,6},{6,4},{1,3},{3,1},{5,7},{7,5},{8,10},{10,8},{12,... | collective-permute-start | bytes 688136 | tf_op jit(solution)/shard_map/ppermute | solution.py:22
  20.0 21.8 %collective-permute-start.3 = (bf16[64,1792]{1,0:T(8,128)(2,1)}, bf16[64,1792]{1,0:T(8,128)(2,1)S(1)}, u32[]{:S(2)}, u32[]{:S(2)}) collective-permute-start(bf16[64,1792]{1,0:T(8,128)(2,1)} %refs_0_), channel_id=1, source_target_pairs={{0,4},{2,6},{4,0},{6,2},{1,5},{3,7},{5,1},{7,3},{8,12},{10,14},{12... | collective-permute-start | bytes 688136 | tf_op jit(solution)/shard_map/ppermute | solution.py:22
  24.8 17.0 %collective-permute-start.4 = (bf16[64,1792]{1,0:T(8,128)(2,1)}, bf16[64,1792]{1,0:T(8,128)(2,1)S(1)}, u32[]{:S(2)}, u32[]{:S(2)}) collective-permute-start(bf16[64,1792]{1,0:T(8,128)(2,1)} %refs_0_), channel_id=1, source_target_pairs={{0,6},{2,4},{4,2},{6,0},{1,7},{3,5},{5,3},{7,1},{8,14},{10,12},{12... | collective-permute-start | bytes 688136 | tf_op jit(solution)/shard_map/ppermute | solution.py:22
  27.0 14.8 %collective-permute-start.1 = (bf16[1,1,16,1536]{3,2,1,0:T(8,128)(2,1)S(1)}, bf16[1,1,16,1536]{3,2,1,0:T(8,128)(2,1)S(1)}, u32[]{:S(2)}, u32[]{:S(2)}) collective-permute-start(bf16[1,1,16,1536]{3,2,1,0:T(8,128)(2,1)S(1)} %dynamic-slice_bitcast_fusion), channel_id=1, source_target_pairs={{0,64},{32,96},{64,0},{96,32},{1,65},{33,97},{65,1},{97,33},{2,66}... | collective-permute-start | bytes 147464 | tf_op jit(solution)/shard_map/ppermute | solution.py:22
  34.0 15.2 %copy-start.5 = (bf16[64,1792]{1,0:T(8,128)(2,1)S(1)}, bf16[64,1792]{1,0:T(8,128)(2,1)}, u32[]{:S(2)}) copy-start(bf16[64,1792]{1,0:T(8,128)(2,1)} %refs_0_) | copy-start | bytes 688132
  42.8 18.3 %all-to-all-start = ((bf16[4,64,1792]{2,1,0:T(8,128)(2,1)}), bf16[4,64,1792]{2,1,0:T(8,128)(2,1)S(1)}, u32[]{:S(2)}, u32[]{:S(2)}) async-start(bf16[4,64,1792]{2,1,0:T(8,128)(2,1)} %broadcast_in_dim.48), calls=%async_computation | async-start | bytes 1835008 | tf_op jit(solution)/shard_map/all_to_all | solution.py:30
  47.2 8.3 %collective-permute-start.6 = (bf16[2,1,16,1536]{3,2,1,0:T(8,128)(2,1)S(1)}, bf16[2,1,16,1536]{3,2,1,0:T(8,128)(2,1)S(1)}, u32[]{:S(2)}, u32[]{:S(2)}) collective-permute-start(bf16[2,1,16,1536]{3,2,1,0:T(8,128)(2,1)S(1)} %maximum_select_fusion.3), channel_id=1, source_target_pairs={{0,32},{32,0},{64,96},{96,64},{1,33},{33,1},{65,97},{97,65},{2,34}... | collective-permute-start | bytes 294920 | tf_op jit(solution)/shard_map/ppermute | solution.py:22
  51.2 15.1 %copy-start.7 = (bf16[512,64]{0,1:T(8,128)(2,1)S(1)}, bf16[512,64]{0,1:T(8,128)(2,1)}, u32[]{:S(2)}) copy-start(bf16[512,64]{0,1:T(8,128)(2,1)} %param.10) | copy-start | bytes 196612
  52.4 14.3 %collective-permute-start.5 = (bf16[256,512]{1,0:T(8,128)(2,1)S(1)}, bf16[256,512]{1,0:T(8,128)(2,1)S(1)}, u32[]{:S(2)}, u32[]{:S(2)}) collective-permute-start(bf16[256,512]{1,0:T(8,128)(2,1)S(1)} %get-tuple-element.22), channel_id=1, source_target_pairs={{0,8},{8,0},{1,9},{9,1},{2,10},{10,2},{3,11},{11,3},{4,12},{12,4},... | collective-permute-start | bytes 786440 | tf_op jit(solution)/shard_map/ppermute | solution.py:22
  63.1 26.4 %copy-start.8 = (bf16[4,1536]{1,0:T(4,128)(2,1)S(1)}, bf16[4,1536]{1,0:T(4,128)(2,1)}, u32[]{:S(2)}) copy-start(bf16[4,1536]{1,0:T(4,128)(2,1)} %param.12) | copy-start | bytes 36868
  64.3 3.4 %collective-permute-start.7 = (bf16[256,512]{1,0:T(8,128)(2,1)S(1)}, bf16[256,512]{1,0:T(8,128)(2,1)S(1)}, u32[]{:S(2)}, u32[]{:S(2)}) collective-permute-start(bf16[256,512]{1,0:T(8,128)(2,1)S(1)} %get-tuple-element.27), channel_id=1, source_target_pairs={{0,8},{8,0},{1,9},{9,1},{2,10},{10,2},{3,11},{11,3},{4,12},{12,4},... | collective-permute-start | bytes 786440 | tf_op jit(solution)/shard_map/ppermute | solution.py:22
  69.4 36.6 %all-to-all-start.1 = ((bf16[8,128,256]{2,1,0:T(8,128)(2,1)}), bf16[8,128,256]{2,1,0:T(8,128)(2,1)S(1)}, u32[]{:S(2)}, u32[]{:S(2)}) async-start(bf16[8,128,256]{2,1,0:T(8,128)(2,1)} %bitcast.15), calls=%async_computation.1 | async-start | bytes 1048576 | tf_op jit(solution)/shard_map/all_to_all | solution.py:30
  76.9 8.5 %collective-permute-start.8 = (bf16[4,1,1,16,1536]{4,3,2,1,0:T(8,128)(2,1)S(1)}, bf16[4,1,1,16,1536]{4,3,2,1,0:T(8,128)(2,1)S(1)}, u32[]{:S(2)}, u32[]{:S(2)}) collective-permute-start(bf16[4,1,1,16,1536]{4,3,2,1,0:T(8,128)(2,1)S(1)} %bitcast.60), channel_id=1, source_target_pairs={{0,128},{128,0},{256,384},{384,256},{1,129},{129,1},{257,385},{385... | collective-permute-start | bytes 589832 | tf_op jit(solution)/shard_map/ppermute | solution.py:22
  85.5 13.4 %collective-permute-start.9 = (bf16[4,1,2,16,1536]{4,3,2,1,0:T(8,128)(2,1)S(1)}, bf16[4,1,2,16,1536]{4,3,2,1,0:T(8,128)(2,1)S(1)}, u32[]{:S(2)}, u32[]{:S(2)}) collective-permute-start(bf16[4,1,2,16,1536]{4,3,2,1,0:T(8,128)(2,1)S(1)} %maximum_select_fusion.1), channel_id=1, source_target_pairs={{0,256},{128,384},{256,0},{384,128},{1,257},{129,385},{257,1},{385... | collective-permute-start | bytes 1179656 | tf_op jit(solution)/shard_map/ppermute | solution.py:22
  89.6 21.1 %copy-start.9 = (s32[1,512]{1,0:T(1,128)S(1)}, s32[1,512]{1,0:T(1,128)}, u32[]{:S(2)}) copy-start(s32[1,512]{1,0:T(1,128)} %param.13) | copy-start | bytes 6148
  107.1 12.8 %all-to-all-start.2 = ((bf16[16,8,1536]{2,1,0:T(8,128)(2,1)}), bf16[16,8,1536]{2,1,0:T(8,128)(2,1)S(1)}, u32[]{:S(2)}, u32[]{:S(2)}) async-start(bf16[16,8,1536]{2,1,0:T(8,128)(2,1)} %fusion.1), calls=%async_computation.2 | async-start | bytes 786432 | tf_op jit(solution)/shard_map/all_to_all | solution.py:30
  111.0 14.5 %collective-permute-start.11 = (bf16[128,256]{1,0:T(8,128)(2,1)S(1)}, bf16[128,256]{1,0:T(8,128)(2,1)S(1)}, u32[]{:S(2)}, u32[]{:S(2)}) collective-permute-start(bf16[128,256]{1,0:T(8,128)(2,1)S(1)} %reduce_sum.43), channel_id=1, source_target_pairs={{0,128},{128,0},{256,384},{384,256},{1,129},{129,1},{257,385},{385... | collective-permute-start | bytes 196616 | tf_op jit(solution)/shard_map/ppermute | solution.py:22
  120.0 14.8 %collective-permute-start.10 = (bf16[8,1536]{1,0:T(8,128)(2,1)S(1)}, bf16[8,1536]{1,0:T(8,128)(2,1)S(1)}, u32[]{:S(2)}, u32[]{:S(2)}) collective-permute-start(bf16[8,1536]{1,0:T(8,128)(2,1)S(1)} %convert_element_type.44), channel_id=1, source_target_pairs={{0,1},{1,0},{2,3},{3,2},{4,5},{5,4},{6,7},{7,6},{8,9},{9,8},{10,11... | collective-permute-start | bytes 73736 | tf_op jit(solution)/shard_map/ppermute | solution.py:22
  125.5 20.8 %collective-permute-start.12 = (bf16[2,128,256]{2,1,0:T(8,128)(2,1)S(1)}, bf16[2,128,256]{2,1,0:T(8,128)(2,1)S(1)}, u32[]{:S(2)}, u32[]{:S(2)}) collective-permute-start(bf16[2,128,256]{2,1,0:T(8,128)(2,1)S(1)} %pad_maximum_fusion.1), channel_id=1, source_target_pairs={{0,256},{128,384},{256,0},{384,128},{1,257},{129,385},{257,1},{385... | collective-permute-start | bytes 393224 | tf_op jit(solution)/shard_map/ppermute | solution.py:22
  141.0 13.7 %all-to-all-start.3 = ((bf16[16,4,8,384]{3,2,1,0:T(8,128)(2,1)}), bf16[16,4,8,384]{3,2,1,0:T(8,128)(2,1)S(1)}, u32[]{:S(2)}, u32[]{:S(2)}) async-start(bf16[16,4,8,384]{3,2,1,0:T(8,128)(2,1)} %bitcast.24), calls=%async_computation.3 | async-start | bytes 786432 | tf_op jit(solution)/shard_map/all_to_all | solution.py:30
  155.8 17.3 %all-to-all-start.4 = ((bf16[4,64,384]{2,1,0:T(8,128)(2,1)}), bf16[4,64,384]{2,1,0:T(8,128)(2,1)S(1)}, u32[]{:S(2)}, u32[]{:S(2)}) async-start(bf16[4,64,384]{2,1,0:T(8,128)(2,1)} %bitcast.28), calls=%async_computation.4 | async-start | bytes 393216 | tf_op jit(solution)/shard_map/all_to_all | solution.py:30
  173.8 10.5 %all-to-all-start.5 = ((bf16[4,64,384]{2,1,0:T(8,128)(2,1)}), bf16[4,64,384]{2,1,0:T(8,128)(2,1)S(1)}, u32[]{:S(2)}, u32[]{:S(2)}) async-start(bf16[4,64,384]{2,1,0:T(8,128)(2,1)} %broadcast_in_dim.54), calls=%async_computation.5 | async-start | bytes 393216 | tf_op jit(solution)/shard_map/all_to_all | solution.py:30
  (5 other events, 8.6 us)

commit v5 on v4

--- a/solution.py
+++ b/solution.py
@@ -157,6 +157,7 @@
     hid_all = jnp.concatenate([hid_two, swap(hid_two, "dp", 2)])
     hid_all = jnp.take(hid_all, x ^ jnp.arange(4), axis=0).reshape(512, 256)
     err = err + swap(err.astype(BF), "zh", 1).astype(F32)
+    err, hid_all = lax.optimization_barrier((err, hid_all))
 
     passage = segments[0]
     same = (passage[:, None] == passage[None, :]).astype(F32)
@@ -164,11 +165,11 @@
     weight = lax.dynamic_slice_in_dim(weight_all, zq * 128 + zp * 64 + core * 32 + y * 8, 8, 0)
     scaled_f = weight[:, None] * err
     student_grad = -lax.dynamic_slice_in_dim(scaled_f, zh * 4, 4, 0)
-    scaled = lax.all_gather(scaled_f.astype(BF), ("zp", "co"))
+    scaled = lax.all_gather(scaled_f.astype(BF), "co")
 
-    quarters = jnp.moveaxis(scaled.reshape(4, 8, 4, 384), 2, 0)[:, None]
-    quarters = jnp.broadcast_to(quarters, (4, 4, 4, 8, 384)).reshape(16, 4, 8, 384)
-    scaled_all = exchange(quarters, ("dp", "y")).reshape(4, 4, 4, 8, 384)
+    quarters = jnp.moveaxis(scaled.reshape(2, 8, 4, 384), 2, 0)[:, None]
+    quarters = jnp.broadcast_to(quarters, (4, 8, 2, 8, 384)).reshape(32, 2, 8, 384)
+    scaled_all = exchange(quarters, ("dp", "zp", "y")).reshape(8, 4, 2, 8, 384)
     scaled_all = jnp.swapaxes(scaled_all, 1, 2).reshape(512, 384)
     grad = lax.dot_general(hid_all, scaled_all, (((0,), (0,)), ((), ())), preferred_element_type=F32)
     grad = jnp.sum(exchange(grad.astype(BF).reshape(4, 64, 384), "zq").astype(F32), 0).astype(BF)

time: 186 us -> 184 us (0.989)
  the two profiles are of different devices: /device:TPU:2 before, /device:TPU:8 now
where the time goes in v5:
time: 184 us; the launch traced here: 182 us
  starting transfers between devices  81.9 us (45%)
  waiting for transfers between devices  59.4 us (32%)
  blocking collectives  18.2 us (10%)
  local copies, waits for them, and re-layouts  11.4 us (6%)
  Pallas kernels  5.65 us (3%)
  matrix products  2.39 us (1%)
  other arithmetic  2.35 us (1%)
    ppermute x13, starting transfers between devices, swap(): lax.ppermute(x, axis, [(i, i ^ mask) for i in range(lax.axis_size(axis))])  57.3 us
    all_to_all x5, waiting for transfers between devices, exchange(): return lax.all_to_all(x, axes, 0, 0, tiled=True)  34.5 us
    ppermute x13, waiting for transfers between devices, swap(): lax.ppermute(x, axis, [(i, i ^ mask) for i in range(lax.axis_size(axis))])  24.9 us
    all_to_all x5, starting transfers between devices, exchange(): return lax.all_to_all(x, axes, 0, 0, tiled=True)  24.7 us
    all_to_all x1, blocking collectives, exchange(): return lax.all_to_all(x, axes, 0, 0, tiled=True)  16.4 us
    unnamed x20, local copies, waits for them, and re-layouts  8.59 us
  transfers between devices with their start and end apart: 18, of which 11 were waited for; matrix products, arithmetic and copies ran while one was open for 1% of the time, Pallas kernels for 2%

profile of v5, /device:TPU:8, one launch (start us, length us, event | category | flops | bytes accessed | tf_op | source)
XLA Modules:
  0.0 182.4 jit_solution(1959560117334121103)
XLA Ops:
  0.6 15.9 %collective-permute-start = (bf16[64,1792]{1,0:T(8,128)(2,1)}, bf16[64,1792]{1,0:T(8,128)(2,1)S(1)}, u32[]{:S(2)}, u32[]{:S(2)}) collective-permute-start(bf16[64,1792]{1,0:T(8,128)(2,1)} %refs_0_), channel_id=1, source_target_pairs={{0,1},{1,0},{2,3},{3,2},{4,5},{5,4},{6,7},{7,6},{8,9},{9,8},{10,11... | collective-permute-start | bytes 688136 | tf_op jit(solution)/shard_map/ppermute | solution.py:22
  18.9 4.5 %collective-permute-start.3 = (bf16[64,1792]{1,0:T(8,128)(2,1)}, bf16[64,1792]{1,0:T(8,128)(2,1)S(1)}, u32[]{:S(2)}, u32[]{:S(2)}) collective-permute-start(bf16[64,1792]{1,0:T(8,128)(2,1)} %refs_0_), channel_id=1, source_target_pairs={{0,4},{2,6},{4,0},{6,2},{1,5},{3,7},{5,1},{7,3},{8,12},{10,14},{12... | collective-permute-start | bytes 688136 | tf_op jit(solution)/shard_map/ppermute | solution.py:22
  23.4 2.4 %collective-permute-start.4 = (bf16[64,1792]{1,0:T(8,128)(2,1)}, bf16[64,1792]{1,0:T(8,128)(2,1)S(1)}, u32[]{:S(2)}, u32[]{:S(2)}) collective-permute-start(bf16[64,1792]{1,0:T(8,128)(2,1)} %refs_0_), channel_id=1, source_target_pairs={{0,6},{2,4},{4,2},{6,0},{1,7},{3,5},{5,3},{7,1},{8,14},{10,12},{12... | collective-permute-start | bytes 688136 | tf_op jit(solution)/shard_map/ppermute | solution.py:22
  25.8 4.3 %collective-permute-start.1 = (bf16[1,1,16,1536]{3,2,1,0:T(8,128)(2,1)S(1)}, bf16[1,1,16,1536]{3,2,1,0:T(8,128)(2,1)S(1)}, u32[]{:S(2)}, u32[]{:S(2)}) collective-permute-start(bf16[1,1,16,1536]{3,2,1,0:T(8,128)(2,1)S(1)} %dynamic-slice_bitcast_fusion), channel_id=1, source_target_pairs={{0,64},{32,96},{64,0},{96,32},{1,65},{33,97},{65,1},{97,33},{2,66}... | collective-permute-start | bytes 147464 | tf_op jit(solution)/shard_map/ppermute | solution.py:22
  36.3 5.5 %collective-permute-done.1 = bf16[1,1,16,1536]{3,2,1,0:T(8,128)(2,1)S(1)} collective-permute-done((bf16[1,1,16,1536]{3,2,1,0:T(8,128)(2,1)S(1)}, bf16[1,1,16,1536]{3,2,1,0:T(8,128)(2,1)S(1)}, u32[]{:S(2)}, u32[]{:S(2)}) %collective-permute-start.1) | collective-permute-done | bytes 49184 | tf_op jit(solution)/shard_map/ppermute | solution.py:22
  42.8 4.9 %all-to-all-start = ((bf16[4,64,1792]{2,1,0:T(8,128)(2,1)}), bf16[4,64,1792]{2,1,0:T(8,128)(2,1)S(1)}, u32[]{:S(2)}, u32[]{:S(2)}) async-start(bf16[4,64,1792]{2,1,0:T(8,128)(2,1)} %broadcast_in_dim.52), calls=%async_computation | async-start | bytes 1835008 | tf_op jit(solution)/shard_map/all_to_all | solution.py:30
  55.8 4.3 %all-to-all-done = bf16[4,64,1792]{2,1,0:T(8,128)(2,1)S(1)} async-done(((bf16[4,64,1792]{2,1,0:T(8,128)(2,1)}), bf16[4,64,1792]{2,1,0:T(8,128)(2,1)S(1)}, u32[]{:S(2)}, u32[]{:S(2)}) %all-to-all-start) | async-done | bytes 917536 | tf_op jit(solution)/shard_map/all_to_all | solution.py:30
  68.4 7.6 %all-to-all-start.1 = ((bf16[8,128,256]{2,1,0:T(8,128)(2,1)}), bf16[8,128,256]{2,1,0:T(8,128)(2,1)S(1)}, u32[]{:S(2)}, u32[]{:S(2)}) async-start(bf16[8,128,256]{2,1,0:T(8,128)(2,1)} %bitcast.15), calls=%async_computation.1 | async-start | bytes 1048576 | tf_op jit(solution)/shard_map/all_to_all | solution.py:30
  75.9 3.4 %collective-permute-start.8 = (bf16[4,1,1,16,1536]{4,3,2,1,0:T(8,128)(2,1)S(1)}, bf16[4,1,1,16,1536]{4,3,2,1,0:T(8,128)(2,1)S(1)}, u32[]{:S(2)}, u32[]{:S(2)}) collective-permute-start(bf16[4,1,1,16,1536]{4,3,2,1,0:T(8,128)(2,1)S(1)} %bitcast.63), channel_id=1, source_target_pairs={{0,128},{128,0},{256,384},{384,256},{1,129},{129,1},{257,385},{385... | collective-permute-start | bytes 589832 | tf_op jit(solution)/shard_map/ppermute | solution.py:22
  79.3 5.1 %collective-permute-done.8 = bf16[4,1,1,16,1536]{4,3,2,1,0:T(8,128)(2,1)S(1)} collective-permute-done((bf16[4,1,1,16,1536]{4,3,2,1,0:T(8,128)(2,1)S(1)}, bf16[4,1,1,16,1536]{4,3,2,1,0:T(8,128)(2,1)S(1)}, u32[]{:S(2)}, u32[]{:S(2)}) %collective-permute-start.8) | collective-permute-done | bytes 196640 | tf_op jit(solution)/shard_map/ppermute | solution.py:22
  84.5 4.9 %collective-permute-start.9 = (bf16[4,1,2,16,1536]{4,3,2,1,0:T(8,128)(2,1)S(1)}, bf16[4,1,2,16,1536]{4,3,2,1,0:T(8,128)(2,1)S(1)}, u32[]{:S(2)}, u32[]{:S(2)}) collective-permute-start(bf16[4,1,2,16,1536]{4,3,2,1,0:T(8,128)(2,1)S(1)} %maximum_select_fusion.1), channel_id=1, source_target_pairs={{0,256},{128,384},{256,0},{384,128},{1,257},{129,385},{257,1},{385... | collective-permute-start | bytes 1179656 | tf_op jit(solution)/shard_map/ppermute | solution.py:22
  89.8 8.1 %collective-permute-done.9 = bf16[4,1,2,16,1536]{4,3,2,1,0:T(8,128)(2,1)S(1)} collective-permute-done((bf16[4,1,2,16,1536]{4,3,2,1,0:T(8,128)(2,1)S(1)}, bf16[4,1,2,16,1536]{4,3,2,1,0:T(8,128)(2,1)S(1)}, u32[]{:S(2)}, u32[]{:S(2)}) %collective-permute-start.9) | collective-permute-done | bytes 393248 | tf_op jit(solution)/shard_map/ppermute | solution.py:22
  98.0 7.0 %all-to-all-done.1 = bf16[8,128,256]{2,1,0:T(8,128)(2,1)S(1)} async-done(((bf16[8,128,256]{2,1,0:T(8,128)(2,1)}), bf16[8,128,256]{2,1,0:T(8,128)(2,1)S(1)}, u32[]{:S(2)}, u32[]{:S(2)}) %all-to-all-start.1) | async-done | bytes 524320 | tf_op jit(solution)/shard_map/all_to_all | solution.py:30
  106.1 4.8 %all-to-all-start.2 = ((bf16[16,8,1536]{2,1,0:T(8,128)(2,1)}), bf16[16,8,1536]{2,1,0:T(8,128)(2,1)S(1)}, u32[]{:S(2)}, u32[]{:S(2)}) async-start(bf16[16,8,1536]{2,1,0:T(8,128)(2,1)} %fusion.1), calls=%async_computation.2 | async-start | bytes 786432 | tf_op jit(solution)/shard_map/all_to_all | solution.py:30
  111.3 3.4 %collective-permute-start.11 = (bf16[128,256]{1,0:T(8,128)(2,1)S(1)}, bf16[128,256]{1,0:T(8,128)(2,1)S(1)}, u32[]{:S(2)}, u32[]{:S(2)}) collective-permute-start(bf16[128,256]{1,0:T(8,128)(2,1)S(1)} %reduce_sum.43), channel_id=1, source_target_pairs={{0,128},{128,0},{256,384},{384,256},{1,129},{129,1},{257,385},{385... | collective-permute-start | bytes 196616 | tf_op jit(solution)/shard_map/ppermute | solution.py:22
  114.7 4.1 %all-to-all-done.2 = bf16[16,8,1536]{2,1,0:T(8,128)(2,1)S(1)} async-done(((bf16[16,8,1536]{2,1,0:T(8,128)(2,1)}), bf16[16,8,1536]{2,1,0:T(8,128)(2,1)S(1)}, u32[]{:S(2)}, u32[]{:S(2)}) %all-to-all-start.2) | async-done | bytes 393248 | tf_op jit(solution)/shard_map/all_to_all | solution.py:30
  118.9 5.5 %collective-permute-start.10 = (bf16[8,1536]{1,0:T(8,128)(2,1)S(1)}, bf16[8,1536]{1,0:T(8,128)(2,1)S(1)}, u32[]{:S(2)}, u32[]{:S(2)}) collective-permute-start(bf16[8,1536]{1,0:T(8,128)(2,1)S(1)} %convert_element_type.44), channel_id=1, source_target_pairs={{0,1},{1,0},{2,3},{3,2},{4,5},{5,4},{6,7},{7,6},{8,9},{9,8},{10,11... | collective-permute-start | bytes 73736 | tf_op jit(solution)/shard_map/ppermute | solution.py:22
  124.5 4.9 %collective-permute-start.12 = (bf16[2,128,256]{2,1,0:T(8,128)(2,1)S(1)}, bf16[2,128,256]{2,1,0:T(8,128)(2,1)S(1)}, u32[]{:S(2)}, u32[]{:S(2)}) collective-permute-start(bf16[2,128,256]{2,1,0:T(8,128)(2,1)S(1)} %pad_maximum_fusion.1), channel_id=1, source_target_pairs={{0,256},{128,384},{256,0},{384,128},{1,257},{129,385},{257,1},{385... | collective-permute-start | bytes 393224 | tf_op jit(solution)/shard_map/ppermute | solution.py:22
  129.4 4.2 %collective-permute-done.10 = bf16[8,1536]{1,0:T(8,128)(2,1)S(1)} collective-permute-done((bf16[8,1536]{1,0:T(8,128)(2,1)S(1)}, bf16[8,1536]{1,0:T(8,128)(2,1)S(1)}, u32[]{:S(2)}, u32[]{:S(2)}) %collective-permute-start.10) | collective-permute-done | bytes 24608 | tf_op jit(solution)/shard_map/ppermute | solution.py:22
  136.3 16.4 %all_to_all.30 = bf16[32,2,8,384]{3,2,1,0:T(8,128)(2,1)S(1)} all-to-all(bf16[32,2,8,384]{3,2,1,0:T(8,128)(2,1)S(1)} %bitcast.60), channel_id=1, replica_groups=mesh['dp'=4,'zq'=4,'zp'=2,'co'=2,'y'=4,'zh'=2] {'dp','zp','y'}, dimensions={0} | all-to-all | bytes 786432 | tf_op jit(solution)/shard_map/all_to_all | solution.py:30
  153.8 4.0 %all-to-all-start.4 = ((bf16[4,64,384]{2,1,0:T(8,128)(2,1)}), bf16[4,64,384]{2,1,0:T(8,128)(2,1)S(1)}, u32[]{:S(2)}, u32[]{:S(2)}) async-start(bf16[4,64,384]{2,1,0:T(8,128)(2,1)} %bitcast.29), calls=%async_computation.4 | async-start | bytes 393216 | tf_op jit(solution)/shard_map/all_to_all | solution.py:30
  157.8 13.4 %all-to-all-done.4 = bf16[4,64,384]{2,1,0:T(8,128)(2,1)S(1)} async-done(((bf16[4,64,384]{2,1,0:T(8,128)(2,1)}), bf16[4,64,384]{2,1,0:T(8,128)(2,1)S(1)}, u32[]{:S(2)}, u32[]{:S(2)}) %all-to-all-start.4) | async-done | bytes 196640 | tf_op jit(solution)/shard_map/all_to_all | solution.py:30
  172.0 3.4 %all-to-all-start.5 = ((bf16[4,64,384]{2,1,0:T(8,128)(2,1)}), bf16[4,64,384]{2,1,0:T(8,128)(2,1)S(1)}, u32[]{:S(2)}, u32[]{:S(2)}) async-start(bf16[4,64,384]{2,1,0:T(8,128)(2,1)} %broadcast_in_dim.60), calls=%async_computation.5 | async-start | bytes 393216 | tf_op jit(solution)/shard_map/all_to_all | solution.py:30
  176.0 5.7 %all-to-all-done.5 = bf16[4,64,384]{2,1,0:T(8,128)(2,1)S(1)} async-done(((bf16[4,64,384]{2,1,0:T(8,128)(2,1)}), bf16[4,64,384]{2,1,0:T(8,128)(2,1)S(1)}, u32[]{:S(2)}, u32[]{:S(2)}) %all-to-all-start.5) | async-done | bytes 196640 | tf_op jit(solution)/shard_map/all_to_all | solution.py:30
  (76 shorter events, 33.7 us)
Async XLA Ops:
  0.6 25.1 %copy-start = (bf16[64,1536]{1,0:T(8,128)(2,1)S(1)}, bf16[64,1536]{1,0:T(8,128)(2,1)}, u32[]{:S(2)}) copy-start(bf16[64,1536]{1,0:T(8,128)(2,1)} %param.11) | copy-start | bytes 589828
  0.6 41.1 %collective-permute-start = (bf16[64,1792]{1,0:T(8,128)(2,1)}, bf16[64,1792]{1,0:T(8,128)(2,1)S(1)}, u32[]{:S(2)}, u32[]{:S(2)}) collective-permute-start(bf16[64,1792]{1,0:T(8,128)(2,1)} %refs_0_), channel_id=1, source_target_pairs={{0,1},{1,0},{2,3},{3,2},{4,5},{5,4},{6,7},{7,6},{8,9},{9,8},{10,11... | collective-permute-start | bytes 688136 | tf_op jit(solution)/shard_map/ppermute | solution.py:22
  16.5 25.3 %collective-permute-start.2 = (bf16[64,1792]{1,0:T(8,128)(2,1)}, bf16[64,1792]{1,0:T(8,128)(2,1)S(1)}, u32[]{:S(2)}, u32[]{:S(2)}) collective-permute-start(bf16[64,1792]{1,0:T(8,128)(2,1)} %refs_0_), channel_id=1, source_target_pairs={{0,2},{2,0},{4,6},{6,4},{1,3},{3,1},{5,7},{7,5},{8,10},{10,8},{12,... | collective-permute-start | bytes 688136 | tf_op jit(solution)/shard_map/ppermute | solution.py:22
  18.9 22.9 %collective-permute-start.3 = (bf16[64,1792]{1,0:T(8,128)(2,1)}, bf16[64,1792]{1,0:T(8,128)(2,1)S(1)}, u32[]{:S(2)}, u32[]{:S(2)}) collective-permute-start(bf16[64,1792]{1,0:T(8,128)(2,1)} %refs_0_), channel_id=1, source_target_pairs={{0,4},{2,6},{4,0},{6,2},{1,5},{3,7},{5,1},{7,3},{8,12},{10,14},{12... | collective-permute-start | bytes 688136 | tf_op jit(solution)/shard_map/ppermute | solution.py:22
  23.4 18.4 %collective-permute-start.4 = (bf16[64,1792]{1,0:T(8,128)(2,1)}, bf16[64,1792]{1,0:T(8,128)(2,1)S(1)}, u32[]{:S(2)}, u32[]{:S(2)}) collective-permute-start(bf16[64,1792]{1,0:T(8,128)(2,1)} %refs_0_), channel_id=1, source_target_pairs={{0,6},{2,4},{4,2},{6,0},{1,7},{3,5},{5,3},{7,1},{8,14},{10,12},{12... | collective-permute-start | bytes 688136 | tf_op jit(solution)/shard_map/ppermute | solution.py:22
  25.8 16.0 %collective-permute-start.1 = (bf16[1,1,16,1536]{3,2,1,0:T(8,128)(2,1)S(1)}, bf16[1,1,16,1536]{3,2,1,0:T(8,128)(2,1)S(1)}, u32[]{:S(2)}, u32[]{:S(2)}) collective-permute-start(bf16[1,1,16,1536]{3,2,1,0:T(8,128)(2,1)S(1)} %dynamic-slice_bitcast_fusion), channel_id=1, source_target_pairs={{0,64},{32,96},{64,0},{96,32},{1,65},{33,97},{65,1},{97,33},{2,66}... | collective-permute-start | bytes 147464 | tf_op jit(solution)/shard_map/ppermute | solution.py:22
  30.1 2.0 %copy-start.4 = (bf16[1792,1024]{1,0:T(8,128)(2,1)S(1)}, bf16[1792,1024]{1,0:T(8,128)(2,1)}, u32[]{:S(2)}) copy-start(bf16[1792,1024]{1,0:T(8,128)(2,1)} %weight_ref.1) | copy-start | bytes 11010052
  32.8 16.8 %copy-start.5 = (bf16[64,1792]{1,0:T(8,128)(2,1)S(1)}, bf16[64,1792]{1,0:T(8,128)(2,1)}, u32[]{:S(2)}) copy-start(bf16[64,1792]{1,0:T(8,128)(2,1)} %refs_0_) | copy-start | bytes 688132
  42.8 17.3 %all-to-all-start = ((bf16[4,64,1792]{2,1,0:T(8,128)(2,1)}), bf16[4,64,1792]{2,1,0:T(8,128)(2,1)S(1)}, u32[]{:S(2)}, u32[]{:S(2)}) async-start(bf16[4,64,1792]{2,1,0:T(8,128)(2,1)} %broadcast_in_dim.52), calls=%async_computation | async-start | bytes 1835008 | tf_op jit(solution)/shard_map/all_to_all | solution.py:30
  47.7 8.0 %collective-permute-start.6 = (bf16[2,1,16,1536]{3,2,1,0:T(8,128)(2,1)S(1)}, bf16[2,1,16,1536]{3,2,1,0:T(8,128)(2,1)S(1)}, u32[]{:S(2)}, u32[]{:S(2)}) collective-permute-start(bf16[2,1,16,1536]{3,2,1,0:T(8,128)(2,1)S(1)} %maximum_select_fusion.3), channel_id=1, source_target_pairs={{0,32},{32,0},{64,96},{96,64},{1,33},{33,1},{65,97},{97,65},{2,34}... | collective-permute-start | bytes 294920 | tf_op jit(solution)/shard_map/ppermute | solution.py:22
  51.7 13.7 %copy-start.7 = (bf16[512,64]{0,1:T(8,128)(2,1)S(1)}, bf16[512,64]{0,1:T(8,128)(2,1)}, u32[]{:S(2)}) copy-start(bf16[512,64]{0,1:T(8,128)(2,1)} %param.10) | copy-start | bytes 196612
  52.9 12.8 %collective-permute-start.5 = (bf16[256,512]{1,0:T(8,128)(2,1)S(1)}, bf16[256,512]{1,0:T(8,128)(2,1)S(1)}, u32[]{:S(2)}, u32[]{:S(2)}) collective-permute-start(bf16[256,512]{1,0:T(8,128)(2,1)S(1)} %get-tuple-element.24), channel_id=1, source_target_pairs={{0,8},{8,0},{1,9},{9,1},{2,10},{10,2},{3,11},{11,3},{4,12},{12,4},... | collective-permute-start | bytes 786440 | tf_op jit(solution)/shard_map/ppermute | solution.py:22
  62.1 27.3 %copy-start.8 = (bf16[4,1536]{1,0:T(4,128)(2,1)S(1)}, bf16[4,1536]{1,0:T(4,128)(2,1)}, u32[]{:S(2)}) copy-start(bf16[4,1536]{1,0:T(4,128)(2,1)} %param.12) | copy-start | bytes 36868
  63.3 3.4 %collective-permute-start.7 = (bf16[256,512]{1,0:T(8,128)(2,1)S(1)}, bf16[256,512]{1,0:T(8,128)(2,1)S(1)}, u32[]{:S(2)}, u32[]{:S(2)}) collective-permute-start(bf16[256,512]{1,0:T(8,128)(2,1)S(1)} %get-tuple-element.29), channel_id=1, source_target_pairs={{0,8},{8,0},{1,9},{9,1},{2,10},{10,2},{3,11},{11,3},{4,12},{12,4},... | collective-permute-start | bytes 786440 | tf_op jit(solution)/shard_map/ppermute | solution.py:22
  68.4 36.6 %all-to-all-start.1 = ((bf16[8,128,256]{2,1,0:T(8,128)(2,1)}), bf16[8,128,256]{2,1,0:T(8,128)(2,1)S(1)}, u32[]{:S(2)}, u32[]{:S(2)}) async-start(bf16[8,128,256]{2,1,0:T(8,128)(2,1)} %bitcast.15), calls=%async_computation.1 | async-start | bytes 1048576 | tf_op jit(solution)/shard_map/all_to_all | solution.py:30
  75.9 8.5 %collective-permute-start.8 = (bf16[4,1,1,16,1536]{4,3,2,1,0:T(8,128)(2,1)S(1)}, bf16[4,1,1,16,1536]{4,3,2,1,0:T(8,128)(2,1)S(1)}, u32[]{:S(2)}, u32[]{:S(2)}) collective-permute-start(bf16[4,1,1,16,1536]{4,3,2,1,0:T(8,128)(2,1)S(1)} %bitcast.63), channel_id=1, source_target_pairs={{0,128},{128,0},{256,384},{384,256},{1,129},{129,1},{257,385},{385... | collective-permute-start | bytes 589832 | tf_op jit(solution)/shard_map/ppermute | solution.py:22
  84.5 13.4 %collective-permute-start.9 = (bf16[4,1,2,16,1536]{4,3,2,1,0:T(8,128)(2,1)S(1)}, bf16[4,1,2,16,1536]{4,3,2,1,0:T(8,128)(2,1)S(1)}, u32[]{:S(2)}, u32[]{:S(2)}) collective-permute-start(bf16[4,1,2,16,1536]{4,3,2,1,0:T(8,128)(2,1)S(1)} %maximum_select_fusion.1), channel_id=1, source_target_pairs={{0,256},{128,384},{256,0},{384,128},{1,257},{129,385},{257,1},{385... | collective-permute-start | bytes 1179656 | tf_op jit(solution)/shard_map/ppermute | solution.py:22
  89.5 21.4 %copy-start.9 = (s32[1,512]{1,0:T(1,128)S(1)}, s32[1,512]{1,0:T(1,128)}, u32[]{:S(2)}) copy-start(s32[1,512]{1,0:T(1,128)} %param.13) | copy-start | bytes 6148
  106.1 12.8 %all-to-all-start.2 = ((bf16[16,8,1536]{2,1,0:T(8,128)(2,1)}), bf16[16,8,1536]{2,1,0:T(8,128)(2,1)S(1)}, u32[]{:S(2)}, u32[]{:S(2)}) async-start(bf16[16,8,1536]{2,1,0:T(8,128)(2,1)} %fusion.1), calls=%async_computation.2 | async-start | bytes 786432 | tf_op jit(solution)/shard_map/all_to_all | solution.py:30
  111.3 13.1 %collective-permute-start.11 = (bf16[128,256]{1,0:T(8,128)(2,1)S(1)}, bf16[128,256]{1,0:T(8,128)(2,1)S(1)}, u32[]{:S(2)}, u32[]{:S(2)}) collective-permute-start(bf16[128,256]{1,0:T(8,128)(2,1)S(1)} %reduce_sum.43), channel_id=1, source_target_pairs={{0,128},{128,0},{256,384},{384,256},{1,129},{129,1},{257,385},{385... | collective-permute-start | bytes 196616 | tf_op jit(solution)/shard_map/ppermute | solution.py:22
  118.9 14.7 %collective-permute-start.10 = (bf16[8,1536]{1,0:T(8,128)(2,1)S(1)}, bf16[8,1536]{1,0:T(8,128)(2,1)S(1)}, u32[]{:S(2)}, u32[]{:S(2)}) collective-permute-start(bf16[8,1536]{1,0:T(8,128)(2,1)S(1)} %convert_element_type.44), channel_id=1, source_target_pairs={{0,1},{1,0},{2,3},{3,2},{4,5},{5,4},{6,7},{7,6},{8,9},{9,8},{10,11... | collective-permute-start | bytes 73736 | tf_op jit(solution)/shard_map/ppermute | solution.py:22
  124.5 9.2 %collective-permute-start.12 = (bf16[2,128,256]{2,1,0:T(8,128)(2,1)S(1)}, bf16[2,128,256]{2,1,0:T(8,128)(2,1)S(1)}, u32[]{:S(2)}, u32[]{:S(2)}) collective-permute-start(bf16[2,128,256]{2,1,0:T(8,128)(2,1)S(1)} %pad_maximum_fusion.1), channel_id=1, source_target_pairs={{0,256},{128,384},{256,0},{384,128},{1,257},{129,385},{257,1},{385... | collective-permute-start | bytes 393224 | tf_op jit(solution)/shard_map/ppermute | solution.py:22
  153.8 17.5 %all-to-all-start.4 = ((bf16[4,64,384]{2,1,0:T(8,128)(2,1)}), bf16[4,64,384]{2,1,0:T(8,128)(2,1)S(1)}, u32[]{:S(2)}, u32[]{:S(2)}) async-start(bf16[4,64,384]{2,1,0:T(8,128)(2,1)} %bitcast.29), calls=%async_computation.4 | async-start | bytes 393216 | tf_op jit(solution)/shard_map/all_to_all | solution.py:30
  172.0 9.7 %all-to-all-start.5 = ((bf16[4,64,384]{2,1,0:T(8,128)(2,1)}), bf16[4,64,384]{2,1,0:T(8,128)(2,1)S(1)}, u32[]{:S(2)}, u32[]{:S(2)}) async-start(bf16[4,64,384]{2,1,0:T(8,128)(2,1)} %broadcast_in_dim.60), calls=%async_computation.5 | async-start | bytes 393216 | tf_op jit(solution)/shard_map/all_to_all | solution.py:30
  (4 other events, 6.5 us)

commit v6 on v5

--- a/solution.py
+++ b/solution.py
@@ -99,10 +99,10 @@
     y, zh = at_ref[0], at_ref[1]
     for far, (keep, got) in enumerate(((near_ref, near_got_ref), (far_ref, far_got_ref))):
         for k in range(4):
-            to_y, to_z = (k, 1 - zh) if far else (y ^ k, zh)
-            value = keep[k].astype(F32) + got[k].astype(F32) + res_ref[2 * to_y + to_z].astype(F32)
+            at, to_z = (k, 1 - zh) if far else (y ^ k, zh)
+            value = keep[at].astype(F32) + got[at].astype(F32) + res_ref[2 * k + to_z].astype(F32)
             for zp in range(2):
-                out_ref[to_y, zp, to_z] = value[:, 256 * zp : 256 * zp + 256].astype(BF)
+                out_ref[k, zp, to_z] = value[:, 256 * zp : 256 * zp + 256].astype(BF)
 
 
 def combine(at, near, near_got, far, far_got, res):
@@ -154,10 +154,11 @@
     err = jnp.dot(hid, pg, preferred_element_type=F32) - own_student
     err = jnp.sum(exchange(err.astype(BF).reshape(16, 8, -1), ("zp", "co", "y")).astype(F32), 0)
     hid_two = after(jnp.stack([hid, swap(hid, "dp", 1)]), err)
-    hid_all = jnp.concatenate([hid_two, swap(hid_two, "dp", 2)])
-    hid_all = jnp.take(hid_all, x ^ jnp.arange(4), axis=0).reshape(512, 256)
+    hid_got = swap(hid_two, "dp", 2)
     err = err + swap(err.astype(BF), "zh", 1).astype(F32)
-    err, hid_all = lax.optimization_barrier((err, hid_all))
+    err, hid_got = lax.optimization_barrier((err, hid_got))
+    hid_two = placed(hid_two[:1], hid_two[1:], x & 1, 0)
+    hid_all = placed(hid_two, placed(hid_got[:1], hid_got[1:], x & 1, 0), x >> 1, 0).reshape(512, 256)
 
     passage = segments[0]
     same = (passage[:, None] == passage[None, :]).astype(F32)

time: 184 us -> 184 us (level)
  blocking collectives: 18.2 us -> 1.83 us
  waiting for transfers between devices: 59.4 us -> 69.2 us
  starting transfers between devices: 81.9 us -> 88.8 us
    all_to_all x1 -> x0, blocking collectives: 16.4 us -> none  [exchange(): return lax.all_to_all(x, axes, 0, 0, tiled=True)]
    all_to_all x5 -> x6, waiting for transfers between devices: 34.5 us -> 44.3 us  [exchange(): return lax.all_to_all(x, axes, 0, 0, tiled=True)]
    all_to_all x5 -> x6, starting transfers between devices: 24.7 us -> 31.5 us  [exchange(): return lax.all_to_all(x, axes, 0, 0, tiled=True)]
  transfers between devices with their start and end apart: 18 -> 19, of which waited for: 11 -> 12; matrix products, arithmetic and copies ran while one was open for 1% -> 1% of each run, Pallas kernels for 2% -> 2%
where the time goes in v6:
time: 184 us; the launch traced here: 183 us
  starting transfers between devices  88.8 us (48%)
  waiting for transfers between devices  69.2 us (38%)
  local copies, waits for them, and re-layouts  11.6 us (6%)
  Pallas kernels  5.62 us (3%)
  matrix products  2.41 us (1%)
  other arithmetic  2.23 us (1%)
    ppermute x13, starting transfers between devices, swap(): lax.ppermute(x, axis, [(i, i ^ mask) for i in range(lax.axis_size(axis))])  57.3 us
    all_to_all x6, waiting for transfers between devices, exchange(): return lax.all_to_all(x, axes, 0, 0, tiled=True)  44.3 us
    all_to_all x6, starting transfers between devices, exchange(): return lax.all_to_all(x, axes, 0, 0, tiled=True)  31.5 us
    ppermute x13, waiting for transfers between devices, swap(): lax.ppermute(x, axis, [(i, i ^ mask) for i in range(lax.axis_size(axis))])  24.9 us
    unnamed x20, local copies, waits for them, and re-layouts  8.59 us
  transfers between devices with their start and end apart: 19, of which 12 were waited for; matrix products, arithmetic and copies ran while one was open for 1% of the time, Pallas kernels for 2%

profile of v6, /device:TPU:8, one launch (start us, length us, event | category | flops | bytes accessed | tf_op | source)
XLA Modules:
  0.0 182.6 jit_solution(3994460031687288025)
XLA Ops:
  0.6 15.9 %collective-permute-start = (bf16[64,1792]{1,0:T(8,128)(2,1)}, bf16[64,1792]{1,0:T(8,128)(2,1)S(1)}, u32[]{:S(2)}, u32[]{:S(2)}) collective-permute-start(bf16[64,1792]{1,0:T(8,128)(2,1)} %refs_0_), channel_id=1, source_target_pairs={{0,1},{1,0},{2,3},{3,2},{4,5},{5,4},{6,7},{7,6},{8,9},{9,8},{10,11... | collective-permute-start | bytes 688136 | tf_op jit(solution)/shard_map/ppermute | solution.py:22
  18.9 4.5 %collective-permute-start.3 = (bf16[64,1792]{1,0:T(8,128)(2,1)}, bf16[64,1792]{1,0:T(8,128)(2,1)S(1)}, u32[]{:S(2)}, u32[]{:S(2)}) collective-permute-start(bf16[64,1792]{1,0:T(8,128)(2,1)} %refs_0_), channel_id=1, source_target_pairs={{0,4},{2,6},{4,0},{6,2},{1,5},{3,7},{5,1},{7,3},{8,12},{10,14},{12... | collective-permute-start | bytes 688136 | tf_op jit(solution)/shard_map/ppermute | solution.py:22
  25.8 4.3 %collective-permute-start.1 = (bf16[1,1,16,1536]{3,2,1,0:T(8,128)(2,1)S(1)}, bf16[1,1,16,1536]{3,2,1,0:T(8,128)(2,1)S(1)}, u32[]{:S(2)}, u32[]{:S(2)}) collective-permute-start(bf16[1,1,16,1536]{3,2,1,0:T(8,128)(2,1)S(1)} %dynamic-slice_bitcast_fusion), channel_id=1, source_target_pairs={{0,64},{32,96},{64,0},{96,32},{1,65},{33,97},{65,1},{97,33},{2,66}... | collective-permute-start | bytes 147464 | tf_op jit(solution)/shard_map/ppermute | solution.py:22
  36.3 5.5 %collective-permute-done.1 = bf16[1,1,16,1536]{3,2,1,0:T(8,128)(2,1)S(1)} collective-permute-done((bf16[1,1,16,1536]{3,2,1,0:T(8,128)(2,1)S(1)}, bf16[1,1,16,1536]{3,2,1,0:T(8,128)(2,1)S(1)}, u32[]{:S(2)}, u32[]{:S(2)}) %collective-permute-start.1) | collective-permute-done | bytes 49184 | tf_op jit(solution)/shard_map/ppermute | solution.py:22
  42.8 4.9 %all-to-all-start = ((bf16[4,64,1792]{2,1,0:T(8,128)(2,1)}), bf16[4,64,1792]{2,1,0:T(8,128)(2,1)S(1)}, u32[]{:S(2)}, u32[]{:S(2)}) async-start(bf16[4,64,1792]{2,1,0:T(8,128)(2,1)} %broadcast_in_dim.21), calls=%async_computation | async-start | bytes 1835008 | tf_op jit(solution)/shard_map/all_to_all | solution.py:30
  55.8 4.3 %all-to-all-done = bf16[4,64,1792]{2,1,0:T(8,128)(2,1)S(1)} async-done(((bf16[4,64,1792]{2,1,0:T(8,128)(2,1)}), bf16[4,64,1792]{2,1,0:T(8,128)(2,1)S(1)}, u32[]{:S(2)}, u32[]{:S(2)}) %all-to-all-start) | async-done | bytes 917536 | tf_op jit(solution)/shard_map/all_to_all | solution.py:30
  68.3 7.6 %all-to-all-start.1 = ((bf16[8,128,256]{2,1,0:T(8,128)(2,1)}), bf16[8,128,256]{2,1,0:T(8,128)(2,1)S(1)}, u32[]{:S(2)}, u32[]{:S(2)}) async-start(bf16[8,128,256]{2,1,0:T(8,128)(2,1)} %bitcast.15), calls=%async_computation.1 | async-start | bytes 1048576 | tf_op jit(solution)/shard_map/all_to_all | solution.py:30
  75.9 3.4 %collective-permute-start.8 = (bf16[4,1,1,16,1536]{4,3,2,1,0:T(8,128)(2,1)S(1)}, bf16[4,1,1,16,1536]{4,3,2,1,0:T(8,128)(2,1)S(1)}, u32[]{:S(2)}, u32[]{:S(2)}) collective-permute-start(bf16[4,1,1,16,1536]{4,3,2,1,0:T(8,128)(2,1)S(1)} %bitcast.58), channel_id=1, source_target_pairs={{0,128},{128,0},{256,384},{384,256},{1,129},{129,1},{257,385},{385... | collective-permute-start | bytes 589832 | tf_op jit(solution)/shard_map/ppermute | solution.py:22
  79.3 5.1 %collective-permute-done.8 = bf16[4,1,1,16,1536]{4,3,2,1,0:T(8,128)(2,1)S(1)} collective-permute-done((bf16[4,1,1,16,1536]{4,3,2,1,0:T(8,128)(2,1)S(1)}, bf16[4,1,1,16,1536]{4,3,2,1,0:T(8,128)(2,1)S(1)}, u32[]{:S(2)}, u32[]{:S(2)}) %collective-permute-start.8) | collective-permute-done | bytes 196640 | tf_op jit(solution)/shard_map/ppermute | solution.py:22
  84.5 4.9 %collective-permute-start.9 = (bf16[4,1,2,16,1536]{4,3,2,1,0:T(8,128)(2,1)S(1)}, bf16[4,1,2,16,1536]{4,3,2,1,0:T(8,128)(2,1)S(1)}, u32[]{:S(2)}, u32[]{:S(2)}) collective-permute-start(bf16[4,1,2,16,1536]{4,3,2,1,0:T(8,128)(2,1)S(1)} %maximum_select_fusion.1), channel_id=1, source_target_pairs={{0,256},{128,384},{256,0},{384,128},{1,257},{129,385},{257,1},{385... | collective-permute-start | bytes 1179656 | tf_op jit(solution)/shard_map/ppermute | solution.py:22
  89.8 8.1 %collective-permute-done.9 = bf16[4,1,2,16,1536]{4,3,2,1,0:T(8,128)(2,1)S(1)} collective-permute-done((bf16[4,1,2,16,1536]{4,3,2,1,0:T(8,128)(2,1)S(1)}, bf16[4,1,2,16,1536]{4,3,2,1,0:T(8,128)(2,1)S(1)}, u32[]{:S(2)}, u32[]{:S(2)}) %collective-permute-start.9) | collective-permute-done | bytes 393248 | tf_op jit(solution)/shard_map/ppermute | solution.py:22
  98.0 7.0 %all-to-all-done.1 = bf16[8,128,256]{2,1,0:T(8,128)(2,1)S(1)} async-done(((bf16[8,128,256]{2,1,0:T(8,128)(2,1)}), bf16[8,128,256]{2,1,0:T(8,128)(2,1)S(1)}, u32[]{:S(2)}, u32[]{:S(2)}) %all-to-all-start.1) | async-done | bytes 524320 | tf_op jit(solution)/shard_map/all_to_all | solution.py:30
  106.0 4.8 %all-to-all-start.2 = ((bf16[16,8,1536]{2,1,0:T(8,128)(2,1)}), bf16[16,8,1536]{2,1,0:T(8,128)(2,1)S(1)}, u32[]{:S(2)}, u32[]{:S(2)}) async-start(bf16[16,8,1536]{2,1,0:T(8,128)(2,1)} %fusion.1), calls=%async_computation.2 | async-start | bytes 786432 | tf_op jit(solution)/shard_map/all_to_all | solution.py:30
  111.2 3.4 %collective-permute-start.11 = (bf16[128,256]{1,0:T(8,128)(2,1)S(1)}, bf16[128,256]{1,0:T(8,128)(2,1)S(1)}, u32[]{:S(2)}, u32[]{:S(2)}) collective-permute-start(bf16[128,256]{1,0:T(8,128)(2,1)S(1)} %reduce_sum.43), channel_id=1, source_target_pairs={{0,128},{128,0},{256,384},{384,256},{1,129},{129,1},{257,385},{385... | collective-permute-start | bytes 196616 | tf_op jit(solution)/shard_map/ppermute | solution.py:22
  114.6 4.2 %all-to-all-done.2 = bf16[16,8,1536]{2,1,0:T(8,128)(2,1)S(1)} async-done(((bf16[16,8,1536]{2,1,0:T(8,128)(2,1)}), bf16[16,8,1536]{2,1,0:T(8,128)(2,1)S(1)}, u32[]{:S(2)}, u32[]{:S(2)}) %all-to-all-start.2) | async-done | bytes 393248 | tf_op jit(solution)/shard_map/all_to_all | solution.py:30
  118.9 5.5 %collective-permute-start.10 = (bf16[8,1536]{1,0:T(8,128)(2,1)S(1)}, bf16[8,1536]{1,0:T(8,128)(2,1)S(1)}, u32[]{:S(2)}, u32[]{:S(2)}) collective-permute-start(bf16[8,1536]{1,0:T(8,128)(2,1)S(1)} %convert_element_type.44), channel_id=1, source_target_pairs={{0,1},{1,0},{2,3},{3,2},{4,5},{5,4},{6,7},{7,6},{8,9},{9,8},{10,11... | collective-permute-start | bytes 73736 | tf_op jit(solution)/shard_map/ppermute | solution.py:22
  124.4 4.9 %collective-permute-start.12 = (bf16[2,128,256]{2,1,0:T(8,128)(2,1)S(1)}, bf16[2,128,256]{2,1,0:T(8,128)(2,1)S(1)}, u32[]{:S(2)}, u32[]{:S(2)}) collective-permute-start(bf16[2,128,256]{2,1,0:T(8,128)(2,1)S(1)} %pad_maximum_fusion), channel_id=1, source_target_pairs={{0,256},{128,384},{256,0},{384,128},{1,257},{129,385},{257,1},{385... | collective-permute-start | bytes 393224 | tf_op jit(solution)/shard_map/ppermute | solution.py:22
  129.4 4.2 %collective-permute-done.10 = bf16[8,1536]{1,0:T(8,128)(2,1)S(1)} collective-permute-done((bf16[8,1536]{1,0:T(8,128)(2,1)S(1)}, bf16[8,1536]{1,0:T(8,128)(2,1)S(1)}, u32[]{:S(2)}, u32[]{:S(2)}) %collective-permute-start.10) | collective-permute-done | bytes 24608 | tf_op jit(solution)/shard_map/ppermute | solution.py:22
  136.3 6.8 %all-to-all-start.3 = ((bf16[32,2,8,384]{3,2,1,0:T(8,128)(2,1)}), bf16[32,2,8,384]{3,2,1,0:T(8,128)(2,1)S(1)}, u32[]{:S(2)}, u32[]{:S(2)}) async-start(bf16[32,2,8,384]{3,2,1,0:T(8,128)(2,1)} %bitcast.23), calls=%async_computation.3 | async-start | bytes 786432 | tf_op jit(solution)/shard_map/all_to_all | solution.py:30
  143.2 9.6 %all-to-all-done.3 = bf16[32,2,8,384]{3,2,1,0:T(8,128)(2,1)S(1)} async-done(((bf16[32,2,8,384]{3,2,1,0:T(8,128)(2,1)}), bf16[32,2,8,384]{3,2,1,0:T(8,128)(2,1)S(1)}, u32[]{:S(2)}, u32[]{:S(2)}) %all-to-all-start.3) | async-done | bytes 393248 | tf_op jit(solution)/shard_map/all_to_all | solution.py:30
  154.0 4.0 %all-to-all-start.4 = ((bf16[4,64,384]{2,1,0:T(8,128)(2,1)}), bf16[4,64,384]{2,1,0:T(8,128)(2,1)S(1)}, u32[]{:S(2)}, u32[]{:S(2)}) async-start(bf16[4,64,384]{2,1,0:T(8,128)(2,1)} %bitcast.27), calls=%async_computation.4 | async-start | bytes 393216 | tf_op jit(solution)/shard_map/all_to_all | solution.py:30
  158.0 13.4 %all-to-all-done.4 = bf16[4,64,384]{2,1,0:T(8,128)(2,1)S(1)} async-done(((bf16[4,64,384]{2,1,0:T(8,128)(2,1)}), bf16[4,64,384]{2,1,0:T(8,128)(2,1)S(1)}, u32[]{:S(2)}, u32[]{:S(2)}) %all-to-all-start.4) | async-done | bytes 196640 | tf_op jit(solution)/shard_map/all_to_all | solution.py:30
  172.1 3.4 %all-to-all-start.5 = ((bf16[4,64,384]{2,1,0:T(8,128)(2,1)}), bf16[4,64,384]{2,1,0:T(8,128)(2,1)S(1)}, u32[]{:S(2)}, u32[]{:S(2)}) async-start(bf16[4,64,384]{2,1,0:T(8,128)(2,1)} %broadcast_in_dim.42), calls=%async_computation.5 | async-start | bytes 393216 | tf_op jit(solution)/shard_map/all_to_all | solution.py:30
  176.1 5.7 %all-to-all-done.5 = bf16[4,64,384]{2,1,0:T(8,128)(2,1)S(1)} async-done(((bf16[4,64,384]{2,1,0:T(8,128)(2,1)}), bf16[4,64,384]{2,1,0:T(8,128)(2,1)S(1)}, u32[]{:S(2)}, u32[]{:S(2)}) %all-to-all-start.5) | async-done | bytes 196640 | tf_op jit(solution)/shard_map/all_to_all | solution.py:30
  (75 shorter events, 36.1 us)
Async XLA Ops:
  0.6 25.1 %copy-start = (bf16[64,1536]{1,0:T(8,128)(2,1)S(1)}, bf16[64,1536]{1,0:T(8,128)(2,1)}, u32[]{:S(2)}) copy-start(bf16[64,1536]{1,0:T(8,128)(2,1)} %param.11) | copy-start | bytes 589828
  0.6 41.1 %collective-permute-start = (bf16[64,1792]{1,0:T(8,128)(2,1)}, bf16[64,1792]{1,0:T(8,128)(2,1)S(1)}, u32[]{:S(2)}, u32[]{:S(2)}) collective-permute-start(bf16[64,1792]{1,0:T(8,128)(2,1)} %refs_0_), channel_id=1, source_target_pairs={{0,1},{1,0},{2,3},{3,2},{4,5},{5,4},{6,7},{7,6},{8,9},{9,8},{10,11... | collective-permute-start | bytes 688136 | tf_op jit(solution)/shard_map/ppermute | solution.py:22
  16.5 25.3 %collective-permute-start.2 = (bf16[64,1792]{1,0:T(8,128)(2,1)}, bf16[64,1792]{1,0:T(8,128)(2,1)S(1)}, u32[]{:S(2)}, u32[]{:S(2)}) collective-permute-start(bf16[64,1792]{1,0:T(8,128)(2,1)} %refs_0_), channel_id=1, source_target_pairs={{0,2},{2,0},{4,6},{6,4},{1,3},{3,1},{5,7},{7,5},{8,10},{10,8},{12,... | collective-permute-start | bytes 688136 | tf_op jit(solution)/shard_map/ppermute | solution.py:22
  18.9 22.9 %collective-permute-start.3 = (bf16[64,1792]{1,0:T(8,128)(2,1)}, bf16[64,1792]{1,0:T(8,128)(2,1)S(1)}, u32[]{:S(2)}, u32[]{:S(2)}) collective-permute-start(bf16[64,1792]{1,0:T(8,128)(2,1)} %refs_0_), channel_id=1, source_target_pairs={{0,4},{2,6},{4,0},{6,2},{1,5},{3,7},{5,1},{7,3},{8,12},{10,14},{12... | collective-permute-start | bytes 688136 | tf_op jit(solution)/shard_map/ppermute | solution.py:22
  23.4 18.4 %collective-permute-start.4 = (bf16[64,1792]{1,0:T(8,128)(2,1)}, bf16[64,1792]{1,0:T(8,128)(2,1)S(1)}, u32[]{:S(2)}, u32[]{:S(2)}) collective-permute-start(bf16[64,1792]{1,0:T(8,128)(2,1)} %refs_0_), channel_id=1, source_target_pairs={{0,6},{2,4},{4,2},{6,0},{1,7},{3,5},{5,3},{7,1},{8,14},{10,12},{12... | collective-permute-start | bytes 688136 | tf_op jit(solution)/shard_map/ppermute | solution.py:22
  25.8 16.0 %collective-permute-start.1 = (bf16[1,1,16,1536]{3,2,1,0:T(8,128)(2,1)S(1)}, bf16[1,1,16,1536]{3,2,1,0:T(8,128)(2,1)S(1)}, u32[]{:S(2)}, u32[]{:S(2)}) collective-permute-start(bf16[1,1,16,1536]{3,2,1,0:T(8,128)(2,1)S(1)} %dynamic-slice_bitcast_fusion), channel_id=1, source_target_pairs={{0,64},{32,96},{64,0},{96,32},{1,65},{33,97},{65,1},{97,33},{2,66}... | collective-permute-start | bytes 147464 | tf_op jit(solution)/shard_map/ppermute | solution.py:22
  32.8 16.8 %copy-start.5 = (bf16[64,1792]{1,0:T(8,128)(2,1)S(1)}, bf16[64,1792]{1,0:T(8,128)(2,1)}, u32[]{:S(2)}) copy-start(bf16[64,1792]{1,0:T(8,128)(2,1)} %refs_0_) | copy-start | bytes 688132
  42.8 17.3 %all-to-all-start = ((bf16[4,64,1792]{2,1,0:T(8,128)(2,1)}), bf16[4,64,1792]{2,1,0:T(8,128)(2,1)S(1)}, u32[]{:S(2)}, u32[]{:S(2)}) async-start(bf16[4,64,1792]{2,1,0:T(8,128)(2,1)} %broadcast_in_dim.21), calls=%async_computation | async-start | bytes 1835008 | tf_op jit(solution)/shard_map/all_to_all | solution.py:30
  47.7 8.0 %collective-permute-start.6 = (bf16[2,1,16,1536]{3,2,1,0:T(8,128)(2,1)S(1)}, bf16[2,1,16,1536]{3,2,1,0:T(8,128)(2,1)S(1)}, u32[]{:S(2)}, u32[]{:S(2)}) collective-permute-start(bf16[2,1,16,1536]{3,2,1,0:T(8,128)(2,1)S(1)} %maximum_select_fusion.6), channel_id=1, source_target_pairs={{0,32},{32,0},{64,96},{96,64},{1,33},{33,1},{65,97},{97,65},{2,34}... | collective-permute-start | bytes 294920 | tf_op jit(solution)/shard_map/ppermute | solution.py:22
  51.7 13.7 %copy-start.7 = (bf16[512,64]{0,1:T(8,128)(2,1)S(1)}, bf16[512,64]{0,1:T(8,128)(2,1)}, u32[]{:S(2)}) copy-start(bf16[512,64]{0,1:T(8,128)(2,1)} %param.10) | copy-start | bytes 196612
  52.9 12.8 %collective-permute-start.5 = (bf16[256,512]{1,0:T(8,128)(2,1)S(1)}, bf16[256,512]{1,0:T(8,128)(2,1)S(1)}, u32[]{:S(2)}, u32[]{:S(2)}) collective-permute-start(bf16[256,512]{1,0:T(8,128)(2,1)S(1)} %get-tuple-element.24), channel_id=1, source_target_pairs={{0,8},{8,0},{1,9},{9,1},{2,10},{10,2},{3,11},{11,3},{4,12},{12,4},... | collective-permute-start | bytes 786440 | tf_op jit(solution)/shard_map/ppermute | solution.py:22
  62.1 27.3 %copy-start.8 = (bf16[4,1536]{1,0:T(4,128)(2,1)S(1)}, bf16[4,1536]{1,0:T(4,128)(2,1)}, u32[]{:S(2)}) copy-start(bf16[4,1536]{1,0:T(4,128)(2,1)} %param.12) | copy-start | bytes 36868
  63.3 3.4 %collective-permute-start.7 = (bf16[256,512]{1,0:T(8,128)(2,1)S(1)}, bf16[256,512]{1,0:T(8,128)(2,1)S(1)}, u32[]{:S(2)}, u32[]{:S(2)}) collective-permute-start(bf16[256,512]{1,0:T(8,128)(2,1)S(1)} %get-tuple-element.29), channel_id=1, source_target_pairs={{0,8},{8,0},{1,9},{9,1},{2,10},{10,2},{3,11},{11,3},{4,12},{12,4},... | collective-permute-start | bytes 786440 | tf_op jit(solution)/shard_map/ppermute | solution.py:22
  68.3 36.6 %all-to-all-start.1 = ((bf16[8,128,256]{2,1,0:T(8,128)(2,1)}), bf16[8,128,256]{2,1,0:T(8,128)(2,1)S(1)}, u32[]{:S(2)}, u32[]{:S(2)}) async-start(bf16[8,128,256]{2,1,0:T(8,128)(2,1)} %bitcast.15), calls=%async_computation.1 | async-start | bytes 1048576 | tf_op jit(solution)/shard_map/all_to_all | solution.py:30
  75.9 8.5 %collective-permute-start.8 = (bf16[4,1,1,16,1536]{4,3,2,1,0:T(8,128)(2,1)S(1)}, bf16[4,1,1,16,1536]{4,3,2,1,0:T(8,128)(2,1)S(1)}, u32[]{:S(2)}, u32[]{:S(2)}) collective-permute-start(bf16[4,1,1,16,1536]{4,3,2,1,0:T(8,128)(2,1)S(1)} %bitcast.58), channel_id=1, source_target_pairs={{0,128},{128,0},{256,384},{384,256},{1,129},{129,1},{257,385},{385... | collective-permute-start | bytes 589832 | tf_op jit(solution)/shard_map/ppermute | solution.py:22
  84.5 13.4 %collective-permute-start.9 = (bf16[4,1,2,16,1536]{4,3,2,1,0:T(8,128)(2,1)S(1)}, bf16[4,1,2,16,1536]{4,3,2,1,0:T(8,128)(2,1)S(1)}, u32[]{:S(2)}, u32[]{:S(2)}) collective-permute-start(bf16[4,1,2,16,1536]{4,3,2,1,0:T(8,128)(2,1)S(1)} %maximum_select_fusion.1), channel_id=1, source_target_pairs={{0,256},{128,384},{256,0},{384,128},{1,257},{129,385},{257,1},{385... | collective-permute-start | bytes 1179656 | tf_op jit(solution)/shard_map/ppermute | solution.py:22
  89.4 21.4 %copy-start.9 = (s32[1,512]{1,0:T(1,128)S(1)}, s32[1,512]{1,0:T(1,128)}, u32[]{:S(2)}) copy-start(s32[1,512]{1,0:T(1,128)} %param.13) | copy-start | bytes 6148
  106.0 12.8 %all-to-all-start.2 = ((bf16[16,8,1536]{2,1,0:T(8,128)(2,1)}), bf16[16,8,1536]{2,1,0:T(8,128)(2,1)S(1)}, u32[]{:S(2)}, u32[]{:S(2)}) async-start(bf16[16,8,1536]{2,1,0:T(8,128)(2,1)} %fusion.1), calls=%async_computation.2 | async-start | bytes 786432 | tf_op jit(solution)/shard_map/all_to_all | solution.py:30
  111.2 13.2 %collective-permute-start.11 = (bf16[128,256]{1,0:T(8,128)(2,1)S(1)}, bf16[128,256]{1,0:T(8,128)(2,1)S(1)}, u32[]{:S(2)}, u32[]{:S(2)}) collective-permute-start(bf16[128,256]{1,0:T(8,128)(2,1)S(1)} %reduce_sum.43), channel_id=1, source_target_pairs={{0,128},{128,0},{256,384},{384,256},{1,129},{129,1},{257,385},{385... | collective-permute-start | bytes 196616 | tf_op jit(solution)/shard_map/ppermute | solution.py:22
  118.9 14.7 %collective-permute-start.10 = (bf16[8,1536]{1,0:T(8,128)(2,1)S(1)}, bf16[8,1536]{1,0:T(8,128)(2,1)S(1)}, u32[]{:S(2)}, u32[]{:S(2)}) collective-permute-start(bf16[8,1536]{1,0:T(8,128)(2,1)S(1)} %convert_element_type.44), channel_id=1, source_target_pairs={{0,1},{1,0},{2,3},{3,2},{4,5},{5,4},{6,7},{7,6},{8,9},{9,8},{10,11... | collective-permute-start | bytes 73736 | tf_op jit(solution)/shard_map/ppermute | solution.py:22
  124.4 9.2 %collective-permute-start.12 = (bf16[2,128,256]{2,1,0:T(8,128)(2,1)S(1)}, bf16[2,128,256]{2,1,0:T(8,128)(2,1)S(1)}, u32[]{:S(2)}, u32[]{:S(2)}) collective-permute-start(bf16[2,128,256]{2,1,0:T(8,128)(2,1)S(1)} %pad_maximum_fusion), channel_id=1, source_target_pairs={{0,256},{128,384},{256,0},{384,128},{1,257},{129,385},{257,1},{385... | collective-permute-start | bytes 393224 | tf_op jit(solution)/shard_map/ppermute | solution.py:22
  136.3 16.6 %all-to-all-start.3 = ((bf16[32,2,8,384]{3,2,1,0:T(8,128)(2,1)}), bf16[32,2,8,384]{3,2,1,0:T(8,128)(2,1)S(1)}, u32[]{:S(2)}, u32[]{:S(2)}) async-start(bf16[32,2,8,384]{3,2,1,0:T(8,128)(2,1)} %bitcast.23), calls=%async_computation.3 | async-start | bytes 786432 | tf_op jit(solution)/shard_map/all_to_all | solution.py:30
  154.0 17.4 %all-to-all-start.4 = ((bf16[4,64,384]{2,1,0:T(8,128)(2,1)}), bf16[4,64,384]{2,1,0:T(8,128)(2,1)S(1)}, u32[]{:S(2)}, u32[]{:S(2)}) async-start(bf16[4,64,384]{2,1,0:T(8,128)(2,1)} %bitcast.27), calls=%async_computation.4 | async-start | bytes 393216 | tf_op jit(solution)/shard_map/all_to_all | solution.py:30
  172.1 9.7 %all-to-all-start.5 = ((bf16[4,64,384]{2,1,0:T(8,128)(2,1)}), bf16[4,64,384]{2,1,0:T(8,128)(2,1)S(1)}, u32[]{:S(2)}, u32[]{:S(2)}) async-start(bf16[4,64,384]{2,1,0:T(8,128)(2,1)} %broadcast_in_dim.42), calls=%async_computation.5 | async-start | bytes 393216 | tf_op jit(solution)/shard_map/all_to_all | solution.py:30
  (5 other events, 8.6 us)

commit v7 on v5

--- a/solution.py
+++ b/solution.py
@@ -128,7 +128,8 @@
 
     pg = pick(projector.reshape(4, 16, -1), x, 0)[None, None]
     got = swap(pg, "zq", 2)
-    far, got, effective, *near = lax.optimization_barrier((far, got, effective, *near))
+    far, effective, *near = lax.optimization_barrier((far, effective, *near))
+    got, *near = lax.optimization_barrier((got, *near))
     pg = placed(pg, got, zq >> 1, 0)
     pg = join(pg.reshape(2, 1, 16, -1), "zq", 1, zq & 1, 1).reshape(4, 1, 1, 16, -1)
 

time: 184 us -> 188 us (1.022)
  starting transfers between devices: 81.9 us -> 84.8 us
    ppermute x13, waiting for transfers between devices: 24.9 us -> 30.6 us  [swap(): lax.ppermute(x, axis, [(i, i ^ mask) for i in range(lax.axis_size(axis))])]
    all_to_all x5, waiting for transfers between devices: 34.5 us -> 30.1 us  [exchange(): return lax.all_to_all(x, axes, 0, 0, tiled=True)]
    ppermute x13, starting transfers between devices: 57.3 us -> 61.1 us  [swap(): lax.ppermute(x, axis, [(i, i ^ mask) for i in range(lax.axis_size(axis))])]
  transfers between devices with their start and end apart: 18 -> 18, of which waited for: 11 -> 12; matrix products, arithmetic and copies ran while one was open for 1% -> 1% of each run, Pallas kernels for 2% -> 2%
where the time goes in v7:
time: 188 us; the launch traced here: 187 us
  starting transfers between devices  84.8 us (45%)
  waiting for transfers between devices  60.7 us (32%)
  blocking collectives  18.4 us (10%)
  local copies, waits for them, and re-layouts  11.4 us (6%)
  Pallas kernels  5.65 us (3%)
  matrix products  2.39 us (1%)
  other arithmetic  2.35 us (1%)
    ppermute x13, starting transfers between devices, swap(): lax.ppermute(x, axis, [(i, i ^ mask) for i in range(lax.axis_size(axis))])  61.1 us
    ppermute x13, waiting for transfers between devices, swap(): lax.ppermute(x, axis, [(i, i ^ mask) for i in range(lax.axis_size(axis))])  30.6 us
    all_to_all x5, waiting for transfers between devices, exchange(): return lax.all_to_all(x, axes, 0, 0, tiled=True)  30.1 us
    all_to_all x5, starting transfers between devices, exchange(): return lax.all_to_all(x, axes, 0, 0, tiled=True)  23.7 us
    all_to_all x1, blocking collectives, exchange(): return lax.all_to_all(x, axes, 0, 0, tiled=True)  16.6 us
    unnamed x20, local copies, waits for them, and re-layouts  8.58 us
  transfers between devices with their start and end apart: 18, of which 12 were waited for; matrix products, arithmetic and copies ran while one was open for 1% of the time, Pallas kernels for 2%

profile of v7, /device:TPU:8, one launch (start us, length us, event | category | flops | bytes accessed | tf_op | source)
XLA Modules:
  0.0 186.7 jit_solution(1023738720222753211)
XLA Ops:
  0.6 15.9 %collective-permute-start = (bf16[64,1792]{1,0:T(8,128)(2,1)}, bf16[64,1792]{1,0:T(8,128)(2,1)S(1)}, u32[]{:S(2)}, u32[]{:S(2)}) collective-permute-start(bf16[64,1792]{1,0:T(8,128)(2,1)} %refs_0_), channel_id=1, source_target_pairs={{0,1},{1,0},{2,3},{3,2},{4,5},{5,4},{6,7},{7,6},{8,9},{9,8},{10,11... | collective-permute-start | bytes 688136 | tf_op jit(solution)/shard_map/ppermute | solution.py:22
  18.9 4.5 %collective-permute-start.2 = (bf16[64,1792]{1,0:T(8,128)(2,1)}, bf16[64,1792]{1,0:T(8,128)(2,1)S(1)}, u32[]{:S(2)}, u32[]{:S(2)}) collective-permute-start(bf16[64,1792]{1,0:T(8,128)(2,1)} %refs_0_), channel_id=1, source_target_pairs={{0,4},{2,6},{4,0},{6,2},{1,5},{3,7},{5,1},{7,3},{8,12},{10,14},{12... | collective-permute-start | bytes 688136 | tf_op jit(solution)/shard_map/ppermute | solution.py:22
  23.4 2.4 %collective-permute-start.3 = (bf16[64,1792]{1,0:T(8,128)(2,1)}, bf16[64,1792]{1,0:T(8,128)(2,1)S(1)}, u32[]{:S(2)}, u32[]{:S(2)}) collective-permute-start(bf16[64,1792]{1,0:T(8,128)(2,1)} %refs_0_), channel_id=1, source_target_pairs={{0,6},{2,4},{4,2},{6,0},{1,7},{3,5},{5,3},{7,1},{8,14},{10,12},{12... | collective-permute-start | bytes 688136 | tf_op jit(solution)/shard_map/ppermute | solution.py:22
  31.9 4.0 %collective-permute-done.3.refs_3_ = bf16[64,1792]{1,0:T(8,128)(2,1)S(1)} collective-permute-done((bf16[64,1792]{1,0:T(8,128)(2,1)}, bf16[64,1792]{1,0:T(8,128)(2,1)S(1)}, u32[]{:S(2)}, u32[]{:S(2)}) %collective-permute-start.3) | collective-permute-done | bytes 229408 | tf_op jit(solution)/shard_map/ppermute | solution.py:22
  37.0 5.9 %all-to-all-start = ((bf16[4,64,1792]{2,1,0:T(8,128)(2,1)}), bf16[4,64,1792]{2,1,0:T(8,128)(2,1)S(1)}, u32[]{:S(2)}, u32[]{:S(2)}) async-start(bf16[4,64,1792]{2,1,0:T(8,128)(2,1)} %broadcast_in_dim.52), calls=%async_computation | async-start | bytes 1835008 | tf_op jit(solution)/shard_map/all_to_all | solution.py:30
  42.9 4.3 %collective-permute-start.4 = (bf16[1,1,16,1536]{3,2,1,0:T(8,128)(2,1)S(1)}, bf16[1,1,16,1536]{3,2,1,0:T(8,128)(2,1)S(1)}, u32[]{:S(2)}, u32[]{:S(2)}) collective-permute-start(bf16[1,1,16,1536]{3,2,1,0:T(8,128)(2,1)S(1)} %dynamic-slice_bitcast_fusion), channel_id=1, source_target_pairs={{0,64},{32,96},{64,0},{96,32},{1,65},{33,97},{65,1},{97,33},{2,66}... | collective-permute-start | bytes 147464 | tf_op jit(solution)/shard_map/ppermute | solution.py:22
  47.2 8.0 %collective-permute-done.4 = bf16[1,1,16,1536]{3,2,1,0:T(8,128)(2,1)S(1)} collective-permute-done((bf16[1,1,16,1536]{3,2,1,0:T(8,128)(2,1)S(1)}, bf16[1,1,16,1536]{3,2,1,0:T(8,128)(2,1)S(1)}, u32[]{:S(2)}, u32[]{:S(2)}) %collective-permute-start.4) | collective-permute-done | bytes 49184 | tf_op jit(solution)/shard_map/ppermute | solution.py:22
  71.5 5.4 %all-to-all-start.1 = ((bf16[8,128,256]{2,1,0:T(8,128)(2,1)}), bf16[8,128,256]{2,1,0:T(8,128)(2,1)S(1)}, u32[]{:S(2)}, u32[]{:S(2)}) async-start(bf16[8,128,256]{2,1,0:T(8,128)(2,1)} %bitcast.15), calls=%async_computation.1 | async-start | bytes 1048576 | tf_op jit(solution)/shard_map/all_to_all | solution.py:30
  76.9 3.4 %collective-permute-start.8 = (bf16[4,1,1,16,1536]{4,3,2,1,0:T(8,128)(2,1)S(1)}, bf16[4,1,1,16,1536]{4,3,2,1,0:T(8,128)(2,1)S(1)}, u32[]{:S(2)}, u32[]{:S(2)}) collective-permute-start(bf16[4,1,1,16,1536]{4,3,2,1,0:T(8,128)(2,1)S(1)} %bitcast.63), channel_id=1, source_target_pairs={{0,128},{128,0},{256,384},{384,256},{1,129},{129,1},{257,385},{385... | collective-permute-start | bytes 589832 | tf_op jit(solution)/shard_map/ppermute | solution.py:22
  80.3 5.1 %collective-permute-done.8 = bf16[4,1,1,16,1536]{4,3,2,1,0:T(8,128)(2,1)S(1)} collective-permute-done((bf16[4,1,1,16,1536]{4,3,2,1,0:T(8,128)(2,1)S(1)}, bf16[4,1,1,16,1536]{4,3,2,1,0:T(8,128)(2,1)S(1)}, u32[]{:S(2)}, u32[]{:S(2)}) %collective-permute-start.8) | collective-permute-done | bytes 196640 | tf_op jit(solution)/shard_map/ppermute | solution.py:22
  85.4 4.9 %collective-permute-start.9 = (bf16[4,1,2,16,1536]{4,3,2,1,0:T(8,128)(2,1)S(1)}, bf16[4,1,2,16,1536]{4,3,2,1,0:T(8,128)(2,1)S(1)}, u32[]{:S(2)}, u32[]{:S(2)}) collective-permute-start(bf16[4,1,2,16,1536]{4,3,2,1,0:T(8,128)(2,1)S(1)} %maximum_select_fusion.1), channel_id=1, source_target_pairs={{0,256},{128,384},{256,0},{384,128},{1,257},{129,385},{257,1},{385... | collective-permute-start | bytes 1179656 | tf_op jit(solution)/shard_map/ppermute | solution.py:22
  90.8 8.1 %collective-permute-done.9 = bf16[4,1,2,16,1536]{4,3,2,1,0:T(8,128)(2,1)S(1)} collective-permute-done((bf16[4,1,2,16,1536]{4,3,2,1,0:T(8,128)(2,1)S(1)}, bf16[4,1,2,16,1536]{4,3,2,1,0:T(8,128)(2,1)S(1)}, u32[]{:S(2)}, u32[]{:S(2)}) %collective-permute-start.9) | collective-permute-done | bytes 393248 | tf_op jit(solution)/shard_map/ppermute | solution.py:22
  98.9 7.0 %all-to-all-done.1 = bf16[8,128,256]{2,1,0:T(8,128)(2,1)S(1)} async-done(((bf16[8,128,256]{2,1,0:T(8,128)(2,1)}), bf16[8,128,256]{2,1,0:T(8,128)(2,1)S(1)}, u32[]{:S(2)}, u32[]{:S(2)}) %all-to-all-start.1) | async-done | bytes 524320 | tf_op jit(solution)/shard_map/all_to_all | solution.py:30
  107.0 4.8 %all-to-all-start.2 = ((bf16[16,8,1536]{2,1,0:T(8,128)(2,1)}), bf16[16,8,1536]{2,1,0:T(8,128)(2,1)S(1)}, u32[]{:S(2)}, u32[]{:S(2)}) async-start(bf16[16,8,1536]{2,1,0:T(8,128)(2,1)} %fusion.1), calls=%async_computation.2 | async-start | bytes 786432 | tf_op jit(solution)/shard_map/all_to_all | solution.py:30
  112.3 3.4 %collective-permute-start.11 = (bf16[128,256]{1,0:T(8,128)(2,1)S(1)}, bf16[128,256]{1,0:T(8,128)(2,1)S(1)}, u32[]{:S(2)}, u32[]{:S(2)}) collective-permute-start(bf16[128,256]{1,0:T(8,128)(2,1)S(1)} %reduce_sum.43), channel_id=1, source_target_pairs={{0,128},{128,0},{256,384},{384,256},{1,129},{129,1},{257,385},{385... | collective-permute-start | bytes 196616 | tf_op jit(solution)/shard_map/ppermute | solution.py:22
  115.7 4.1 %all-to-all-done.2 = bf16[16,8,1536]{2,1,0:T(8,128)(2,1)S(1)} async-done(((bf16[16,8,1536]{2,1,0:T(8,128)(2,1)}), bf16[16,8,1536]{2,1,0:T(8,128)(2,1)S(1)}, u32[]{:S(2)}, u32[]{:S(2)}) %all-to-all-start.2) | async-done | bytes 393248 | tf_op jit(solution)/shard_map/all_to_all | solution.py:30
  119.8 9.3 %collective-permute-start.10 = (bf16[8,1536]{1,0:T(8,128)(2,1)S(1)}, bf16[8,1536]{1,0:T(8,128)(2,1)S(1)}, u32[]{:S(2)}, u32[]{:S(2)}) collective-permute-start(bf16[8,1536]{1,0:T(8,128)(2,1)S(1)} %convert_element_type.44), channel_id=1, source_target_pairs={{0,1},{1,0},{2,3},{3,2},{4,5},{5,4},{6,7},{7,6},{8,9},{9,8},{10,11... | collective-permute-start | bytes 73736 | tf_op jit(solution)/shard_map/ppermute | solution.py:22
  129.1 4.9 %collective-permute-start.12 = (bf16[2,128,256]{2,1,0:T(8,128)(2,1)S(1)}, bf16[2,128,256]{2,1,0:T(8,128)(2,1)S(1)}, u32[]{:S(2)}, u32[]{:S(2)}) collective-permute-start(bf16[2,128,256]{2,1,0:T(8,128)(2,1)S(1)} %pad_maximum_fusion.1), channel_id=1, source_target_pairs={{0,256},{128,384},{256,0},{384,128},{1,257},{129,385},{257,1},{385... | collective-permute-start | bytes 393224 | tf_op jit(solution)/shard_map/ppermute | solution.py:22
  134.4 3.1 %collective-permute-done.12 = bf16[2,128,256]{2,1,0:T(8,128)(2,1)S(1)} collective-permute-done((bf16[2,128,256]{2,1,0:T(8,128)(2,1)S(1)}, bf16[2,128,256]{2,1,0:T(8,128)(2,1)S(1)}, u32[]{:S(2)}, u32[]{:S(2)}) %collective-permute-start.12) | collective-permute-done | bytes 131104 | tf_op jit(solution)/shard_map/ppermute | solution.py:22
  140.2 16.6 %all_to_all.30 = bf16[32,2,8,384]{3,2,1,0:T(8,128)(2,1)S(1)} all-to-all(bf16[32,2,8,384]{3,2,1,0:T(8,128)(2,1)S(1)} %bitcast.60), channel_id=1, replica_groups=mesh['dp'=4,'zq'=4,'zp'=2,'co'=2,'y'=4,'zh'=2] {'dp','zp','y'}, dimensions={0} | all-to-all | bytes 786432 | tf_op jit(solution)/shard_map/all_to_all | solution.py:30
  157.8 4.3 %all-to-all-start.4 = ((bf16[4,64,384]{2,1,0:T(8,128)(2,1)}), bf16[4,64,384]{2,1,0:T(8,128)(2,1)S(1)}, u32[]{:S(2)}, u32[]{:S(2)}) async-start(bf16[4,64,384]{2,1,0:T(8,128)(2,1)} %bitcast.29), calls=%async_computation.4 | async-start | bytes 393216 | tf_op jit(solution)/shard_map/all_to_all | solution.py:30
  162.1 13.4 %all-to-all-done.4 = bf16[4,64,384]{2,1,0:T(8,128)(2,1)S(1)} async-done(((bf16[4,64,384]{2,1,0:T(8,128)(2,1)}), bf16[4,64,384]{2,1,0:T(8,128)(2,1)S(1)}, u32[]{:S(2)}, u32[]{:S(2)}) %all-to-all-start.4) | async-done | bytes 196640 | tf_op jit(solution)/shard_map/all_to_all | solution.py:30
  176.3 3.4 %all-to-all-start.5 = ((bf16[4,64,384]{2,1,0:T(8,128)(2,1)}), bf16[4,64,384]{2,1,0:T(8,128)(2,1)S(1)}, u32[]{:S(2)}, u32[]{:S(2)}) async-start(bf16[4,64,384]{2,1,0:T(8,128)(2,1)} %broadcast_in_dim.60), calls=%async_computation.5 | async-start | bytes 393216 | tf_op jit(solution)/shard_map/all_to_all | solution.py:30
  180.3 5.7 %all-to-all-done.5 = bf16[4,64,384]{2,1,0:T(8,128)(2,1)S(1)} async-done(((bf16[4,64,384]{2,1,0:T(8,128)(2,1)}), bf16[4,64,384]{2,1,0:T(8,128)(2,1)S(1)}, u32[]{:S(2)}, u32[]{:S(2)}) %all-to-all-start.5) | async-done | bytes 196640 | tf_op jit(solution)/shard_map/all_to_all | solution.py:30
  (76 shorter events, 33.9 us)
Async XLA Ops:
  0.6 42.2 %copy-start = (bf16[64,1536]{1,0:T(8,128)(2,1)S(1)}, bf16[64,1536]{1,0:T(8,128)(2,1)}, u32[]{:S(2)}) copy-start(bf16[64,1536]{1,0:T(8,128)(2,1)} %param.11) | copy-start | bytes 589828
  0.6 31.3 %collective-permute-start = (bf16[64,1792]{1,0:T(8,128)(2,1)}, bf16[64,1792]{1,0:T(8,128)(2,1)S(1)}, u32[]{:S(2)}, u32[]{:S(2)}) collective-permute-start(bf16[64,1792]{1,0:T(8,128)(2,1)} %refs_0_), channel_id=1, source_target_pairs={{0,1},{1,0},{2,3},{3,2},{4,5},{5,4},{6,7},{7,6},{8,9},{9,8},{10,11... | collective-permute-start | bytes 688136 | tf_op jit(solution)/shard_map/ppermute | solution.py:22
  16.5 15.4 %collective-permute-start.1 = (bf16[64,1792]{1,0:T(8,128)(2,1)}, bf16[64,1792]{1,0:T(8,128)(2,1)S(1)}, u32[]{:S(2)}, u32[]{:S(2)}) collective-permute-start(bf16[64,1792]{1,0:T(8,128)(2,1)} %refs_0_), channel_id=1, source_target_pairs={{0,2},{2,0},{4,6},{6,4},{1,3},{3,1},{5,7},{7,5},{8,10},{10,8},{12,... | collective-permute-start | bytes 688136 | tf_op jit(solution)/shard_map/ppermute | solution.py:22
  18.9 13.1 %collective-permute-start.2 = (bf16[64,1792]{1,0:T(8,128)(2,1)}, bf16[64,1792]{1,0:T(8,128)(2,1)S(1)}, u32[]{:S(2)}, u32[]{:S(2)}) collective-permute-start(bf16[64,1792]{1,0:T(8,128)(2,1)} %refs_0_), channel_id=1, source_target_pairs={{0,4},{2,6},{4,0},{6,2},{1,5},{3,7},{5,1},{7,3},{8,12},{10,14},{12... | collective-permute-start | bytes 688136 | tf_op jit(solution)/shard_map/ppermute | solution.py:22
  23.4 12.6 %collective-permute-start.3 = (bf16[64,1792]{1,0:T(8,128)(2,1)}, bf16[64,1792]{1,0:T(8,128)(2,1)S(1)}, u32[]{:S(2)}, u32[]{:S(2)}) collective-permute-start(bf16[64,1792]{1,0:T(8,128)(2,1)} %refs_0_), channel_id=1, source_target_pairs={{0,6},{2,4},{4,2},{6,0},{1,7},{3,5},{5,3},{7,1},{8,14},{10,12},{12... | collective-permute-start | bytes 688136 | tf_op jit(solution)/shard_map/ppermute | solution.py:22
  25.7 2.0 %copy-start.4 = (bf16[1792,1024]{1,0:T(8,128)(2,1)S(1)}, bf16[1792,1024]{1,0:T(8,128)(2,1)}, u32[]{:S(2)}) copy-start(bf16[1792,1024]{1,0:T(8,128)(2,1)} %weight_ref.1) | copy-start | bytes 11010052
  28.5 28.7 %copy-start.5 = (bf16[64,1792]{1,0:T(8,128)(2,1)S(1)}, bf16[64,1792]{1,0:T(8,128)(2,1)}, u32[]{:S(2)}) copy-start(bf16[64,1792]{1,0:T(8,128)(2,1)} %refs_0_) | copy-start | bytes 688132
  37.0 26.3 %all-to-all-start = ((bf16[4,64,1792]{2,1,0:T(8,128)(2,1)}), bf16[4,64,1792]{2,1,0:T(8,128)(2,1)S(1)}, u32[]{:S(2)}, u32[]{:S(2)}) async-start(bf16[4,64,1792]{2,1,0:T(8,128)(2,1)} %broadcast_in_dim.52), calls=%async_computation | async-start | bytes 1835008 | tf_op jit(solution)/shard_map/all_to_all | solution.py:30
  42.9 12.3 %collective-permute-start.4 = (bf16[1,1,16,1536]{3,2,1,0:T(8,128)(2,1)S(1)}, bf16[1,1,16,1536]{3,2,1,0:T(8,128)(2,1)S(1)}, u32[]{:S(2)}, u32[]{:S(2)}) collective-permute-start(bf16[1,1,16,1536]{3,2,1,0:T(8,128)(2,1)S(1)} %dynamic-slice_bitcast_fusion), channel_id=1, source_target_pairs={{0,64},{32,96},{64,0},{96,32},{1,65},{33,97},{65,1},{97,33},{2,66}... | collective-permute-start | bytes 147464 | tf_op jit(solution)/shard_map/ppermute | solution.py:22
  55.2 8.0 %collective-permute-start.6 = (bf16[2,1,16,1536]{3,2,1,0:T(8,128)(2,1)S(1)}, bf16[2,1,16,1536]{3,2,1,0:T(8,128)(2,1)S(1)}, u32[]{:S(2)}, u32[]{:S(2)}) collective-permute-start(bf16[2,1,16,1536]{3,2,1,0:T(8,128)(2,1)S(1)} %maximum_select_fusion.3), channel_id=1, source_target_pairs={{0,32},{32,0},{64,96},{96,64},{1,33},{33,1},{65,97},{97,65},{2,34}... | collective-permute-start | bytes 294920 | tf_op jit(solution)/shard_map/ppermute | solution.py:22
  59.2 9.3 %copy-start.7 = (bf16[512,64]{0,1:T(8,128)(2,1)S(1)}, bf16[512,64]{0,1:T(8,128)(2,1)}, u32[]{:S(2)}) copy-start(bf16[512,64]{0,1:T(8,128)(2,1)} %param.10) | copy-start | bytes 196612
  60.4 8.4 %collective-permute-start.5 = (bf16[256,512]{1,0:T(8,128)(2,1)S(1)}, bf16[256,512]{1,0:T(8,128)(2,1)S(1)}, u32[]{:S(2)}, u32[]{:S(2)}) collective-permute-start(bf16[256,512]{1,0:T(8,128)(2,1)S(1)} %get-tuple-element.32), channel_id=1, source_target_pairs={{0,8},{8,0},{1,9},{9,1},{2,10},{10,2},{3,11},{11,3},{4,12},{12,4},... | collective-permute-start | bytes 786440 | tf_op jit(solution)/shard_map/ppermute | solution.py:22
  65.3 25.1 %copy-start.8 = (bf16[4,1536]{1,0:T(4,128)(2,1)S(1)}, bf16[4,1536]{1,0:T(4,128)(2,1)}, u32[]{:S(2)}) copy-start(bf16[4,1536]{1,0:T(4,128)(2,1)} %param.12) | copy-start | bytes 36868
  66.5 3.4 %collective-permute-start.7 = (bf16[256,512]{1,0:T(8,128)(2,1)S(1)}, bf16[256,512]{1,0:T(8,128)(2,1)S(1)}, u32[]{:S(2)}, u32[]{:S(2)}) collective-permute-start(bf16[256,512]{1,0:T(8,128)(2,1)S(1)} %get-tuple-element.37), channel_id=1, source_target_pairs={{0,8},{8,0},{1,9},{9,1},{2,10},{10,2},{3,11},{11,3},{4,12},{12,4},... | collective-permute-start | bytes 786440 | tf_op jit(solution)/shard_map/ppermute | solution.py:22
  71.5 34.4 %all-to-all-start.1 = ((bf16[8,128,256]{2,1,0:T(8,128)(2,1)}), bf16[8,128,256]{2,1,0:T(8,128)(2,1)S(1)}, u32[]{:S(2)}, u32[]{:S(2)}) async-start(bf16[8,128,256]{2,1,0:T(8,128)(2,1)} %bitcast.15), calls=%async_computation.1 | async-start | bytes 1048576 | tf_op jit(solution)/shard_map/all_to_all | solution.py:30
  76.9 8.5 %collective-permute-start.8 = (bf16[4,1,1,16,1536]{4,3,2,1,0:T(8,128)(2,1)S(1)}, bf16[4,1,1,16,1536]{4,3,2,1,0:T(8,128)(2,1)S(1)}, u32[]{:S(2)}, u32[]{:S(2)}) collective-permute-start(bf16[4,1,1,16,1536]{4,3,2,1,0:T(8,128)(2,1)S(1)} %bitcast.63), channel_id=1, source_target_pairs={{0,128},{128,0},{256,384},{384,256},{1,129},{129,1},{257,385},{385... | collective-permute-start | bytes 589832 | tf_op jit(solution)/shard_map/ppermute | solution.py:22
  85.4 13.4 %collective-permute-start.9 = (bf16[4,1,2,16,1536]{4,3,2,1,0:T(8,128)(2,1)S(1)}, bf16[4,1,2,16,1536]{4,3,2,1,0:T(8,128)(2,1)S(1)}, u32[]{:S(2)}, u32[]{:S(2)}) collective-permute-start(bf16[4,1,2,16,1536]{4,3,2,1,0:T(8,128)(2,1)S(1)} %maximum_select_fusion.1), channel_id=1, source_target_pairs={{0,256},{128,384},{256,0},{384,128},{1,257},{129,385},{257,1},{385... | collective-permute-start | bytes 1179656 | tf_op jit(solution)/shard_map/ppermute | solution.py:22
  90.4 21.4 %copy-start.9 = (s32[1,512]{1,0:T(1,128)S(1)}, s32[1,512]{1,0:T(1,128)}, u32[]{:S(2)}) copy-start(s32[1,512]{1,0:T(1,128)} %param.13) | copy-start | bytes 6148
  107.0 12.7 %all-to-all-start.2 = ((bf16[16,8,1536]{2,1,0:T(8,128)(2,1)}), bf16[16,8,1536]{2,1,0:T(8,128)(2,1)S(1)}, u32[]{:S(2)}, u32[]{:S(2)}) async-start(bf16[16,8,1536]{2,1,0:T(8,128)(2,1)} %fusion.1), calls=%async_computation.2 | async-start | bytes 786432 | tf_op jit(solution)/shard_map/all_to_all | solution.py:30
  112.3 16.8 %collective-permute-start.11 = (bf16[128,256]{1,0:T(8,128)(2,1)S(1)}, bf16[128,256]{1,0:T(8,128)(2,1)S(1)}, u32[]{:S(2)}, u32[]{:S(2)}) collective-permute-start(bf16[128,256]{1,0:T(8,128)(2,1)S(1)} %reduce_sum.43), channel_id=1, source_target_pairs={{0,128},{128,0},{256,384},{384,256},{1,129},{129,1},{257,385},{385... | collective-permute-start | bytes 196616 | tf_op jit(solution)/shard_map/ppermute | solution.py:22
  119.8 14.6 %collective-permute-start.10 = (bf16[8,1536]{1,0:T(8,128)(2,1)S(1)}, bf16[8,1536]{1,0:T(8,128)(2,1)S(1)}, u32[]{:S(2)}, u32[]{:S(2)}) collective-permute-start(bf16[8,1536]{1,0:T(8,128)(2,1)S(1)} %convert_element_type.44), channel_id=1, source_target_pairs={{0,1},{1,0},{2,3},{3,2},{4,5},{5,4},{6,7},{7,6},{8,9},{9,8},{10,11... | collective-permute-start | bytes 73736 | tf_op jit(solution)/shard_map/ppermute | solution.py:22
  129.1 8.4 %collective-permute-start.12 = (bf16[2,128,256]{2,1,0:T(8,128)(2,1)S(1)}, bf16[2,128,256]{2,1,0:T(8,128)(2,1)S(1)}, u32[]{:S(2)}, u32[]{:S(2)}) collective-permute-start(bf16[2,128,256]{2,1,0:T(8,128)(2,1)S(1)} %pad_maximum_fusion.1), channel_id=1, source_target_pairs={{0,256},{128,384},{256,0},{384,128},{1,257},{129,385},{257,1},{385... | collective-permute-start | bytes 393224 | tf_op jit(solution)/shard_map/ppermute | solution.py:22
  157.8 17.7 %all-to-all-start.4 = ((bf16[4,64,384]{2,1,0:T(8,128)(2,1)}), bf16[4,64,384]{2,1,0:T(8,128)(2,1)S(1)}, u32[]{:S(2)}, u32[]{:S(2)}) async-start(bf16[4,64,384]{2,1,0:T(8,128)(2,1)} %bitcast.29), calls=%async_computation.4 | async-start | bytes 393216 | tf_op jit(solution)/shard_map/all_to_all | solution.py:30
  176.3 9.7 %all-to-all-start.5 = ((bf16[4,64,384]{2,1,0:T(8,128)(2,1)}), bf16[4,64,384]{2,1,0:T(8,128)(2,1)S(1)}, u32[]{:S(2)}, u32[]{:S(2)}) async-start(bf16[4,64,384]{2,1,0:T(8,128)(2,1)} %broadcast_in_dim.60), calls=%async_computation.5 | async-start | bytes 393216 | tf_op jit(solution)/shard_map/all_to_all | solution.py:30
  (4 other events, 6.5 us)
